TPU v7x, 32 devices: a whole 2x2x4 slice. The times are simulated.
32 devices in a mesh: parts: 2 (over y), dp: 4 (over z), fsdp: 4 (over x, core).
Axes of the slice: x: 2, y: 2, z: 4, core: 2. Of those that a mesh axis runs over, the one named last changes fastest.
Arguments:
- hidden: bfloat16 [7168, 2560], P(('parts', 'dp'), 'fsdp'), parts along dimension 0
- lengths: int32 [24], P(('parts', 'dp')), parts along dimension 0, may hold values from 1 to 560, as said below
- mask_pos: int32 [24], P(('parts', 'dp')), parts along dimension 0, may hold values from 0 to 559, as said below
- token_ids: int32 [7168], P(('parts', 'dp')), parts along dimension 0, may hold values from 4 to 23
- assignment: int32 [24], P(('parts', 'dp')), parts along dimension 0, may hold values from 0 to 11, each once
- w_query: bfloat16 [2560, 2560], P('dp', 'fsdp')
- w_key: bfloat16 [2560, 2560], P('dp', 'fsdp')
- w_value: bfloat16 [2560, 2560], P('dp', 'fsdp'), may hold values from -0.5 to 0.5
- w_out: bfloat16 [2560, 2560], P('fsdp', 'dp'), may hold values from -0.125 to 0.125
- embed: bfloat16 [33, 2560], replicated
Outputs:
- states: bfloat16 [7168, 2560], P(('parts', 'dp'), 'fsdp'), parts along dimension 0
- logits: float32 [24, 33], P(('parts', 'dp')), parts along dimension 0
- scored: float32 [24], P(('parts', 'dp')), parts along dimension 0
There are 2 independent parts, one for each index of `parts`. A program takes and returns all parts, laid end to end along the dimension named above; an argument that names none is the same for every part. Nothing has to cross between parts.
Inputs may be any that keep to these rules, and one draw needn't show every extreme that they name: `lengths`: each run of 3 entries belonging to one index of dp sums to 896, and one entry of each run equals 560. `mask_pos`: each entry lies below its own sequence's length.
All inputs are finite; a program needn't handle non-finite values.
Results may differ from a plain program's by a relative error of at most 0.013.
The roundings to bfloat16 on the way count: a program that leaves them out, or rounds other values in their place, can miss the bound.
Values may be sent and summed in bfloat16 or wider, within the bound.
No kernel may reach another device: no remote copies, remote signals or barrier semaphores. Data moves between devices by JAX's collectives and lax.ppermute only.
A program may use at most 128 MiB of HBM per device.

v0:
```python
import jax
import jax.numpy as jnp
from jax import lax
from jax.sharding import PartitionSpec as P

HS = 128
SEQ_G = 3


EPSILON = 1e-05


def norm_rows(values):
    average = jnp.mean(values, -1, keepdims=True)
    centred = values - average
    spread = jnp.mean(centred * centred, -1, keepdims=True)
    return centred * lax.rsqrt(spread + EPSILON)


def rotate(field, position):
    half_width = field.shape[-1] // 2
    frequency = 10000.0 ** (-2.0 * jnp.arange(half_width, dtype=jnp.float32) / field.shape[-1])
    angles = position.astype(jnp.float32)[:, None] * frequency[None, :]
    angles = jnp.concatenate([angles, angles], -1)[:, None, :]
    turned = jnp.concatenate([-field[..., half_width:], field[..., :half_width]], -1)
    return field * jnp.cos(angles) + turned * jnp.sin(angles)


def layout(lengths, count):
    ends = jnp.cumsum(lengths)
    starts = ends - lengths
    tok_index = jnp.arange(count, dtype=jnp.int32)
    inside = (tok_index[:, None] >= starts[None, :]) & (tok_index[:, None] < ends[None, :])
    labels = jnp.arange(lengths.shape[0], dtype=jnp.int32)
    segment = jnp.sum(jnp.where(inside, labels[None, :], 0), 1)
    position = tok_index - jnp.sum(jnp.where(inside, starts[None, :], 0), 1)
    return (segment, position, starts)


def attend(queries, key_rows, value_rows, same_seq):

    def one_head(triple):
        query_head, key_head, value_head = triple
        scores = jnp.dot(query_head, key_head.T, preferred_element_type=jnp.float32)
        scores = jnp.where(same_seq, scores, -1e30)
        weights = jax.nn.softmax(scores, -1).astype(jnp.bfloat16)
        return jnp.dot(weights, value_head, preferred_element_type=jnp.float32).astype(jnp.bfloat16)

    stacked = lax.map(
        one_head,
        (queries.transpose(1, 0, 2), key_rows.transpose(1, 0, 2), value_rows.transpose(1, 0, 2)),
    )
    return stacked.transpose(1, 0, 2).reshape(queries.shape[0], -1)


def target_score(logits, target_ids):
    vocab_index = jnp.arange(logits.shape[1], dtype=jnp.int32)
    target = jnp.sum(jnp.where(vocab_index[None, :] == target_ids[:, None], logits, 0.0), 1)
    return target - jax.nn.logsumexp(logits, -1)


def per_device(
    hidden, lengths, mask_pos, token_ids, assignment, w_query, w_key, w_value, w_out, embed
):
    tokens_here = hidden.shape[0]
    gathered = lax.all_gather(hidden, "fsdp", axis=1, tiled=True)
    normed = norm_rows(gathered.astype(jnp.float32)).astype(jnp.bfloat16)
    query_sum = jnp.dot(
        normed,
        lax.all_gather(w_query, "dp", axis=0, tiled=True),
        preferred_element_type=jnp.float32,
    )
    key_sum = jnp.dot(
        normed, lax.all_gather(w_key, "dp", axis=0, tiled=True), preferred_element_type=jnp.float32
    )
    value_sum = jnp.dot(
        normed,
        lax.all_gather(w_value, "dp", axis=0, tiled=True),
        preferred_element_type=jnp.float32,
    )
    heads_here = w_query.shape[1] // HS
    segment, position, starts = layout(lengths, tokens_here)
    queries = rotate(
        (query_sum * HS ** (-0.5)).reshape(tokens_here, heads_here, HS), position
    ).astype(jnp.bfloat16)
    key_rows = rotate(key_sum.reshape(tokens_here, heads_here, HS), position).astype(jnp.bfloat16)
    value_rows = value_sum.astype(jnp.bfloat16).reshape(tokens_here, heads_here, HS)
    context = attend(queries, key_rows, value_rows, segment[:, None] == segment[None, :])
    partials = jnp.dot(
        context, lax.all_gather(w_out, "dp", axis=1, tiled=True), preferred_element_type=jnp.float32
    )
    attended = lax.psum_scatter(
        partials.astype(jnp.bfloat16), "fsdp", scatter_dimension=1, tiled=True
    ).astype(jnp.float32)
    states = (hidden.astype(jnp.float32) + attended).astype(jnp.bfloat16)
    picked = starts + mask_pos
    chosen = jnp.arange(tokens_here, dtype=jnp.int32)[None, :] == picked[:, None]
    local_rows = jnp.dot(
        chosen.astype(jnp.bfloat16), states, preferred_element_type=jnp.float32
    ).astype(jnp.bfloat16)
    local_ids = jnp.sum(jnp.where(chosen, token_ids[None, :], 0), 1)
    row_full = lax.all_gather(local_rows, "fsdp", axis=1, tiled=True)
    owned_slots = lax.axis_index("dp") * SEQ_G + jnp.arange(SEQ_G, dtype=jnp.int32)
    all_rows, all_ids, all_owner = (
        lax.all_gather(row_full, "dp", axis=0, tiled=True),
        lax.all_gather(local_ids, "dp", axis=0, tiled=True),
        lax.all_gather(assignment, "dp", axis=0, tiled=True),
    )
    match_owner = all_owner[None, :] == owned_slots[:, None]
    mine_rows = jnp.dot(
        match_owner.astype(jnp.bfloat16), all_rows, preferred_element_type=jnp.float32
    ).astype(jnp.bfloat16)
    mine_ids = jnp.sum(jnp.where(match_owner, all_ids[None, :], 0), 1).astype(jnp.int32)
    normed_rows = norm_rows(mine_rows.astype(jnp.float32)).astype(jnp.bfloat16)
    logits = jnp.dot(normed_rows, embed.T, preferred_element_type=jnp.float32)
    scored = target_score(logits, mine_ids)
    return (states, logits, scored)


def solution(mesh):
    return jax.shard_map(
        per_device,
        mesh=mesh,
        in_specs=(
            P(("parts", "dp"), "fsdp"),
            P(("parts", "dp")),
            P(("parts", "dp")),
            P(("parts", "dp")),
            P(("parts", "dp")),
            P("dp", "fsdp"),
            P("dp", "fsdp"),
            P("dp", "fsdp"),
            P("fsdp", "dp"),
            P(),
        ),
        out_specs=(P(("parts", "dp"), "fsdp"), P(("parts", "dp"), None), P(("parts", "dp"))),
        check_vma=False,
    )
```

profile of v0, /device:TPU:0, one launch (start us, length us, event | category | flops | bytes accessed | tf_op | source)
XLA Modules:
  0.0 406.1 jit_solution(3996527999382112884)
XLA Ops:
  8.0 0.7 all-gather.11.cloned.1.call-update
  11.1 1.8 fusion.29
  13.0 36.0 %all-gather.7.cloned.1.call-done = bf16[896,2560]{1,0:T(8,128)(2,1)} async-done(((bf16[896,640]{1,0:T(8,128)(2,1)}), bf16[896,2560]{1,0:T(8,128)(2,1)}) %all-gather.7.cloned.1.call-update) | async-done | bytes 4587536 | tf_op jit(solution)/shard_map/all_gather | solution.py:66
  49.0 3.1 convert_reduce_fusion
  52.7 1.3 fusion.19
  54.0 3.3 fusion.20
  57.3 59.0 %all-gather.11.cloned.1.call-done = bf16[2560,640]{1,0:T(8,128)(2,1)} async-done(((bf16[640,640]{1,0:T(8,128)(2,1)}), bf16[2560,640]{1,0:T(8,128)(2,1)}) %all-gather.11.cloned.1.call-update) | async-done | bytes 3276816 | tf_op jit(solution)/shard_map/all_gather | solution.py:74
  116.3 8.3 %fusion.42 = f32[896,640]{0,1:T(8,128)} fusion(bf16[896,2560]{1,0:T(8,128)(2,1)} %fusion.20, bf16[2560,640]{1,0:T(8,128)(2,1)} %all-gather.11.cloned.1.call-done), kind=kOutput, calls=%fused_computation.81 | convolution fusion | flops 2936012800 | bytes 10158080 | tf_op jit(solution)/shard_map/dot_general | solution.py:73
  124.6 2.4 copy.39
  127.0 2.9 slice_negate_fusion
  130.0 52.2 %all-gather.9.cloned.1.call-done = bf16[2560,640]{1,0:T(8,128)(2,1)} async-done(((bf16[640,640]{1,0:T(8,128)(2,1)}), bf16[2560,640]{1,0:T(8,128)(2,1)}) %all-gather.9.cloned.1.call-update) | async-done | bytes 3276816 | tf_op jit(solution)/shard_map/all_gather | solution.py:70
  182.2 8.3 %convolution_multiply_fusion = f32[896,640]{0,1:T(8,128)} fusion(bf16[896,2560]{1,0:T(8,128)(2,1)} %fusion.20, bf16[2560,640]{1,0:T(8,128)(2,1)} %all-gather.9.cloned.1.call-done), kind=kOutput, calls=%fused_computation.38 | convolution fusion | flops 2936586240 | bytes 10158080 | tf_op jit(solution)/shard_map/dot_general | solution.py:68
  190.5 3.2 copy.36
  193.7 5.2 %slice_negate_fusion.1 = (f32[896,5,64]{2,0,1:T(8,128)}, f32[896,5,64]{2,0,1:T(8,128)}) fusion(f32[896,5,128]{2,0,1:T(8,128)} %copy.36), kind=kLoop, calls=%fused_computation.30 | loop fusion | flops 286720 | bytes 4587520 | tf_op jit(solution)/shard_map/neg | solution.py:25
  198.9 49.1 %all-gather.13.cloned.1.call-done = bf16[2560,640]{1,0:T(8,128)(2,1)} async-done(((bf16[640,640]{1,0:T(8,128)(2,1)}), bf16[2560,640]{1,0:T(8,128)(2,1)}) %all-gather.13.cloned.1.call-update) | async-done | bytes 3276816 | tf_op jit(solution)/shard_map/all_gather | solution.py:78
  247.9 7.9 %convolution_convert_fusion.2 = bf16[896,640]{0,1:T(8,128)(2,1)} fusion(bf16[896,2560]{1,0:T(8,128)(2,1)} %fusion.20, bf16[2560,640]{1,0:T(8,128)(2,1)} %all-gather.13.cloned.1.call-done), kind=kOutput, calls=%fused_computation.39 | convolution fusion | flops 2936586240 | bytes 9011200 | tf_op jit(solution)/shard_map/dot_general | solution.py:76
  255.9 2.4 copy.42
  258.3 7.2 %fusion.26 = (bf16[5,896,128]{2,1,0:T(8,128)(2,1)}, bf16[5,896,128]{2,1,0:T(8,128)(2,1)}) fusion(f32[896,5,64]{2,0,1:T(8,128)} %get-tuple-element.74, f32[896,5,64]{2,0,1:T(8,128)} %get-tuple-element.73, f32[896,5,128]{2,0,1:T(8,128)S(1)} %copy.39, f32[896,128]{1,0:T(8,128)S(1)} %get-tuple-element.80, f32[896,128]{1,0:T(8,128)S(1)} %get-tuple-element.79, ...), kind=kLoop, calls=%fused_computation.40 | loop fusion | flops 5734400 | bytes 12386304 | tf_op jit(solution)/shard_map/transpose | solution.py:51
  265.5 26.5 %while.11 = (s32[]{:T(128)}, bf16[5,896,128]{1,2,0:T(8,128)(2,1)}, bf16[5,896,128]{2,1,0:T(8,128)(2,1)}, bf16[5,896,128]{2,1,0:T(8,128)(2,1)}, bf16[5,896,128]{2,1,0:T(8,128)(2,1)}, /*index=5*/s32[896]{0:T(1024)S(1)}, s32[]{:T(128)}) while((s32[]{:T(128)}, bf16[5,896,128]{1,2,0:T(8,128)(2,1)}, bf16[5,896,128]{2,1,0:T(8,128)(2,1)}, ...), condition=%wide.region_8.9_spmd.clone, body=%wide.region_5.8_spmd.clone.sunk | while | flops 420788480 | bytes 11509837 | solution.py:49
  265.5 1.6 fusion.59
  267.2 0.7 fusion.60
  267.9 2.0 fusion.61
  270.1 0.7 constant_dynamic-update-slice_fusion.2
  270.8 1.7 fusion.59
  272.5 0.7 fusion.60
  273.2 2.0 fusion.61
  275.4 0.7 constant_dynamic-update-slice_fusion.2
  276.1 1.7 fusion.59
  277.8 0.7 fusion.60
  278.5 2.0 fusion.61
  280.7 0.7 constant_dynamic-update-slice_fusion.2
  281.4 1.7 fusion.59
  283.1 0.7 fusion.60
  283.8 2.0 fusion.61
  286.0 0.7 constant_dynamic-update-slice_fusion.2
  286.7 1.7 fusion.59
  288.4 0.7 fusion.60
  289.1 2.0 fusion.61
  291.3 0.7 constant_dynamic-update-slice_fusion.2
  292.0 21.6 %all-gather.15.cloned.1.call-done = bf16[640,2560]{1,0:T(8,128)(2,1)} async-done(((bf16[640,640]{1,0:T(8,128)(2,1)}), bf16[640,2560]{1,0:T(8,128)(2,1)}) %all-gather.15.cloned.1.call-update) | async-done | bytes 3276816 | tf_op jit(solution)/shard_map/all_gather | solution.py:90
  313.6 8.1 %convolution_convert_fusion = bf16[896,2560]{1,0:T(8,128)(2,1)} fusion(bf16[896,640]{0,1:T(8,128)(2,1)} %bitcast.62, bf16[640,2560]{1,0:T(8,128)(2,1)} %all-gather.15.cloned.1.call-done), kind=kOutput, calls=%fused_computation.26 | convolution fusion | flops 2938306560 | bytes 9011200 | tf_op jit(solution)/shard_map/dot_general | solution.py:89
  321.7 7.2 %copy.44 = bf16[896,2560]{0,1:T(8,128)(2,1)} copy(bf16[896,2560]{1,0:T(8,128)(2,1)} %convolution_convert_fusion) | data formatting | bytes 9175040
  331.5 7.0 %all-reduce.2 = (s32[12]{0:T(128)S(1)}, s32[12]{0:T(128)S(1)}) all-reduce(s32[12]{0:T(128)S(1)} %dynamic-update-slice, s32[12]{0:T(128)S(1)} %dynamic-update-slice.1), channel_id=1, replica_groups=mesh['parts'=2,'dp'=4,'fsdp'=4] {'dp'}, use_global_device_ids=true, to_apply=%add | all-reduce | flops 24 | bytes 192
  338.7 36.1 %reduce-scatter.4.cloned.1.call-done = bf16[640,896]{1,0:T(8,128)(2,1)} async-done(((bf16[2560,896]{1,0:T(8,128)(2,1)}), bf16[640,896]{1,0:T(8,128)(2,1)}) %reduce-scatter.4.cloned.1.call-update) | async-done | bytes 1146896
  374.8 2.4 copy.45
  377.2 1.6 add_convert_fusion
  379.1 5.2 %all_gather.33 = bf16[3,2560]{1,0:T(4,128)(2,1)S(1)} all-gather(bf16[3,640]{1,0:T(4,128)(2,1)S(1)} %convolution_convert_fusion.3), channel_id=1, replica_groups=mesh['parts'=2,'dp'=4,'fsdp'=4] {'fsdp'}, dimensions={1}, use_global_device_ids=true | all-gather | bytes 19200 | tf_op jit(solution)/shard_map/all_gather | solution.py:102
  384.3 13.2 %all-gather = bf16[4,3,2560]{2,1,0:T(4,128)(2,1)S(1)} all-gather(bf16[1,3,2560]{2,1,0:T(4,128)(2,1)S(1)} %bitcast.59), channel_id=1, replica_groups=mesh['parts'=2,'dp'=4,'fsdp'=4] {'dp'}, dimensions={0}, use_global_device_ids=true | all-gather | bytes 76800 | tf_op jit(solution)/shard_map/all_gather | solution.py:105
  (63 shorter events, 8.6 us)
Async XLA Ops:
  7.2 390.9 %copy-start = (bf16[33,2560]{1,0:T(8,128)(2,1)S(1)}, bf16[33,2560]{1,0:T(8,128)(2,1)}, u32[]{:S(2)}) copy-start(bf16[33,2560]{1,0:T(8,128)(2,1)} %param.21) | copy-start | bytes 506884
  7.2 3.5 copy-start.6
  7.2 3.7 copy-start.7
  7.2 41.8 %all-gather.7.cloned.1.call-start = ((), (), s32[]{:S(2)}) async-start(), calls=%async_computation.1 | async-start | bytes 5734400 | tf_op jit(solution)/shard_map/all_gather | solution.py:66
  7.9 108.3 %all-gather.11.cloned.1.call-start = ((), (), s32[]{:S(2)}) async-start(), calls=%async_computation.3 | async-start | bytes 4096000 | tf_op jit(solution)/shard_map/all_gather | solution.py:74
  8.7 173.5 %all-gather.9.cloned.1.call-start = ((), (), s32[]{:S(2)}) async-start(), calls=%async_computation.2 | async-start | bytes 4096000 | tf_op jit(solution)/shard_map/all_gather | solution.py:70
  9.4 238.5 %all-gather.13.cloned.1.call-start = ((), (), s32[]{:S(2)}) async-start(), calls=%async_computation.4 | async-start | bytes 4096000 | tf_op jit(solution)/shard_map/all_gather | solution.py:78
  10.0 303.6 %all-gather.15.cloned.1.call-start = ((), (), s32[]{:S(2)}) async-start(), calls=%async_computation.5 | async-start | bytes 4096000 | tf_op jit(solution)/shard_map/all_gather | solution.py:90
  10.6 364.3 %reduce-scatter.4.cloned.1.call-start = ((), (), s32[]{:S(2)}) async-start(), calls=%async_computation.6 | async-start | bytes 5734400
  49.0 3.7 copy-start.1
  329.0 0.7 copy-start.9
  329.0 1.9 copy-start.4
  329.0 2.3 copy-start.8
  329.0 48.2 %copy-start.2 = (bf16[896,640]{1,0:T(8,128)(2,1)S(1)}, bf16[896,640]{1,0:T(8,128)(2,1)}, u32[]{:S(2)}) copy-start(bf16[896,640]{1,0:T(8,128)(2,1)} %param.12) | copy-start | bytes 3440644
  378.8 20.4 %copy-start.3 = (bf16[896,640]{1,0:T(8,128)(2,1)}, bf16[896,640]{1,0:T(8,128)(2,1)S(1)}, u32[]{:S(2)}) copy-start(bf16[896,640]{1,0:T(8,128)(2,1)S(1)} %add_convert_fusion) | copy-start | bytes 3440644
  398.4 0.8 copy-start.5
Sparse Core Ops, SparseCore 0:
  9.6 39.3 all-gather.6
  50.6 65.6 all-gather.10
  117.9 64.2 all-gather.8
  183.6 64.2 all-gather.12
  249.3 64.2 all-gather.14
  329.1 45.6 reduce-scatter.3
where the time goes:
time: 407 us; the launch traced here: 406 us
  waiting for transfers between devices  257 us (63%)
  matrix products  52.1 us (13%)
  other arithmetic  31.9 us (8%)
  blocking collectives  25.4 us (6%)
  local copies, waits for them, and re-layouts  24.3 us (6%)
  between operations  14.9 us (4%)
    all_gather x1, waiting for transfers between devices, per_device(): lax.all_gather(w_key, 'dp', axis=0, tiled=True)  59 us
    all_gather x1, waiting for transfers between devices, per_device(): lax.all_gather(w_query, 'dp', axis=0, tiled=True)  52.2 us
    all_gather x1, waiting for transfers between devices, per_device(): lax.all_gather(w_value, 'dp', axis=0, tiled=True)  49.1 us
    unnamed x7, waiting for transfers between devices  39.3 us
    all_gather x1, waiting for transfers between devices, per_device(): gathered = lax.all_gather(hidden, 'fsdp', axis=1, tiled=True)  36 us
    all_gather x1, waiting for transfers between devices, per_device(): lax.all_gather(w_out, 'dp', axis=1, tiled=True)  21.6 us
    all_gather x1, blocking collectives, per_device(): lax.all_gather(row_full, 'dp', axis=0, tiled=True)  13.2 us
    unnamed x28, local copies, waits for them, and re-layouts  11.9 us
  transfers between devices with their start and end apart: 6, of which 6 were waited for; matrix products, arithmetic and copies ran while one was open for 21% of the time, Pallas kernels for 0%

commit v1 on v0

--- a/solution.py
+++ b/solution.py
@@ -1,6 +1,10 @@
+import functools
+
 import jax
 import jax.numpy as jnp
 from jax import lax
+from jax.experimental import pallas as pl
+from jax.experimental.pallas import tpu as pltpu
 from jax.sharding import PartitionSpec as P
 
 HS = 128
@@ -59,7 +63,7 @@
     return target - jax.nn.logsumexp(logits, -1)
 
 
-def per_device(
+def per_device_any(
     hidden, lengths, mask_pos, token_ids, assignment, w_query, w_key, w_value, w_out, embed
 ):
     tokens_here = hidden.shape[0]
@@ -116,10 +120,395 @@
     scored = target_score(logits, mine_ids)
     return (states, logits, scored)
 
+F32 = jnp.float32
+BF16 = jnp.bfloat16
+VMEM_LIMIT = 48 * 1024 * 1024
+SMEM_SPEC = pl.BlockSpec(memory_space=pltpu.SMEM)
+ANY_SPEC = pl.BlockSpec(memory_space=pl.ANY)
+
+
+def params(*semantics):
+    return pltpu.CompilerParams(
+        vmem_limit_bytes=VMEM_LIMIT, dimension_semantics=semantics or None
+    )
+
+
+def norm_kernel(x_ref, out_ref):
+    blocks, _, width = x_ref.shape
+    count = blocks * width
+    values = [x_ref[b].astype(F32) for b in range(blocks)]
+    average = sum(jnp.sum(v, -1, keepdims=True) for v in values) / count
+    centred = [v - average for v in values]
+    spread = sum(jnp.sum(v * v, -1, keepdims=True) for v in centred) / count
+    scale = lax.rsqrt(spread + EPSILON)
+    for b in range(blocks):
+        out_ref[b] = (centred[b] * scale).astype(BF16)
+
+
+def norm_blocks(stack, row_block=128):
+    blocks, rows, width = stack.shape
+    spec = pl.BlockSpec((blocks, row_block, width), lambda i: (0, i, 0))
+    return pl.pallas_call(
+        norm_kernel,
+        grid=(rows // row_block,),
+        in_specs=[spec],
+        out_specs=spec,
+        out_shape=jax.ShapeDtypeStruct(stack.shape, BF16),
+        compiler_params=params("arbitrary"),
+        cost_estimate=pl.CostEstimate(
+            flops=8 * stack.size, bytes_accessed=4 * stack.size, transcendentals=rows
+        ),
+        name="norm_rows",
+    )(stack)
+
+
+def weight_copies(part, own, pieces, wbuf, sems):
+    copies = []
+    slot = 0
+    if own is not None:
+        copies.append([pltpu.make_async_copy(own, wbuf.at[0], sems.at[0])])
+        slot = 1
+    half = wbuf.shape[1] // 2
+    for k, (mine, other) in enumerate(pieces):
+        first = pl.multiple_of(part * half, half)
+        second = pl.multiple_of((1 - part) * half, half)
+        copies.append(
+            [
+                pltpu.make_async_copy(
+                    mine, wbuf.at[slot + k, pl.ds(first, half)], sems.at[slot + 2 * k]
+                ),
+                pltpu.make_async_copy(
+                    other, wbuf.at[slot + k, pl.ds(second, half)], sems.at[slot + 2 * k + 1]
+                ),
+            ]
+        )
+    return copies
+
+
+def project_kernel(scale, rotated, place_ref, x_ref, *refs):
+    own, a1, b1, a2, b2, a3, b3 = refs[:7]
+    if rotated:
+        cos_ref, sin_ref = refs[7:9]
+    out_ref, wbuf, sems = refs[-3:]
+    copies = weight_copies(place_ref[4], own, ((a1, b1), (a2, b2), (a3, b3)), wbuf, sems)
+    first_step = pl.program_id(0) == 0
+
+    @pl.when(first_step)
+    def _():
+        for group in copies:
+            for copy in group:
+                copy.start()
+
+    total = None
+    for k in range(4):
+
+        @pl.when(first_step)
+        def _():
+            for copy in copies[k]:
+                copy.wait()
+
+        term = jnp.dot(x_ref[place_ref[k]], wbuf[k], preferred_element_type=F32)
+        total = term if total is None else total + term
+    if scale is not None:
+        total = total * scale
+    if not rotated:
+        out_ref[...] = total.astype(BF16)
+        return
+    cos, sin = cos_ref[...], sin_ref[...]
+    for h in range(total.shape[1] // HS):
+        field = total[:, h * HS : (h + 1) * HS]
+        turned = pltpu.roll(field, HS // 2, 1)
+        out_ref[:, h * HS : (h + 1) * HS] = (field * cos + turned * sin).astype(BF16)
+
+
+def project(place, normed, own, pieces, turn=None, scale=None, row_block=448):
+    blocks, rows, depth = normed.shape
+    columns = own.shape[1]
+    flat = [ref for pair in pieces for ref in pair]
+    in_specs = [SMEM_SPEC, pl.BlockSpec((blocks, row_block, depth), lambda i: (0, i, 0))]
+    in_specs += [ANY_SPEC] * 7
+    operands = [place, normed, own, *flat]
+    if turn is not None:
+        in_specs += [pl.BlockSpec((row_block, HS), lambda i: (i, 0))] * 2
+        operands += list(turn)
+    return pl.pallas_call(
+        functools.partial(project_kernel, scale, turn is not None),
+        grid=(rows // row_block,),
+        in_specs=in_specs,
+        out_specs=pl.BlockSpec((row_block, columns), lambda i: (i, 0)),
+        out_shape=jax.ShapeDtypeStruct((rows, columns), BF16),
+        scratch_shapes=[
+            pltpu.VMEM((blocks, depth, columns), BF16),
+            pltpu.SemaphoreType.DMA((7,)),
+        ],
+        compiler_params=params("arbitrary"),
+        cost_estimate=pl.CostEstimate(
+            flops=2 * rows * blocks * depth * columns,
+            bytes_accessed=2 * (normed.size + blocks * depth * columns + rows * columns),
+            transcendentals=0,
+        ),
+        name="project",
+    )(*operands)
+
+
+def attend_kernel(ends_ref, q_ref, k_ref, v_ref, out_ref, *, row_block):
+    count = k_ref.shape[0]
+    keys, values = k_ref[...], v_ref[...]
+    base = pl.program_id(0) * q_ref.shape[0]
+    col = lax.broadcasted_iota(jnp.int32, (1, count), 1)
+    sequences = ends_ref.shape[0]
+    col_label = sum((col >= ends_ref[j]).astype(jnp.int32) for j in range(sequences - 1))
+    for r in range(q_ref.shape[0] // row_block):
+        span = slice(r * row_block, (r + 1) * row_block)
+        row = lax.broadcasted_iota(jnp.int32, (row_block, 1), 0) + (base + r * row_block)
+        row_label = sum((row >= ends_ref[j]).astype(jnp.int32) for j in range(sequences - 1))
+        scores = lax.dot_general(
+            q_ref[span, :], keys, (((1,), (1,)), ((), ())), preferred_element_type=F32
+        )
+        scores = jnp.where(row_label == col_label, scores, -1e30)
+        top = jnp.max(scores, -1, keepdims=True)
+        raised = jnp.exp(scores - top)
+        weights = raised * (1.0 / jnp.sum(raised, -1, keepdims=True))
+        out_ref[span, :] = jnp.dot(
+            weights.astype(BF16), values, preferred_element_type=F32
+        ).astype(BF16)
+
+
+def attention(ends, queries, key_rows, value_rows, q_block=448, row_block=224):
+    rows, columns = queries.shape
+    heads = columns // HS
+    return pl.pallas_call(
+        functools.partial(attend_kernel, row_block=row_block),
+        grid=(rows // q_block, heads),
+        in_specs=[
+            SMEM_SPEC,
+            pl.BlockSpec((q_block, HS), lambda i, h: (i, h)),
+            pl.BlockSpec((rows, HS), lambda i, h: (0, h)),
+            pl.BlockSpec((rows, HS), lambda i, h: (0, h)),
+        ],
+        out_specs=pl.BlockSpec((q_block, HS), lambda i, h: (i, h)),
+        out_shape=jax.ShapeDtypeStruct((rows, columns), BF16),
+        compiler_params=params("arbitrary", "arbitrary"),
+        cost_estimate=pl.CostEstimate(
+            flops=4 * rows * rows * columns,
+            bytes_accessed=8 * rows * columns,
+            transcendentals=rows * rows * heads,
+        ),
+        name="attention",
+    )(ends, queries, key_rows, value_rows)
+
+
+def out_kernel(with_own, pairs, place_ref, x_ref, *refs):
+    refs = list(refs)
+    own = refs.pop(0) if with_own else None
+    pieces = [(refs.pop(0), refs.pop(0)) for _ in range(pairs)]
+    shards = pairs + with_own
+    outs = [refs.pop(0) for _ in range(shards)]
+    wbuf, sems = refs
+    copies = weight_copies(place_ref[0], own, pieces, wbuf, sems)
+    for group in copies:
+        for copy in group:
+            copy.start()
+    context = x_ref[...]
+    for k in range(shards):
+        for copy in copies[k]:
+            copy.wait()
+        outs[k][...] = jnp.dot(context, wbuf[k], preferred_element_type=F32).astype(
+            outs[k].dtype
+        )
+
+
+def out_project(place, context, own, pieces, dtype):
+    rows, depth = context.shape
+    half = rows // 2
+    columns = pieces[0][0].shape[1]
+    flat = [ref for pair in pieces for ref in pair]
+    with_own = own is not None
+    operands = ([own] if with_own else []) + flat
+    shards = len(pieces) + with_own
+    return pl.pallas_call(
+        functools.partial(out_kernel, int(with_own), len(pieces)),
+        grid_spec=pltpu.PrefetchScalarGridSpec(
+            num_scalar_prefetch=1,
+            grid=(1,),
+            in_specs=[pl.BlockSpec((half, depth), lambda i, place: (place[1], 0))]
+            + [ANY_SPEC] * len(operands),
+            out_specs=[pl.BlockSpec((half, columns), lambda i, place: (0, 0))] * shards,
+            scratch_shapes=[
+                pltpu.VMEM((shards, depth, columns), BF16),
+                pltpu.SemaphoreType.DMA((2 * len(pieces) + with_own,)),
+            ],
+        ),
+        out_shape=[jax.ShapeDtypeStruct((half, columns), dtype)] * shards,
+        compiler_params=params("arbitrary"),
+        cost_estimate=pl.CostEstimate(
+            flops=2 * shards * half * depth * columns,
+            bytes_accessed=2 * (half * depth + shards * (depth + 2 * half) * columns),
+            transcendentals=0,
+        ),
+        name="out_project",
+    )(place, context, *operands)
+
+
+def tie(value, *earlier):
+    return lax.optimization_barrier((value, *earlier))[0]
+
+
+def gather_weights(weights, dp):
+    part = lax.axis_index("parts")
+    ring = lambda x, step: lax.ppermute(x, "dp", [(i, (i + step) % dp) for i in range(dp)])
+    swap = lambda x: lax.ppermute(x, "parts", [(0, 1), (1, 0)])
+    along, across = [], []
+    result = []
+    for weight in weights:
+        half = weight.shape[0] // 2
+        mine = lax.dynamic_slice_in_dim(weight, part * half, half, 0)
+        first = len(along)
+        for step in range(3):
+            i = len(along)
+            source, shift = ((mine, 1), (mine, -1), (along[first] if step == 2 else None, 1))[step]
+            if i >= 2:
+                source = tie(source, along[i - 2])
+            along.append(ring(source, shift))
+            source = along[i]
+            if i >= 2:
+                source = tie(source, across[i - 2])
+            across.append(swap(source))
+        order = (first, first + 2, first + 1)
+        result.append([(along[i], across[i]) for i in order])
+    return result
+
+
+def per_device(
+    hidden, lengths, mask_pos, token_ids, assignment, w_query, w_key, w_value, w_out, embed
+):
+    dp, fsdp = 4, 4
+    rows, width = hidden.shape
+    half = rows // 2
+    sequences = lengths.shape[0]
+    part = lax.axis_index("parts")
+    group = lax.axis_index("dp")
+    column = lax.axis_index("fsdp")
+    core = column % 2
+    ring_order = [lax.rem(group + dp - k, dp) for k in range(dp)]
+    place = jnp.stack(ring_order + [part]).astype(jnp.int32)
+
+    stack = lax.all_gather(hidden, "fsdp", axis=0, tiled=False)
+    key_in, query_in, value_in, out_in = gather_weights((w_key, w_query, w_value, w_out), dp)
+
+    segment, position, starts = layout(lengths, rows)
+    half_width = HS // 2
+    frequency = 10000.0 ** (-2.0 * jnp.arange(half_width, dtype=F32) / HS)
+    angles = position.astype(F32)[:, None] * frequency[None, :]
+    sine, cosine = jnp.sin(angles), jnp.cos(angles)
+    turn = (jnp.concatenate([cosine, cosine], -1), jnp.concatenate([-sine, sine], -1))
+    picked = starts + mask_pos
+    chosen = jnp.arange(rows, dtype=jnp.int32)[None, :] == picked[:, None]
+    local_ids = jnp.sum(jnp.where(chosen, token_ids[None, :], 0), 1)
+
+    normed = norm_blocks(stack)
+    key_rows = project(place, normed, w_key, key_in, turn)
+    queries = project(place, normed, w_query, query_in, turn, HS ** (-0.5))
+    value_rows = project(place, normed, w_value, value_in)
+    context = attention(jnp.cumsum(lengths), queries, key_rows, value_rows)
+
+    swap_core = lambda x: lax.ppermute(x, "fsdp", [(i, i ^ 1) for i in range(fsdp)])
+    keep_place = jnp.stack([part, core]).astype(jnp.int32)
+    send_place = jnp.stack([part, 1 - core]).astype(jnp.int32)
+    early = [out_in[0], out_in[2]]
+    sent = out_project(send_place, context, w_out, early, BF16)
+    sent_late = lambda c: out_project(send_place, c, None, [out_in[1]], BF16)
+    arrived = [swap_core(x) for x in sent]
+    kept = out_project(keep_place, context, w_out, early, F32)
+    late = sent_late(context)
+    arrived_late = swap_core(late[0])
+    kept_late = out_project(keep_place, context, None, [out_in[1]], F32)
+
+    def cross(k, value):
+        pairs = []
+        for z in range(dp):
+            target = ((z - k) % dp) // 2
+            for c in range(2):
+                pairs.append((z * fsdp + (1 - target) * 2 + c, z * fsdp + target * 2 + c))
+        return lax.ppermute(value, ("dp", "fsdp"), pairs)
+
+    chip, crossed = {}, {}
+    for k, keep, come in (
+        (0, kept[0], arrived[0]),
+        (1, kept[1], arrived[1]),
+        (3, kept[2], arrived[2]),
+        (2, kept_late[0], arrived_late),
+    ):
+        chip[k] = keep + come.astype(F32)
+        crossed[k] = cross(k, chip[k].astype(BF16)).astype(F32)
+
+    def block_rows(index):
+        total = stack_half(index)
+        for k in range(dp):
+            total += jnp.where(ring_order[k] == index, chip[k] + crossed[k], 0.0)
+        return total.astype(BF16)
+
+    def stack_half(index):
+        return lax.dynamic_slice(stack, (index, core * half, 0), (1, half, width))[0].astype(F32)
+
+    other_rows = swap_core(block_rows(column ^ 1))
+    my_rows = block_rows(column)
+    states = jnp.where(
+        core == 0,
+        jnp.concatenate([my_rows, other_rows], 0),
+        jnp.concatenate([other_rows, my_rows], 0),
+    )
+
+    one_hot = chosen.astype(BF16)
+    context_rows = jnp.dot(one_hot, context, preferred_element_type=F32).astype(BF16)
+    hidden_rows = jnp.einsum("sr,brw->bsw", one_hot, stack, preferred_element_type=F32)
+    piece_height = width // 2
+    by_ring = [jnp.dot(context_rows, w_out, preferred_element_type=F32)]
+    mine_part = lax.dynamic_slice_in_dim(context_rows, part * piece_height, piece_height, 1)
+    other_part = lax.dynamic_slice_in_dim(context_rows, (1 - part) * piece_height, piece_height, 1)
+    for mine, other in out_in:
+        by_ring.append(
+            jnp.dot(mine_part, mine, preferred_element_type=F32)
+            + jnp.dot(other_part, other, preferred_element_type=F32)
+        )
+    by_ring = jnp.stack(by_ring)
+    row_sum = jnp.stack(
+        [
+            lax.dynamic_index_in_dim(by_ring, lax.rem(group + dp - b, dp), 0, keepdims=False)
+            for b in range(dp)
+        ]
+    )
+    row_sum = row_sum + swap_core(row_sum)
+    row_sum = row_sum + lax.ppermute(row_sum, "fsdp", [(i, i ^ 2) for i in range(fsdp)])
+    full_rows = (hidden_rows + row_sum).astype(BF16)
+    full_rows = full_rows.transpose(1, 0, 2).reshape(sequences, dp * width)
+    extra = jnp.stack([local_ids, assignment], 1).astype(BF16)
+    extra = jnp.pad(extra, ((0, 0), (0, HS - 2)))
+    packet = jnp.concatenate([full_rows, extra], 1)
+    packets = [packet] + [
+        lax.ppermute(packet, "dp", [(i, (i + s) % dp) for i in range(dp)]) for s in range(1, dp)
+    ]
+    packets = jnp.concatenate(packets, 0)
+    all_rows = packets[:, : dp * width]
+    all_ids = packets[:, dp * width].astype(jnp.int32)
+    all_owner = packets[:, dp * width + 1].astype(jnp.int32)
+    owned = group * sequences + jnp.arange(sequences, dtype=jnp.int32)
+    match = all_owner[None, :] == owned[:, None]
+    mine_rows = jnp.dot(match.astype(BF16), all_rows, preferred_element_type=F32)
+    mine_ids = jnp.sum(jnp.where(match, all_ids[None, :], 0), 1).astype(jnp.int32)
+    normed_rows = norm_rows(mine_rows).astype(BF16)
+    logits = jnp.dot(normed_rows, embed.T, preferred_element_type=F32)
+    scored = target_score(logits, mine_ids)
+    return (states, logits, scored)
+
+
+def ring_fits(mesh):
+    return (mesh.shape["parts"], mesh.shape["dp"], mesh.shape["fsdp"]) == (2, 4, 4)
+
 
 def solution(mesh):
     return jax.shard_map(
-        per_device,
+        per_device if ring_fits(mesh) else per_device_any,
         mesh=mesh,
         in_specs=(
             P(("parts", "dp"), "fsdp"),

time: 407 us -> 250 us (0.61)
  waiting for transfers between devices: 257 us -> 105 us
  Pallas kernels: 0 us -> 59.1 us
  matrix products: 52.1 us -> 5.2 us
  starting transfers between devices: 0.23 us -> 44.4 us
  blocking collectives: 25.4 us -> 0 us
  other arithmetic: 31.9 us -> 8.66 us
  local copies, waits for them, and re-layouts: 24.3 us -> 11.7 us
    all_gather x5 -> x1, waiting for transfers between devices: 218 us -> 0.01 us  [per_device(): stack = lax.all_gather(hidden, 'fsdp', axis=0, tiled=False)]
    ppermute x0 -> x38, waiting for transfers between devices: none -> 105 us  [the longest x12 43 us: gather_weights(): swap = lambda x: lax.ppermute(x, 'parts', [(0, 1), (1, 0)])]
    pallas_call x0 -> x9, Pallas kernels: none -> 59.1 us  [the longest x3 26.5 us: project(): pl.pallas_call(functools.partial(project_kernel, scale, turn is not None)...]
    dot_general x17 -> x11, matrix products: 52.1 us -> 5.2 us  [the longest x3 1.66 us: per_device(): jnp.dot(mine_part, mine, preferred_element_type=F32)]
    ppermute x0 -> x38, starting transfers between devices: none -> 44.3 us  [the longest x12 16 us: gather_weights(): lax.ppermute(x, 'dp', [(i, (i + step) % dp) for i in range(dp)])]
    unnamed x7 -> x1, waiting for transfers between devices: 39.3 us -> 0.68 us
    all_gather x2 -> x0, blocking collectives: 18.4 us -> none  [the longest x1 13.2 us: per_device(): lax.all_gather(row_full, 'dp', axis=0, tiled=True)]
    reshape x3 -> x0, local copies, waits for them, and re-layouts: 8.07 us -> none  [the longest x1 3.2 us: per_device(): (query_sum * HS ** (-0.5)).reshape(tokens_here, heads_here, HS)]
  transfers between devices with their start and end apart: 6 -> 39, of which waited for: 6 -> 22; matrix products, arithmetic and copies ran while one was open for 21% -> 6% of each run, Pallas kernels for 0% -> 24%
where the time goes in v1:
time: 250 us; the launch traced here: 249 us
  waiting for transfers between devices  105 us (42%)
  Pallas kernels  59.1 us (24%)
  starting transfers between devices  44.4 us (18%)
  between operations  14.7 us (6%)
  local copies, waits for them, and re-layouts  11.7 us (5%)
  other arithmetic  8.66 us (3%)
  matrix products  5.2 us (2%)
    ppermute x12, waiting for transfers between devices, gather_weights(): swap = lambda x: lax.ppermute(x, 'parts', [(0, 1), (1, 0)])  43 us
    ppermute x12, waiting for transfers between devices, gather_weights(): lax.ppermute(x, 'dp', [(i, (i + step) % dp) for i in range(dp)])  37.1 us
    pallas_call x3, Pallas kernels, project(): pl.pallas_call(functools.partial(project_kernel, scale, turn is not None)...  26.5 us
    ppermute x4, waiting for transfers between devices, cross(): return lax.ppermute(value, ('dp', 'fsdp'), pairs)  20.3 us
    ppermute x12, starting transfers between devices, gather_weights(): lax.ppermute(x, 'dp', [(i, (i + step) % dp) for i in range(dp)])  16 us
    pallas_call x1, Pallas kernels, attention(): pl.pallas_call(functools.partial(attend_kernel, row_block=row_block), gri...  14.3 us
    ppermute x12, starting transfers between devices, gather_weights(): swap = lambda x: lax.ppermute(x, 'parts', [(0, 1), (1, 0)])  14.2 us
    pallas_call x4, Pallas kernels, out_project(): pl.pallas_call(functools.partial(out_kernel, int(with_own), len(pieces)),...  11.4 us
  transfers between devices with their start and end apart: 39, of which 22 were waited for; matrix products, arithmetic and copies ran while one was open for 6% of the time, Pallas kernels for 24%

profile of v1, /device:TPU:0, one launch (start us, length us, event | category | flops | bytes accessed | tf_op | source)
XLA Modules:
  0.0 249.0 jit_solution(9775943262096210387)
XLA Ops:
  9.2 5.0 %collective-permute-start = (bf16[320,640]{1,0:T(8,128)(2,1)}, bf16[320,640]{1,0:T(8,128)(2,1)S(1)}, u32[]{:S(2)}, u32[]{:S(2)}) collective-permute-start(bf16[320,640]{1,0:T(8,128)(2,1)} %constant_dynamic-slice_fusion.8), channel_id=1, source_target_pairs={{0,12},{4,0},{8,4},{12,8},{1,13},{5,1},{9,5},{13,9},{2,14},{6,2},{... | collective-permute-start | bytes 1228808 | tf_op jit(solution)/shard_map/ppermute | solution.py:359
  15.2 9.2 %collective-permute-done.refs_5_ = bf16[320,640]{1,0:T(8,128)(2,1)S(1)} collective-permute-done((bf16[320,640]{1,0:T(8,128)(2,1)}, bf16[320,640]{1,0:T(8,128)(2,1)S(1)}, u32[]{:S(2)}, u32[]{:S(2)}) %collective-permute-start) | collective-permute-done | bytes 409632 | tf_op jit(solution)/shard_map/ppermute | solution.py:359
  24.4 9.6 %collective-permute-done.6.refs_1_ = bf16[320,640]{1,0:T(8,128)(2,1)S(1)} collective-permute-done((bf16[320,640]{1,0:T(8,128)(2,1)}, bf16[320,640]{1,0:T(8,128)(2,1)S(1)}, u32[]{:S(2)}, u32[]{:S(2)}) %collective-permute-start.6) | collective-permute-done | bytes 409632 | tf_op jit(solution)/shard_map/ppermute | solution.py:359
  34.0 1.6 collective-permute-start.7
  35.6 1.5 collective-permute-start.2
  37.7 5.0 %collective-permute-done.1.refs_1_ = bf16[320,640]{1,0:T(8,128)(2,1)S(1)} collective-permute-done((bf16[320,640]{1,0:T(8,128)(2,1)}, bf16[320,640]{1,0:T(8,128)(2,1)S(1)}, u32[]{:S(2)}, u32[]{:S(2)}) %collective-permute-start.1) | collective-permute-done | bytes 409632 | tf_op jit(solution)/shard_map/ppermute | solution.py:359
  42.8 5.3 %collective-permute-done.2.refs_6_ = bf16[320,640]{1,0:T(8,128)(2,1)} collective-permute-done((bf16[320,640]{1,0:T(8,128)(2,1)S(1)}, bf16[320,640]{1,0:T(8,128)(2,1)}, u32[]{:S(2)}, u32[]{:S(2)}) %collective-permute-start.2) | collective-permute-done | bytes 409632 | tf_op jit(solution)/shard_map/ppermute | solution.py:360
  48.1 1.5 collective-permute-start.3
  49.6 1.9 collective-permute-done.7.refs_3_
  51.6 2.1 collective-permute-start.8
  53.6 3.2 %collective-permute-done.9.refs_2_ = bf16[320,640]{1,0:T(8,128)(2,1)} collective-permute-done((bf16[320,640]{1,0:T(8,128)(2,1)S(1)}, bf16[320,640]{1,0:T(8,128)(2,1)}, u32[]{:S(2)}, u32[]{:S(2)}) %collective-permute-start.9) | collective-permute-done | bytes 409632 | tf_op jit(solution)/shard_map/ppermute | solution.py:360
  56.9 1.5 collective-permute-start.10
  58.7 6.9 %collective-permute-done.3.refs_2_ = bf16[320,640]{1,0:T(8,128)(2,1)} collective-permute-done((bf16[320,640]{1,0:T(8,128)(2,1)S(1)}, bf16[320,640]{1,0:T(8,128)(2,1)}, u32[]{:S(2)}, u32[]{:S(2)}) %collective-permute-start.3) | collective-permute-done | bytes 409632 | tf_op jit(solution)/shard_map/ppermute | solution.py:360
  65.6 1.5 collective-permute-start.5
  68.1 6.4 %collective-permute-done.10.refs_4_ = bf16[320,640]{1,0:T(8,128)(2,1)} collective-permute-done((bf16[320,640]{1,0:T(8,128)(2,1)S(1)}, bf16[320,640]{1,0:T(8,128)(2,1)}, u32[]{:S(2)}, u32[]{:S(2)}) %collective-permute-start.10) | collective-permute-done | bytes 409632 | tf_op jit(solution)/shard_map/ppermute | solution.py:360
  74.4 1.5 collective-permute-start.11
  76.0 3.8 %collective-permute-start.16 = (bf16[320,640]{1,0:T(8,128)(2,1)S(1)}, bf16[320,640]{1,0:T(8,128)(2,1)S(1)}, u32[]{:S(2)}, u32[]{:S(2)}) collective-permute-start(bf16[320,640]{1,0:T(8,128)(2,1)S(1)} %constant_dynamic-slice_fusion.7), channel_id=1, source_target_pairs={{0,12},{4,0},{8,4},{12,8},{1,13},{5,1},{9,5},{13,9},{2,14},{6,2},{... | collective-permute-start | bytes 1228808 | tf_op jit(solution)/shard_map/ppermute | solution.py:359
  80.7 7.8 %collective-permute-done.11.refs_6_ = bf16[320,640]{1,0:T(8,128)(2,1)S(1)} collective-permute-done((bf16[320,640]{1,0:T(8,128)(2,1)}, bf16[320,640]{1,0:T(8,128)(2,1)S(1)}, u32[]{:S(2)}, u32[]{:S(2)}) %collective-permute-start.11) | collective-permute-done | bytes 409632 | tf_op jit(solution)/shard_map/ppermute | solution.py:360
  89.3 1.5 collective-permute-start.13
  95.2 6.5 %collective-permute-done.13.refs_2_ = bf16[320,640]{1,0:T(8,128)(2,1)S(1)} collective-permute-done((bf16[320,640]{1,0:T(8,128)(2,1)S(1)}, bf16[320,640]{1,0:T(8,128)(2,1)S(1)}, u32[]{:S(2)}, u32[]{:S(2)}) %collective-permute-start.13) | collective-permute-done | bytes 409632 | tf_op jit(solution)/shard_map/ppermute | solution.py:360
  102.5 2.6 %collective-permute-done.14.refs_3_ = bf16[320,640]{1,0:T(8,128)(2,1)} collective-permute-done((bf16[320,640]{1,0:T(8,128)(2,1)S(1)}, bf16[320,640]{1,0:T(8,128)(2,1)}, u32[]{:S(2)}, u32[]{:S(2)}) %collective-permute-start.14) | collective-permute-done | bytes 409632 | tf_op jit(solution)/shard_map/ppermute | solution.py:359
  105.5 5.0 %collective-permute-done.17.refs_6_ = bf16[320,640]{1,0:T(8,128)(2,1)S(1)} collective-permute-done((bf16[320,640]{1,0:T(8,128)(2,1)S(1)}, bf16[320,640]{1,0:T(8,128)(2,1)S(1)}, u32[]{:S(2)}, u32[]{:S(2)}) %collective-permute-start.17) | collective-permute-done | bytes 409632 | tf_op jit(solution)/shard_map/ppermute | solution.py:360
  111.3 1.5 collective-permute-start.19
  112.8 2.1 collective-permute-start.20
  115.5 1.7 fusion.15
  117.5 1.9 collective-permute-done.15.refs_4_
  119.4 7.9 %collective-permute-done.20.refs_3_ = bf16[320,640]{1,0:T(8,128)(2,1)} collective-permute-done((bf16[320,640]{1,0:T(8,128)(2,1)}, bf16[320,640]{1,0:T(8,128)(2,1)}, u32[]{:S(2)}, u32[]{:S(2)}) %collective-permute-start.20) | collective-permute-done | bytes 409632 | tf_op jit(solution)/shard_map/ppermute | solution.py:359
  130.1 6.8 %norm_rows.1.x_ref = bf16[4,896,640]{2,1,0:T(8,128)(2,1)S(1)} custom-call(bf16[4,896,640]{2,1,0:T(8,128)(2,1)} %bitcast.51), custom_call_target="tpu_custom_call" | custom-call | flops 18350080 | bytes 9175040 | tf_op jit(solution)/shard_map/norm_rows/pallas_call | solution.py:151
  136.9 2.1 copy-done.3
  139.1 9.0 %project.3.q_ref = bf16[896,640]{1,0:T(8,128)(2,1)S(1)} custom-call(s32[5]{0:T(128)S(1)} %stack.73.place_ref, bf16[4,896,640]{2,1,0:T(8,128)(2,1)} %copy-done.3, bf16[640,640]{1,0:T(8,128)(2,1)S(1)} %copy-done.8, bf16[320,640]{1,0:T(8,128)(2,1)S(1)} %copy-done.20, bf16[320,640]{1,0:T(8,128)(2,1)} %collective-permute-done.3.refs_2_, ...), custom_call_target="tpu_custom_call" | custom-call | flops 2936012800 | bytes 9011200 | tf_op jit(solution)/shard_map/project/pallas_call | solution.py:234
  148.2 9.0 %project.4.k_ref = bf16[896,640]{1,0:T(8,128)(2,1)S(1)} custom-call(s32[5]{0:T(128)S(1)} %stack.73.place_ref, bf16[4,896,640]{2,1,0:T(8,128)(2,1)} %copy-done.3, bf16[640,640]{1,0:T(8,128)(2,1)S(1)} %copy-done.10, bf16[320,640]{1,0:T(8,128)(2,1)S(1)} %copy-done.16, bf16[320,640]{1,0:T(8,128)(2,1)} %collective-permute-done.9.refs_2_, ...), custom_call_target="tpu_custom_call" | custom-call | flops 2936012800 | bytes 9011200 | tf_op jit(solution)/shard_map/project/pallas_call | solution.py:234
  157.3 8.5 %project.5.v_ref = bf16[896,640]{1,0:T(8,128)(2,1)S(1)} custom-call(s32[5]{0:T(128)S(1)} %stack.73.place_ref, bf16[4,896,640]{2,1,0:T(8,128)(2,1)} %copy-done.3, bf16[640,640]{1,0:T(8,128)(2,1)S(1)} %copy-done.12, bf16[320,640]{1,0:T(8,128)(2,1)S(1)} %copy-done.24, bf16[320,640]{1,0:T(8,128)(2,1)S(1)} %copy-done.30, ...), custom_call_target="tpu_custom_call" | custom-call | flops 2936012800 | bytes 9011200 | tf_op jit(solution)/shard_map/project/pallas_call | solution.py:234
  165.8 14.3 %attention.1.x_ref = bf16[896,640]{1,0:T(8,128)(2,1)S(1)} custom-call(s32[3]{0:T(128)S(1)} %bitcast.50, bf16[896,640]{1,0:T(8,128)(2,1)S(1)} %project.3.q_ref, bf16[896,640]{1,0:T(8,128)(2,1)S(1)} %project.4.k_ref, bf16[896,640]{1,0:T(8,128)(2,1)S(1)} %project.5.v_ref), custom_call_target="tpu_custom_call" | custom-call | flops 2055208960 | bytes 4587520 | tf_op jit(solution)/shard_map/attention/pallas_call | solution.py:280
  181.4 3.4 %out_project.5 = (bf16[448,640]{1,0:T(8,128)(2,1)S(1)}, bf16[448,640]{1,0:T(8,128)(2,1)S(1)}, bf16[448,640]{1,0:T(8,128)(2,1)S(1)}) custom-call(s32[2]{0:T(128)S(1)} %pad_add_fusion.1.place_ref, bf16[896,640]{1,0:T(8,128)(2,1)S(1)} %attention.1.x_ref, bf16[640,640]{1,0:T(8,128)(2,1)S(1)} %copy-done.4, bf16[320,640]{1,0:T(8,128)(2,1)S(1)} %collective-permute-done.18.refs_1_, ...), custom_call_target="tpu_custom_call" | custom-call | flops 1101004800 | bytes 6471680 | tf_op jit(solution)/shard_map/out_project/pallas_call | solution.py:329
  189.9 4.6 %out_project.4 = (f32[448,640]{1,0:T(8,128)S(1)}, f32[448,640]{1,0:T(8,128)S(1)}, f32[448,640]{1,0:T(8,128)S(1)}) custom-call(s32[2]{0:T(128)S(1)} %pad_add_fusion.place_ref, bf16[896,640]{1,0:T(8,128)(2,1)} %copy-done.1, bf16[640,640]{1,0:T(8,128)(2,1)S(1)} %copy-done.4, bf16[320,640]{1,0:T(8,128)(2,1)S(1)} %collective-permute-done.18.refs_1_, ...), custom_call_target="tpu_custom_call" | custom-call | flops 1101004800 | bytes 6471680 | tf_op jit(solution)/shard_map/out_project/pallas_call | solution.py:329
  194.6 1.6 collective-permute-start.34
  196.1 1.7 out_project.6
  198.7 2.4 collective-permute-start.37
  201.9 1.7 out_project.7
  203.7 2.1 collective-permute-done.36
  207.6 1.3 collective-permute-start.23
  209.1 4.6 %collective-permute-start.25 = (bf16[448,640]{1,0:T(8,128)(2,1)S(1)}, bf16[448,640]{1,0:T(8,128)(2,1)S(1)}, u32[]{:S(2)}, u32[]{:S(2)}) collective-permute-start(bf16[448,640]{1,0:T(8,128)(2,1)S(1)} %fusion.12), channel_id=1, source_target_pairs={{0,2},{1,3},{6,4},{7,5},{10,8},{11,9},{12,14},{13,15},{16,18},{17,... | collective-permute-start | bytes 1720328 | tf_op jit(solution)/shard_map/ppermute | solution.py:433
  213.8 1.3 collective-permute-start.29
  215.3 1.3 collective-permute-start.31
  217.3 8.1 %collective-permute-done.23 = bf16[448,640]{1,0:T(8,128)(2,1)S(1)} collective-permute-done((bf16[448,640]{1,0:T(8,128)(2,1)S(1)}, bf16[448,640]{1,0:T(8,128)(2,1)S(1)}, u32[]{:S(2)}, u32[]{:S(2)}) %collective-permute-start.23) | collective-permute-done | bytes 573472 | tf_op jit(solution)/shard_map/ppermute | solution.py:433
  225.4 1.6 collective-permute-done.25
  227.1 10.6 %collective-permute-done.29 = bf16[448,640]{1,0:T(8,128)(2,1)S(1)} collective-permute-done((bf16[448,640]{1,0:T(8,128)(2,1)S(1)}, bf16[448,640]{1,0:T(8,128)(2,1)S(1)}, u32[]{:S(2)}, u32[]{:S(2)}) %collective-permute-start.29) | collective-permute-done | bytes 573472 | tf_op jit(solution)/shard_map/ppermute | solution.py:433
  240.7 1.5 maximum_select_fusion
  (177 shorter events, 30.8 us)
Async XLA Ops:
  7.2 209.6 %copy-start = (bf16[33,2560]{1,0:T(8,128)(2,1)S(1)}, bf16[33,2560]{1,0:T(8,128)(2,1)}, u32[]{:S(2)}) copy-start(bf16[33,2560]{1,0:T(8,128)(2,1)} %param.19) | copy-start | bytes 506884
  7.2 51.1 %copy-start.33 = (s32[896]{0:T(1024)S(1)}, s32[896]{0:T(1024)}, u32[]{:S(2)}) copy-start(s32[896]{0:T(1024)} %param.13) | copy-start | bytes 10756
  7.2 51.4 %copy-start.11 = (bf16[640,640]{1,0:T(8,128)(2,1)S(1)}, bf16[640,640]{1,0:T(8,128)(2,1)}, u32[]{:S(2)}) copy-start(bf16[640,640]{1,0:T(8,128)(2,1)} %refs_0_.7) | copy-start | bytes 2457604
  7.3 122.8 %all-gather.3.cloned.1.call-start = ((), (), s32[]{:S(2)}) async-start(), calls=%async_computation | async-start | bytes 5734400 | tf_op jit(solution)/shard_map/all_gather | solution.py:396
  8.4 71.6 %copy-start.4 = (bf16[640,640]{1,0:T(8,128)(2,1)S(1)}, bf16[640,640]{1,0:T(8,128)(2,1)}, u32[]{:S(2)}) copy-start(bf16[640,640]{1,0:T(8,128)(2,1)} %refs_0_.9) | copy-start | bytes 2457604
  9.2 15.2 %collective-permute-start = (bf16[320,640]{1,0:T(8,128)(2,1)}, bf16[320,640]{1,0:T(8,128)(2,1)S(1)}, u32[]{:S(2)}, u32[]{:S(2)}) collective-permute-start(bf16[320,640]{1,0:T(8,128)(2,1)} %constant_dynamic-slice_fusion.8), channel_id=1, source_target_pairs={{0,12},{4,0},{8,4},{12,8},{1,13},{5,1},{9,5},{13,9},{2,14},{6,2},{... | collective-permute-start | bytes 1228808 | tf_op jit(solution)/shard_map/ppermute | solution.py:359
  14.2 19.8 %collective-permute-start.6 = (bf16[320,640]{1,0:T(8,128)(2,1)}, bf16[320,640]{1,0:T(8,128)(2,1)S(1)}, u32[]{:S(2)}, u32[]{:S(2)}) collective-permute-start(bf16[320,640]{1,0:T(8,128)(2,1)} %constant_dynamic-slice_fusion.8), channel_id=1, source_target_pairs={{0,4},{4,8},{8,12},{12,0},{1,5},{5,9},{9,13},{13,1},{2,6},{6,10},{... | collective-permute-start | bytes 1228808 | tf_op jit(solution)/shard_map/ppermute | solution.py:359
  24.4 92.8 %copy-start.13 = (bf16[320,640]{1,0:T(8,128)(2,1)}, bf16[320,640]{1,0:T(8,128)(2,1)S(1)}, u32[]{:S(2)}) copy-start(bf16[320,640]{1,0:T(8,128)(2,1)S(1)} %collective-permute-done.refs_5_) | copy-start | bytes 1228804
  24.4 18.4 %collective-permute-start.1 = (bf16[320,640]{1,0:T(8,128)(2,1)}, bf16[320,640]{1,0:T(8,128)(2,1)S(1)}, u32[]{:S(2)}, u32[]{:S(2)}) collective-permute-start(bf16[320,640]{1,0:T(8,128)(2,1)} %constant_dynamic-slice_fusion.9), channel_id=1, source_target_pairs={{0,4},{4,8},{8,12},{12,0},{1,5},{5,9},{9,13},{13,1},{2,6},{6,10},{... | collective-permute-start | bytes 1228808 | tf_op jit(solution)/shard_map/ppermute | solution.py:359
  34.0 83.2 %copy-start.15 = (bf16[320,640]{1,0:T(8,128)(2,1)}, bf16[320,640]{1,0:T(8,128)(2,1)S(1)}, u32[]{:S(2)}) copy-start(bf16[320,640]{1,0:T(8,128)(2,1)S(1)} %collective-permute-done.6.refs_1_) | copy-start | bytes 1228804
  34.0 17.6 %collective-permute-start.7 = (bf16[320,640]{1,0:T(8,128)(2,1)S(1)}, bf16[320,640]{1,0:T(8,128)(2,1)S(1)}, u32[]{:S(2)}, u32[]{:S(2)}) collective-permute-start(bf16[320,640]{1,0:T(8,128)(2,1)S(1)} %collective-permute-done.6.refs_1_), channel_id=1, source_target_pairs={{0,4},{4,8},{8,12},{12,0},{1,5},{5,9},{9,13},{13,1},{2,6},{6,10},{... | collective-permute-start | bytes 1228808 | tf_op jit(solution)/shard_map/ppermute | solution.py:359
  35.6 12.5 %collective-permute-start.2 = (bf16[320,640]{1,0:T(8,128)(2,1)S(1)}, bf16[320,640]{1,0:T(8,128)(2,1)}, u32[]{:S(2)}, u32[]{:S(2)}) collective-permute-start(bf16[320,640]{1,0:T(8,128)(2,1)S(1)} %collective-permute-done.refs_5_), channel_id=1, source_target_pairs={{0,16},{16,0},{1,17},{17,1},{2,18},{18,2},{3,19},{19,3},{4,20},{20... | collective-permute-start | bytes 1228808 | tf_op jit(solution)/shard_map/ppermute | solution.py:360
  37.1 19.8 %collective-permute-start.9 = (bf16[320,640]{1,0:T(8,128)(2,1)S(1)}, bf16[320,640]{1,0:T(8,128)(2,1)}, u32[]{:S(2)}, u32[]{:S(2)}) collective-permute-start(bf16[320,640]{1,0:T(8,128)(2,1)S(1)} %collective-permute-done.6.refs_1_), channel_id=1, source_target_pairs={{0,16},{16,0},{1,17},{17,1},{2,18},{18,2},{3,19},{19,3},{4,20},{20... | collective-permute-start | bytes 1228808 | tf_op jit(solution)/shard_map/ppermute | solution.py:360
  42.8 67.7 %copy-start.19 = (bf16[320,640]{1,0:T(8,128)(2,1)}, bf16[320,640]{1,0:T(8,128)(2,1)S(1)}, u32[]{:S(2)}) copy-start(bf16[320,640]{1,0:T(8,128)(2,1)S(1)} %collective-permute-done.1.refs_1_) | copy-start | bytes 1228804
  48.1 17.6 %collective-permute-start.3 = (bf16[320,640]{1,0:T(8,128)(2,1)S(1)}, bf16[320,640]{1,0:T(8,128)(2,1)}, u32[]{:S(2)}, u32[]{:S(2)}) collective-permute-start(bf16[320,640]{1,0:T(8,128)(2,1)S(1)} %collective-permute-done.1.refs_1_), channel_id=1, source_target_pairs={{0,16},{16,0},{1,17},{17,1},{2,18},{18,2},{3,19},{19,3},{4,20},{20... | collective-permute-start | bytes 1228808 | tf_op jit(solution)/shard_map/ppermute | solution.py:360
  49.6 16.0 %collective-permute-start.4 = (bf16[320,640]{1,0:T(8,128)(2,1)S(1)}, bf16[320,640]{1,0:T(8,128)(2,1)}, u32[]{:S(2)}, u32[]{:S(2)}) collective-permute-start(bf16[320,640]{1,0:T(8,128)(2,1)S(1)} %collective-permute-done.1.refs_1_), channel_id=1, source_target_pairs={{0,4},{4,8},{8,12},{12,0},{1,5},{5,9},{9,13},{13,1},{2,6},{6,10},{... | collective-permute-start | bytes 1228808 | tf_op jit(solution)/shard_map/ppermute | solution.py:359
  51.6 61.2 %copy-start.17 = (bf16[320,640]{1,0:T(8,128)(2,1)}, bf16[320,640]{1,0:T(8,128)(2,1)S(1)}, u32[]{:S(2)}) copy-start(bf16[320,640]{1,0:T(8,128)(2,1)S(1)} %collective-permute-done.7.refs_3_) | copy-start | bytes 1228804
  51.6 16.5 %collective-permute-start.8 = (bf16[320,640]{1,0:T(8,128)(2,1)}, bf16[320,640]{1,0:T(8,128)(2,1)}, u32[]{:S(2)}, u32[]{:S(2)}) collective-permute-start(bf16[320,640]{1,0:T(8,128)(2,1)} %constant_dynamic-slice_fusion.9), channel_id=1, source_target_pairs={{0,12},{4,0},{8,4},{12,8},{1,13},{5,1},{9,5},{13,9},{2,14},{6,2},{... | collective-permute-start | bytes 1228808 | tf_op jit(solution)/shard_map/ppermute | solution.py:359
  56.9 17.6 %collective-permute-start.10 = (bf16[320,640]{1,0:T(8,128)(2,1)S(1)}, bf16[320,640]{1,0:T(8,128)(2,1)}, u32[]{:S(2)}, u32[]{:S(2)}) collective-permute-start(bf16[320,640]{1,0:T(8,128)(2,1)S(1)} %collective-permute-done.7.refs_3_), channel_id=1, source_target_pairs={{0,16},{16,0},{1,17},{17,1},{2,18},{18,2},{3,19},{19,3},{4,20},{20... | collective-permute-start | bytes 1228808 | tf_op jit(solution)/shard_map/ppermute | solution.py:360
  65.6 26.2 %collective-permute-start.5 = (bf16[320,640]{1,0:T(8,128)(2,1)}, bf16[320,640]{1,0:T(8,128)(2,1)S(1)}, u32[]{:S(2)}, u32[]{:S(2)}) collective-permute-start(bf16[320,640]{1,0:T(8,128)(2,1)} %collective-permute-done.4.refs_3_), channel_id=1, source_target_pairs={{0,16},{16,0},{1,17},{17,1},{2,18},{18,2},{3,19},{19,3},{4,20},{20... | collective-permute-start | bytes 1228808 | tf_op jit(solution)/shard_map/ppermute | solution.py:360
  74.4 14.1 %collective-permute-start.11 = (bf16[320,640]{1,0:T(8,128)(2,1)}, bf16[320,640]{1,0:T(8,128)(2,1)S(1)}, u32[]{:S(2)}, u32[]{:S(2)}) collective-permute-start(bf16[320,640]{1,0:T(8,128)(2,1)} %collective-permute-done.8.refs_5_), channel_id=1, source_target_pairs={{0,16},{16,0},{1,17},{17,1},{2,18},{18,2},{3,19},{19,3},{4,20},{20... | collective-permute-start | bytes 1228808 | tf_op jit(solution)/shard_map/ppermute | solution.py:360
  75.9 13.4 %collective-permute-start.12 = (bf16[320,640]{1,0:T(8,128)(2,1)S(1)}, bf16[320,640]{1,0:T(8,128)(2,1)S(1)}, u32[]{:S(2)}, u32[]{:S(2)}) collective-permute-start(bf16[320,640]{1,0:T(8,128)(2,1)S(1)} %constant_dynamic-slice_fusion.7), channel_id=1, source_target_pairs={{0,4},{4,8},{8,12},{12,0},{1,5},{5,9},{9,13},{13,1},{2,6},{6,10},{... | collective-permute-start | bytes 1228808 | tf_op jit(solution)/shard_map/ppermute | solution.py:359
  76.0 16.7 %collective-permute-start.16 = (bf16[320,640]{1,0:T(8,128)(2,1)S(1)}, bf16[320,640]{1,0:T(8,128)(2,1)S(1)}, u32[]{:S(2)}, u32[]{:S(2)}) collective-permute-start(bf16[320,640]{1,0:T(8,128)(2,1)S(1)} %constant_dynamic-slice_fusion.7), channel_id=1, source_target_pairs={{0,12},{4,0},{8,4},{12,8},{1,13},{5,1},{9,5},{13,9},{2,14},{6,2},{... | collective-permute-start | bytes 1228808 | tf_op jit(solution)/shard_map/ppermute | solution.py:359
  89.3 12.4 %collective-permute-start.13 = (bf16[320,640]{1,0:T(8,128)(2,1)S(1)}, bf16[320,640]{1,0:T(8,128)(2,1)S(1)}, u32[]{:S(2)}, u32[]{:S(2)}) collective-permute-start(bf16[320,640]{1,0:T(8,128)(2,1)S(1)} %collective-permute-done.12.refs_1_), channel_id=1, source_target_pairs={{0,16},{16,0},{1,17},{17,1},{2,18},{18,2},{3,19},{19,3},{4,20},{20... | collective-permute-start | bytes 1228808 | tf_op jit(solution)/shard_map/ppermute | solution.py:360
  90.8 14.2 %collective-permute-start.14 = (bf16[320,640]{1,0:T(8,128)(2,1)S(1)}, bf16[320,640]{1,0:T(8,128)(2,1)}, u32[]{:S(2)}, u32[]{:S(2)}) collective-permute-start(bf16[320,640]{1,0:T(8,128)(2,1)S(1)} %collective-permute-done.12.refs_1_), channel_id=1, source_target_pairs={{0,4},{4,8},{8,12},{12,0},{1,5},{5,9},{9,13},{13,1},{2,6},{6,10},{... | collective-permute-start | bytes 1228808 | tf_op jit(solution)/shard_map/ppermute | solution.py:359
  92.6 17.9 %collective-permute-start.17 = (bf16[320,640]{1,0:T(8,128)(2,1)S(1)}, bf16[320,640]{1,0:T(8,128)(2,1)S(1)}, u32[]{:S(2)}, u32[]{:S(2)}) collective-permute-start(bf16[320,640]{1,0:T(8,128)(2,1)S(1)} %collective-permute-done.16.refs_5_), channel_id=1, source_target_pairs={{0,16},{16,0},{1,17},{17,1},{2,18},{18,2},{3,19},{19,3},{4,20},{20... | collective-permute-start | bytes 1228808 | tf_op jit(solution)/shard_map/ppermute | solution.py:360
  93.9 17.3 %collective-permute-start.18 = (bf16[320,640]{1,0:T(8,128)(2,1)}, bf16[320,640]{1,0:T(8,128)(2,1)S(1)}, u32[]{:S(2)}, u32[]{:S(2)}) collective-permute-start(bf16[320,640]{1,0:T(8,128)(2,1)} %constant_dynamic-slice_fusion.6), channel_id=1, source_target_pairs={{0,4},{4,8},{8,12},{12,0},{1,5},{5,9},{9,13},{13,1},{2,6},{6,10},{... | collective-permute-start | bytes 1228808 | tf_op jit(solution)/shard_map/ppermute | solution.py:359
  105.0 14.4 %collective-permute-start.15 = (bf16[320,640]{1,0:T(8,128)(2,1)}, bf16[320,640]{1,0:T(8,128)(2,1)}, u32[]{:S(2)}, u32[]{:S(2)}) collective-permute-start(bf16[320,640]{1,0:T(8,128)(2,1)} %collective-permute-done.14.refs_3_), channel_id=1, source_target_pairs={{0,16},{16,0},{1,17},{17,1},{2,18},{18,2},{3,19},{19,3},{4,20},{20... | collective-permute-start | bytes 1228808 | tf_op jit(solution)/shard_map/ppermute | solution.py:360
  111.3 17.0 %collective-permute-start.19 = (bf16[320,640]{1,0:T(8,128)(2,1)S(1)}, bf16[320,640]{1,0:T(8,128)(2,1)S(1)}, u32[]{:S(2)}, u32[]{:S(2)}) collective-permute-start(bf16[320,640]{1,0:T(8,128)(2,1)S(1)} %collective-permute-done.18.refs_1_), channel_id=1, source_target_pairs={{0,16},{16,0},{1,17},{17,1},{2,18},{18,2},{3,19},{19,3},{4,20},{20... | collective-permute-start | bytes 1228808 | tf_op jit(solution)/shard_map/ppermute | solution.py:360
  112.8 14.5 %collective-permute-start.20 = (bf16[320,640]{1,0:T(8,128)(2,1)}, bf16[320,640]{1,0:T(8,128)(2,1)}, u32[]{:S(2)}, u32[]{:S(2)}) collective-permute-start(bf16[320,640]{1,0:T(8,128)(2,1)} %constant_dynamic-slice_fusion.6), channel_id=1, source_target_pairs={{0,12},{4,0},{8,4},{12,8},{1,13},{5,1},{9,5},{13,9},{2,14},{6,2},{... | collective-permute-start | bytes 1228808 | tf_op jit(solution)/shard_map/ppermute | solution.py:359
  114.8 14.2 %collective-permute-start.26 = (bf16[320,640]{1,0:T(8,128)(2,1)S(1)}, bf16[320,640]{1,0:T(8,128)(2,1)S(1)}, u32[]{:S(2)}, u32[]{:S(2)}) collective-permute-start(bf16[320,640]{1,0:T(8,128)(2,1)S(1)} %collective-permute-done.18.refs_1_), channel_id=1, source_target_pairs={{0,4},{4,8},{8,12},{12,0},{1,5},{5,9},{9,13},{13,1},{2,6},{6,10},{... | collective-permute-start | bytes 1228808 | tf_op jit(solution)/shard_map/ppermute | solution.py:359
  127.2 53.2 %collective-permute-start.21 = (bf16[320,640]{1,0:T(8,128)(2,1)}, bf16[320,640]{1,0:T(8,128)(2,1)}, u32[]{:S(2)}, u32[]{:S(2)}) collective-permute-start(bf16[320,640]{1,0:T(8,128)(2,1)} %collective-permute-done.20.refs_3_), channel_id=1, source_target_pairs={{0,16},{16,0},{1,17},{17,1},{2,18},{18,2},{3,19},{19,3},{4,20},{20... | collective-permute-start | bytes 1228808 | tf_op jit(solution)/shard_map/ppermute | solution.py:360
  129.0 60.0 %collective-permute-start.27 = (bf16[320,640]{1,0:T(8,128)(2,1)S(1)}, bf16[320,640]{1,0:T(8,128)(2,1)S(1)}, u32[]{:S(2)}, u32[]{:S(2)}) collective-permute-start(bf16[320,640]{1,0:T(8,128)(2,1)S(1)} %collective-permute-done.26.refs_0_), channel_id=1, source_target_pairs={{0,16},{16,0},{1,17},{17,1},{2,18},{18,2},{3,19},{19,3},{4,20},{20... | collective-permute-start | bytes 1228808 | tf_op jit(solution)/shard_map/ppermute | solution.py:360
  157.3 31.0 %slice-start = ((s8[4587520]{0:T(1024)(128)(4,1)}), s8[4194304]{0:T(1024)(128)(4,1)S(1)}, s32[]{:S(2)}) async-start(s8[4587520]{0:T(1024)(128)(4,1)} %bitcast.52), calls=%async_computation.1 | async-start | bytes 8388608
  184.8 22.7 %collective-permute-start.22 = (bf16[448,640]{1,0:T(8,128)(2,1)S(1)}, bf16[448,640]{1,0:T(8,128)(2,1)S(1)}, u32[]{:S(2)}, u32[]{:S(2)}) collective-permute-start(bf16[448,640]{1,0:T(8,128)(2,1)S(1)} %get-tuple-element.48), channel_id=1, source_target_pairs={{0,1},{1,0},{2,3},{3,2},{4,5},{5,4},{6,7},{7,6},{8,9},{9,8},{10,11... | collective-permute-start | bytes 1720328 | tf_op jit(solution)/shard_map/ppermute | solution.py:415
  184.9 24.1 %collective-permute-start.24 = (bf16[448,640]{1,0:T(8,128)(2,1)S(1)}, bf16[448,640]{1,0:T(8,128)(2,1)S(1)}, u32[]{:S(2)}, u32[]{:S(2)}) collective-permute-start(bf16[448,640]{1,0:T(8,128)(2,1)S(1)} %get-tuple-element.50), channel_id=1, source_target_pairs={{0,1},{1,0},{2,3},{3,2},{4,5},{5,4},{6,7},{7,6},{8,9},{9,8},{10,11... | collective-permute-start | bytes 1720328 | tf_op jit(solution)/shard_map/ppermute | solution.py:415
  189.8 4.8 %collective-permute-start.33 = (f32[4,3,640]{2,1,0:T(4,128)S(1)}, f32[4,3,640]{2,1,0:T(4,128)S(1)}, u32[]{:S(2)}, u32[]{:S(2)}) collective-permute-start(f32[4,3,640]{2,1,0:T(4,128)S(1)} %pad_maximum_fusion.4), channel_id=1, source_target_pairs={{0,1},{1,0},{2,3},{3,2},{4,5},{5,4},{6,7},{7,6},{8,9},{9,8},{10,11... | collective-permute-start | bytes 92168 | tf_op jit(solution)/shard_map/ppermute | solution.py:415
  194.6 4.1 %collective-permute-start.34 = (f32[4,3,640]{2,1,0:T(4,128)S(1)}, f32[4,3,640]{2,1,0:T(4,128)S(1)}, u32[]{:S(2)}, u32[]{:S(2)}) collective-permute-start(f32[4,3,640]{2,1,0:T(4,128)S(1)} %fusion.36), channel_id=1, source_target_pairs={{0,2},{1,3},{2,0},{3,1},{4,6},{5,7},{6,4},{7,5},{8,10},{9,11},{10,... | collective-permute-start | bytes 92168 | tf_op jit(solution)/shard_map/ppermute | solution.py:482
  198.7 4.9 %collective-permute-start.37 = (bf16[3,2688]{1,0:T(4,128)(2,1)S(1)}, bf16[3,2688]{1,0:T(4,128)(2,1)S(1)}, u32[]{:S(2)}, u32[]{:S(2)}) collective-permute-start(bf16[3,2688]{1,0:T(4,128)(2,1)S(1)} %pad_maximum_fusion.5), channel_id=1, source_target_pairs={{0,12},{4,0},{8,4},{12,8},{1,13},{5,1},{9,5},{13,9},{2,14},{6,2},{... | collective-permute-start | bytes 48392 | tf_op jit(solution)/shard_map/ppermute | solution.py:489
  201.1 4.7 %collective-permute-start.36 = (bf16[3,2688]{1,0:T(4,128)(2,1)S(1)}, bf16[3,2688]{1,0:T(4,128)(2,1)S(1)}, u32[]{:S(2)}, u32[]{:S(2)}) collective-permute-start(bf16[3,2688]{1,0:T(4,128)(2,1)S(1)} %pad_maximum_fusion.5), channel_id=1, source_target_pairs={{0,8},{4,12},{8,0},{12,4},{1,9},{5,13},{9,1},{13,5},{2,10},{6,14},... | collective-permute-start | bytes 48392 | tf_op jit(solution)/shard_map/ppermute | solution.py:489
  201.1 5.6 %collective-permute-start.35 = (bf16[3,2688]{1,0:T(4,128)(2,1)S(1)}, bf16[3,2688]{1,0:T(4,128)(2,1)S(1)}, u32[]{:S(2)}, u32[]{:S(2)}) collective-permute-start(bf16[3,2688]{1,0:T(4,128)(2,1)S(1)} %pad_maximum_fusion.5), channel_id=1, source_target_pairs={{0,4},{4,8},{8,12},{12,0},{1,5},{5,9},{9,13},{13,1},{2,6},{6,10},{... | collective-permute-start | bytes 48392 | tf_op jit(solution)/shard_map/ppermute | solution.py:489
  203.6 10.1 %collective-permute-start.28 = (bf16[448,640]{1,0:T(8,128)(2,1)S(1)}, bf16[448,640]{1,0:T(8,128)(2,1)S(1)}, u32[]{:S(2)}, u32[]{:S(2)}) collective-permute-start(bf16[448,640]{1,0:T(8,128)(2,1)S(1)} %out_project.7), channel_id=1, source_target_pairs={{0,1},{1,0},{2,3},{3,2},{4,5},{5,4},{6,7},{7,6},{8,9},{9,8},{10,11... | collective-permute-start | bytes 1720328 | tf_op jit(solution)/shard_map/ppermute | solution.py:415
  205.8 9.3 %collective-permute-start.30 = (bf16[448,640]{1,0:T(8,128)(2,1)S(1)}, bf16[448,640]{1,0:T(8,128)(2,1)S(1)}, u32[]{:S(2)}, u32[]{:S(2)}) collective-permute-start(bf16[448,640]{1,0:T(8,128)(2,1)S(1)} %get-tuple-element.54), channel_id=1, source_target_pairs={{0,1},{1,0},{2,3},{3,2},{4,5},{5,4},{6,7},{7,6},{8,9},{9,8},{10,11... | collective-permute-start | bytes 1720328 | tf_op jit(solution)/shard_map/ppermute | solution.py:415
  207.6 17.8 %collective-permute-start.23 = (bf16[448,640]{1,0:T(8,128)(2,1)S(1)}, bf16[448,640]{1,0:T(8,128)(2,1)S(1)}, u32[]{:S(2)}, u32[]{:S(2)}) collective-permute-start(bf16[448,640]{1,0:T(8,128)(2,1)S(1)} %fusion.11), channel_id=1, source_target_pairs={{2,0},{3,1},{6,4},{7,5},{8,10},{9,11},{12,14},{13,15},{18,16},{19,... | collective-permute-start | bytes 1720328 | tf_op jit(solution)/shard_map/ppermute | solution.py:433
  209.1 18.0 %collective-permute-start.25 = (bf16[448,640]{1,0:T(8,128)(2,1)S(1)}, bf16[448,640]{1,0:T(8,128)(2,1)S(1)}, u32[]{:S(2)}, u32[]{:S(2)}) collective-permute-start(bf16[448,640]{1,0:T(8,128)(2,1)S(1)} %fusion.12), channel_id=1, source_target_pairs={{0,2},{1,3},{6,4},{7,5},{10,8},{11,9},{12,14},{13,15},{16,18},{17,... | collective-permute-start | bytes 1720328 | tf_op jit(solution)/shard_map/ppermute | solution.py:433
  213.8 23.8 %collective-permute-start.29 = (bf16[448,640]{1,0:T(8,128)(2,1)S(1)}, bf16[448,640]{1,0:T(8,128)(2,1)S(1)}, u32[]{:S(2)}, u32[]{:S(2)}) collective-permute-start(bf16[448,640]{1,0:T(8,128)(2,1)S(1)} %fusion.13), channel_id=1, source_target_pairs={{0,2},{1,3},{4,6},{5,7},{10,8},{11,9},{14,12},{15,13},{16,18},{17,... | collective-permute-start | bytes 1720328 | tf_op jit(solution)/shard_map/ppermute | solution.py:433
  215.3 22.4 %collective-permute-start.31 = (bf16[448,640]{1,0:T(8,128)(2,1)S(1)}, bf16[448,640]{1,0:T(8,128)(2,1)S(1)}, u32[]{:S(2)}, u32[]{:S(2)}) collective-permute-start(bf16[448,640]{1,0:T(8,128)(2,1)S(1)} %fusion.14), channel_id=1, source_target_pairs={{2,0},{3,1},{4,6},{5,7},{8,10},{9,11},{14,12},{15,13},{18,16},{19,... | collective-permute-start | bytes 1720328 | tf_op jit(solution)/shard_map/ppermute | solution.py:433
  238.7 2.0 collective-permute-start.32
  (32 other events, 266.1 us)
Sparse Core Ops, SparseCore 0:
  9.7 39.3 all-gather.2

commit v2 on v0

--- a/solution.py
+++ b/solution.py
@@ -1,6 +1,10 @@
+import functools
+
 import jax
 import jax.numpy as jnp
 from jax import lax
+from jax.experimental import pallas as pl
+from jax.experimental.pallas import tpu as pltpu
 from jax.sharding import PartitionSpec as P
 
 HS = 128
@@ -59,7 +63,7 @@
     return target - jax.nn.logsumexp(logits, -1)
 
 
-def per_device(
+def per_device_any(
     hidden, lengths, mask_pos, token_ids, assignment, w_query, w_key, w_value, w_out, embed
 ):
     tokens_here = hidden.shape[0]
@@ -116,10 +120,410 @@
     scored = target_score(logits, mine_ids)
     return (states, logits, scored)
 
+F32 = jnp.float32
+BF16 = jnp.bfloat16
+VMEM_LIMIT = 60 * 1024 * 1024
+SMEM_SPEC = pl.BlockSpec(memory_space=pltpu.SMEM)
+HBM_SPEC = pl.BlockSpec(memory_space=pltpu.HBM)
+
+
+def params(*semantics):
+    return pltpu.CompilerParams(
+        vmem_limit_bytes=VMEM_LIMIT, dimension_semantics=semantics or None
+    )
+
+
+def norm_kernel(x_ref, out_ref):
+    blocks, _, width = x_ref.shape
+    count = blocks * width
+    values = [x_ref[b].astype(F32) for b in range(blocks)]
+    average = sum(jnp.sum(v, -1, keepdims=True) for v in values) / count
+    centred = [v - average for v in values]
+    spread = sum(jnp.sum(v * v, -1, keepdims=True) for v in centred) / count
+    scale = lax.rsqrt(spread + EPSILON)
+    for b in range(blocks):
+        out_ref[:, b * width : (b + 1) * width] = (centred[b] * scale).astype(BF16)
+
+
+def norm_blocks(stack, row_block=224):
+    blocks, rows, width = stack.shape
+    return pl.pallas_call(
+        norm_kernel,
+        grid=(rows // row_block,),
+        in_specs=[pl.BlockSpec((blocks, row_block, width), lambda i: (0, i, 0))],
+        out_specs=pl.BlockSpec((row_block, blocks * width), lambda i: (i, 0)),
+        out_shape=jax.ShapeDtypeStruct((rows, blocks * width), BF16),
+        compiler_params=params("arbitrary"),
+        cost_estimate=pl.CostEstimate(
+            flops=8 * stack.size, bytes_accessed=4 * stack.size, transcendentals=rows
+        ),
+        name="norm_rows",
+    )(stack)
+
+
+def shard_parts(part, shard, half):
+    if len(shard) == 2:
+        mine, other = shard
+        return [
+            (mine, pl.multiple_of(part * half, half)),
+            (other, pl.multiple_of((1 - part) * half, half)),
+        ]
+    return [(shard[0].at[pl.ds(j * half, half)], j * half) for j in range(2)]
+
+
+def take_shards(refs, lengths):
+    return [tuple(refs.pop(0) for _ in range(n)) for n in lengths]
+
+
+def project_kernel(scale, rotated, lengths, place_ref, x_ref, *refs):
+    refs = list(refs)
+    shards = take_shards(refs, lengths)
+    if rotated:
+        cos, sin = refs.pop(0)[...], refs.pop(0)[...]
+    out_ref, wbuf, sems = refs
+    depth, width = shards[0][0].shape
+    half = depth // 2
+
+    @pl.when(pl.program_id(0) == 0)
+    def _():
+        copies = []
+        for k, shard in enumerate(shards):
+            for j, (source, row) in enumerate(shard_parts(place_ref[0], shard, half)):
+                row = pl.multiple_of(place_ref[1 + k] * depth + row, half)
+                copies.append(
+                    pltpu.make_async_copy(source, wbuf.at[pl.ds(row, half)], sems.at[k, j])
+                )
+        for copy in copies:
+            copy.start()
+        for copy in copies:
+            copy.wait()
+
+    total = jnp.dot(x_ref[...], wbuf[...], preferred_element_type=F32)
+    if not rotated:
+        out_ref[...] = total.astype(BF16)
+        return
+    if scale is not None:
+        total = total * scale
+    for h in range(width // HS):
+        field = total[:, h * HS : (h + 1) * HS]
+        turned = pltpu.roll(field, HS // 2, 1)
+        out_ref[:, h * HS : (h + 1) * HS] = (field * cos + turned * sin).astype(BF16)
+
+
+def project(place, normed, shards, scale=None, turn=(), row_block=448):
+    rows, features = normed.shape
+    width = shards[0][0].shape[1]
+    flat = [ref for shard in shards for ref in shard]
+    in_specs = [SMEM_SPEC, pl.BlockSpec((row_block, features), lambda i: (i, 0))]
+    in_specs += [HBM_SPEC] * len(flat)
+    in_specs += [pl.BlockSpec((row_block, HS), lambda i: (i, 0)) for _ in turn]
+    return pl.pallas_call(
+        functools.partial(
+            project_kernel, scale, bool(turn), [len(shard) for shard in shards]
+        ),
+        grid=(rows // row_block,),
+        in_specs=in_specs,
+        out_specs=pl.BlockSpec((row_block, width), lambda i: (i, 0)),
+        out_shape=jax.ShapeDtypeStruct((rows, width), BF16),
+        scratch_shapes=[
+            pltpu.VMEM((features, width), BF16),
+            pltpu.SemaphoreType.DMA((4, 2)),
+        ],
+        compiler_params=params("arbitrary"),
+        cost_estimate=pl.CostEstimate(
+            flops=2 * rows * features * width,
+            bytes_accessed=2 * (normed.size + (features + rows) * width),
+            transcendentals=0,
+        ),
+        name="project",
+    )(place, normed, *flat, *turn)
+
+
+def attend_kernel(place_ref, ends_ref, q_ref, k_ref, v_ref, out_ref, *, row_block):
+    count = k_ref.shape[0]
+    keys, values = k_ref[...], v_ref[...]
+    base = place_ref[1] * q_ref.shape[0]
+    col = lax.broadcasted_iota(jnp.int32, (1, count), 1)
+    sequences = ends_ref.shape[0]
+    col_label = sum((col >= ends_ref[j]).astype(jnp.int32) for j in range(sequences - 1))
+    for r in range(q_ref.shape[0] // row_block):
+        span = slice(r * row_block, (r + 1) * row_block)
+        row = lax.broadcasted_iota(jnp.int32, (row_block, 1), 0) + (base + r * row_block)
+        row_label = sum((row >= ends_ref[j]).astype(jnp.int32) for j in range(sequences - 1))
+        scores = lax.dot_general(
+            q_ref[span, :], keys, (((1,), (1,)), ((), ())), preferred_element_type=F32
+        )
+        scores = jnp.where(row_label == col_label, scores, -1e30)
+        top = jnp.max(scores, -1, keepdims=True)
+        raised = jnp.exp(scores - top)
+        weights = raised * (1.0 / jnp.sum(raised, -1, keepdims=True))
+        out_ref[span, :] = jnp.dot(
+            weights.astype(BF16), values, preferred_element_type=F32
+        ).astype(BF16)
+
+
+def attention(place, ends, queries, key_rows, value_rows, row_block=224):
+    rows, columns = queries.shape
+    half = rows // 2
+    heads = columns // HS
+    return pl.pallas_call(
+        functools.partial(attend_kernel, row_block=row_block),
+        grid_spec=pltpu.PrefetchScalarGridSpec(
+            num_scalar_prefetch=2,
+            grid=(heads,),
+            in_specs=[
+                pl.BlockSpec((half, HS), lambda h, place, ends: (place[1], h)),
+                pl.BlockSpec((rows, HS), lambda h, place, ends: (0, h)),
+                pl.BlockSpec((rows, HS), lambda h, place, ends: (0, h)),
+            ],
+            out_specs=pl.BlockSpec((half, HS), lambda h, place, ends: (0, h)),
+        ),
+        out_shape=jax.ShapeDtypeStruct((half, columns), BF16),
+        compiler_params=params("arbitrary"),
+        cost_estimate=pl.CostEstimate(
+            flops=4 * half * rows * columns,
+            bytes_accessed=6 * rows * columns,
+            transcendentals=half * rows * heads,
+        ),
+        name="attention",
+    )(place, ends, queries, key_rows, value_rows)
+
+
+def out_kernel(adding, lengths, place_ref, *refs):
+    refs = list(refs)
+    if adding:
+        x_ref, come_ref = refs.pop(0), refs.pop(0)
+    else:
+        picked_ref, x_ref, kept_ref = refs.pop(0), refs.pop(0), refs.pop(0)
+    shards = take_shards(refs, lengths)
+    out_ref = refs.pop(0)
+    if not adding:
+        rows_ref, marked = refs.pop(0), refs.pop()
+    wbuf, sems = refs
+    block = pl.program_id(0)
+    half = wbuf.shape[1] // 2
+    part, core, column = place_ref[0], place_ref[5], place_ref[6]
+
+    @pl.when(block == 0)
+    def _():
+        for k, shard in enumerate(shards):
+            spot = place_ref[1 + k]
+            for j, (source, row) in enumerate(shard_parts(part, shard, half)):
+                pltpu.make_async_copy(
+                    source, wbuf.at[spot, pl.ds(row, half)], sems.at[spot, j]
+                ).start()
+        if not adding:
+            size = x_ref.shape[0]
+            slot = lax.broadcasted_iota(jnp.int32, (marked.shape[0], size), 0)
+            row = lax.broadcasted_iota(jnp.int32, (marked.shape[0], size), 1)
+            total = None
+            for ref, base in ((x_ref, (1 - core) * size), (kept_ref, core * size)):
+                hit = sum(
+                    ((slot == j) & (row + base == picked_ref[j])).astype(F32)
+                    for j in range(picked_ref.shape[0])
+                )
+                term = jnp.dot(hit.astype(BF16), ref[...], preferred_element_type=F32)
+                total = term if total is None else total + term
+            marked[...] = total.astype(BF16)
+
+    for j in range(2):
+        pltpu.make_async_copy(
+            shards[0][0].at[pl.ds(0, half)],
+            wbuf.at[block, pl.ds(j * half, half)],
+            sems.at[block, j],
+        ).wait()
+    total = jnp.dot(x_ref[...], wbuf[block], preferred_element_type=F32)
+    if adding:
+        total = total + come_ref[...].astype(F32)
+    else:
+        rows_ref[block ^ column] = jnp.dot(
+            marked[...], wbuf[block], preferred_element_type=F32
+        )
+    out_ref[...] = total.astype(BF16)
+
+
+def out_project(place, context, shards, come=None, picked=None, kept=None):
+    half, depth = context.shape
+    width = shards[0][0].shape[1]
+    flat = [ref for shard in shards for ref in shard]
+    adding = come is not None
+    whole = pl.BlockSpec((half, depth), lambda j: (0, 0))
+    if adding:
+        operands = [place, context, come]
+        in_specs = [SMEM_SPEC, whole]
+        in_specs += [pl.BlockSpec((None, half, width), lambda j: (j ^ 1, 0, 0))]
+    else:
+        operands = [place, picked, context, kept]
+        in_specs = [SMEM_SPEC, SMEM_SPEC, whole, whole]
+    out_specs = [pl.BlockSpec((None, half, width), lambda j: (j, 0, 0))]
+    out_shape = [jax.ShapeDtypeStruct((4, half, width), BF16)]
+    scratch = [pltpu.VMEM((4, depth, width), BF16), pltpu.SemaphoreType.DMA((4, 2))]
+    if not adding:
+        out_specs.append(pl.BlockSpec((4, 8, width), lambda j: (0, 0, 0)))
+        out_shape.append(jax.ShapeDtypeStruct((4, 8, width), F32))
+        scratch.append(pltpu.VMEM((8, depth), BF16))
+    return pl.pallas_call(
+        functools.partial(out_kernel, adding, [len(shard) for shard in shards]),
+        grid=(4,),
+        in_specs=in_specs + [HBM_SPEC] * len(flat),
+        out_specs=out_specs,
+        out_shape=out_shape,
+        scratch_shapes=scratch,
+        compiler_params=params("arbitrary"),
+        cost_estimate=pl.CostEstimate(
+            flops=8 * half * depth * width,
+            bytes_accessed=2 * (half * depth + 4 * (depth + (1 + adding) * half) * width),
+            transcendentals=0,
+        ),
+        name="out_project",
+    )(*operands, *flat)
+
+
+def tie(value, *earlier):
+    return lax.optimization_barrier((value, *earlier))[0]
+
+
+class WeightRing:
+    def __init__(self, dp):
+        self.dp = dp
+        self.part = lax.axis_index("parts")
+        self.along, self.across, self.shards = [], [], []
+
+    def ring(self, value, step):
+        return lax.ppermute(value, "dp", [(i, (i + step) % self.dp) for i in range(self.dp)])
+
+    def step(self, value, step, before=(), before_swap=(), gather=False):
+        i = len(self.along)
+        waits = list(before) + self.along[i - 2 : i - 1] if i >= 2 else list(before)
+        self.along.append(self.ring(tie(value, *waits), step))
+        if gather:
+            whole = lax.all_gather(self.along[i], "parts", axis=0, tiled=True)
+            self.shards.append((whole,))
+            return
+        waits = self.across[-2:-1]
+        self.across.append(
+            lax.ppermute(tie(self.along[i], *waits, *before_swap), "parts", [(0, 1), (1, 0)])
+        )
+        self.shards.append((self.along[i], self.across[-1]))
+
+    def half(self, weight):
+        size = weight.shape[0] // 2
+        return lax.dynamic_slice_in_dim(weight, self.part * size, size, 0)
+
+    def pieces(self, group):
+        first = 3 * group
+        return [self.shards[i] for i in (first, first + 2, first + 1)]
+
+
+def per_device(
+    hidden, lengths, mask_pos, token_ids, assignment, w_query, w_key, w_value, w_out, embed
+):
+    dp, fsdp = 4, 4
+    rows, width = hidden.shape
+    half = rows // 2
+    sequences = lengths.shape[0]
+    part = lax.axis_index("parts")
+    group = lax.axis_index("dp")
+    column = lax.axis_index("fsdp")
+    core = column % 2
+    ring_order = [lax.rem(group + dp - k, dp) for k in range(dp)]
+    place = jnp.stack([part] + ring_order).astype(jnp.int32)
+    stack = lax.all_gather(hidden, "fsdp", axis=0, tiled=False)
+    segment, position, starts = layout(lengths, rows)
+    half_width = HS // 2
+    frequency = 10000.0 ** (-2.0 * jnp.arange(half_width, dtype=F32) / HS)
+    angles = position.astype(F32)[:, None] * frequency[None, :]
+    sine, cosine = jnp.sin(angles), jnp.cos(angles)
+    turn = (jnp.concatenate([cosine, cosine], -1), jnp.concatenate([-sine, sine], -1))
+    picked = starts + mask_pos
+    chosen = jnp.arange(rows, dtype=jnp.int32)[None, :] == picked[:, None]
+    local_ids = jnp.sum(jnp.where(chosen, token_ids[None, :], 0), 1)
+
+    ends = jnp.cumsum(lengths)
+    keep_place = jnp.stack([part, core]).astype(jnp.int32)
+    send_place = jnp.stack([part, 1 - core]).astype(jnp.int32)
+    out_place = jnp.stack([part] + [s ^ column for s in ring_order] + [core, column]).astype(jnp.int32)
+
+    def swap_by(value, mask):
+        return lax.ppermute(value, "fsdp", [(i, i ^ mask) for i in range(fsdp)])
+
+    one_hot = chosen.astype(BF16)
+    hidden_rows = jnp.einsum("sr,brw->bsw", one_hot, stack, preferred_element_type=F32)
+    hidden_rows = jnp.pad(hidden_rows, ((0, 0), (0, 8 - sequences), (0, 0)))
+    extra = jnp.stack([local_ids, assignment], 1).astype(BF16)
+    extra = jnp.pad(extra, ((0, 8 - sequences), (0, width - 2)))[None]
+
+    ring = WeightRing(dp)
+    mine = ring.half(w_key)
+    ring.step(mine, 1)
+    ring.step(mine, -1)
+    ring.step(ring.along[0], 1)
+    mine = ring.half(w_query)
+    ring.step(mine, 1)
+    ring.step(mine, -1)
+    normed = norm_blocks(stack)
+    ring.step(ring.along[3], 1, before=[normed])
+    key_rows = project(place, normed, [(w_key,), *ring.pieces(0)], None, turn)
+    mine = ring.half(w_value)
+    ring.step(mine, 1, before=[key_rows])
+    ring.step(mine, -1)
+    ring.step(ring.along[6], 1)
+    queries = project(place, normed, [(w_query,), *ring.pieces(1)], HS ** (-0.5), turn)
+    mine = ring.half(w_out)
+    ring.step(mine, 1, before=[queries])
+    value_rows = project(place, normed, [(w_value,), *ring.pieces(2)])
+    ring.step(mine, -1, before_swap=[value_rows])
+    context_sent = attention(send_place, ends, queries, key_rows, value_rows)
+    last_along = ring.ring(tie(ring.along[9], ring.along[9]), 1)
+    last_other = ring.ring(tie(ring.across[-2], ring.along[10], context_sent), 1)
+    out_in = [(w_out,), ring.shards[9], (last_along, last_other), ring.shards[10]]
+    context_kept = attention(keep_place, ends, queries, key_rows, tie(value_rows, context_sent))
+
+    sent, row_sum = out_project(out_place, context_sent, out_in, None, picked, context_kept)
+    arrived = swap_by(sent, 1)
+
+    row_sum = row_sum + sum(swap_by(row_sum, mask) for mask in range(1, fsdp))
+    full_rows = (hidden_rows + row_sum).astype(BF16)
+    packet = jnp.concatenate([full_rows, extra], 0)
+
+    (chip,) = out_project(out_place, tie(context_kept, packet), out_in, arrived)
+    crossed = swap_by(chip[2:], 2)
+
+    packets = [packet] + [ring.ring(packet, shift) for shift in range(1, dp)]
+    packets = jnp.stack(packets)[:, :, :sequences]
+    all_rows = packets[:, :dp].transpose(0, 2, 1, 3).reshape(dp * sequences, dp * width)
+    all_ids = packets[:, dp, :, 0].reshape(-1).astype(jnp.int32)
+    all_owner = packets[:, dp, :, 1].reshape(-1).astype(jnp.int32)
+    owned = group * sequences + jnp.arange(sequences, dtype=jnp.int32)
+    match = all_owner[None, :] == owned[:, None]
+    mine_rows = jnp.dot(match.astype(BF16), all_rows, preferred_element_type=F32)
+    mine_ids = jnp.sum(jnp.where(match, all_ids[None, :], 0), 1).astype(jnp.int32)
+    normed_rows = norm_rows(mine_rows).astype(BF16)
+    logits = jnp.dot(normed_rows, embed.T, preferred_element_type=F32)
+    scored = target_score(logits, mine_ids)
+
+    def block_rows(index, place_in_chip):
+        before = lax.dynamic_slice(stack, (index, core * half, 0), (1, half, width))[0]
+        summed = chip[place_in_chip].astype(F32) + crossed[place_in_chip].astype(F32)
+        return (before.astype(F32) + summed).astype(BF16)
+
+    other_rows = swap_by(block_rows(column ^ 1, 1), 1)
+    own_rows = block_rows(column, 0)
+    states = jnp.where(
+        core == 0,
+        jnp.concatenate([own_rows, other_rows], 0),
+        jnp.concatenate([other_rows, own_rows], 0),
+    )
+    return (states, logits, scored)
+
+
+def ring_fits(mesh):
+    return (mesh.shape["parts"], mesh.shape["dp"], mesh.shape["fsdp"]) == (2, 4, 4)
+
 
 def solution(mesh):
     return jax.shard_map(
-        per_device,
+        per_device if ring_fits(mesh) else per_device_any,
         mesh=mesh,
         in_specs=(
             P(("parts", "dp"), "fsdp"),

time: 407 us -> 225 us (0.55)
  waiting for transfers between devices: 257 us -> 72.4 us
  Pallas kernels: 0 us -> 63.9 us
  starting transfers between devices: 0.23 us -> 49.4 us
  matrix products: 52.1 us -> 3.69 us
  blocking collectives: 25.4 us -> 0 us
  other arithmetic: 31.9 us -> 10.2 us
  local copies, waits for them, and re-layouts: 24.3 us -> 10.3 us
    all_gather x5 -> x1, waiting for transfers between devices: 218 us -> 0.01 us  [per_device(): stack = lax.all_gather(hidden, 'fsdp', axis=0, tiled=False)]
    ppermute x0 -> x33, waiting for transfers between devices: none -> 71.8 us  [the longest x16 44.9 us: ring(): lax.ppermute(value, 'dp', [(i, (i + step) % self.dp) for i in range(self....]
    pallas_call x0 -> x8, Pallas kernels: none -> 63.9 us  [the longest x3 26.5 us: project(): pl.pallas_call(functools.partial(project_kernel, scale, bool(turn), [len(...]
    ppermute x0 -> x33, starting transfers between devices: none -> 49.4 us  [the longest x16 33.7 us: ring(): lax.ppermute(value, 'dp', [(i, (i + step) % self.dp) for i in range(self....]
    dot_general x17 -> x3, matrix products: 52.1 us -> 3.69 us  [the longest x1 3.03 us: per_device(): jnp.einsum('sr,brw->bsw', one_hot, stack, preferred_element_type=F32)]
    unnamed x7 -> x1, waiting for transfers between devices: 39.3 us -> 0.68 us
    all_gather x2 -> x0, blocking collectives: 18.4 us -> none  [the longest x1 13.2 us: per_device(): lax.all_gather(row_full, 'dp', axis=0, tiled=True)]
    reshape x3 -> x0, local copies, waits for them, and re-layouts: 8.07 us -> none  [the longest x1 3.2 us: per_device(): (query_sum * HS ** (-0.5)).reshape(tokens_here, heads_here, HS)]
  transfers between devices with their start and end apart: 6 -> 34, of which waited for: 6 -> 11; matrix products, arithmetic and copies ran while one was open for 21% -> 7% of each run, Pallas kernels for 0% -> 26%
where the time goes in v2:
time: 225 us; the launch traced here: 224 us
  waiting for transfers between devices  72.4 us (32%)
  Pallas kernels  63.9 us (28%)
  starting transfers between devices  49.4 us (22%)
  between operations  14.5 us (6%)
  local copies, waits for them, and re-layouts  10.3 us (5%)
  other arithmetic  10.2 us (5%)
  matrix products  3.69 us (2%)
    ppermute x16, waiting for transfers between devices, ring(): lax.ppermute(value, 'dp', [(i, (i + step) % self.dp) for i in range(self....  44.9 us
    ppermute x16, starting transfers between devices, ring(): lax.ppermute(value, 'dp', [(i, (i + step) % self.dp) for i in range(self....  33.7 us
    ppermute x6, waiting for transfers between devices, swap_by(): return lax.ppermute(value, 'fsdp', [(i, i ^ mask) for i in range(fsdp)])  26.8 us
    pallas_call x3, Pallas kernels, project(): pl.pallas_call(functools.partial(project_kernel, scale, bool(turn), [len(...  26.5 us
    pallas_call x2, Pallas kernels, attention(): pl.pallas_call(functools.partial(attend_kernel, row_block=row_block), gri...  17.7 us
    pallas_call x2, Pallas kernels, out_project(): pl.pallas_call(functools.partial(out_kernel, adding, [len(shard) for shar...  13.4 us
    ppermute x11, starting transfers between devices, step(): lax.ppermute(tie(self.along[i], *waits, *before_swap), 'parts', [(0, 1),...  12.2 us
    pallas_call x1, Pallas kernels, norm_blocks(): pl.pallas_call(norm_kernel, grid=(rows // row_block,), in_specs=[pl.Block...  6.28 us
  transfers between devices with their start and end apart: 34, of which 11 were waited for; matrix products, arithmetic and copies ran while one was open for 7% of the time, Pallas kernels for 26%

profile of v2, /device:TPU:0, one launch (start us, length us, event | category | flops | bytes accessed | tf_op | source)
XLA Modules:
  0.0 224.4 jit_solution(1362265976966521740)
XLA Ops:
  8.4 3.1 %collective-permute-start.6 = (bf16[320,640]{1,0:T(8,128)(2,1)S(1)}, bf16[320,640]{1,0:T(8,128)(2,1)S(1)}, u32[]{:S(2)}, u32[]{:S(2)}) collective-permute-start(bf16[320,640]{1,0:T(8,128)(2,1)S(1)} %constant_dynamic-slice_fusion.2), channel_id=1, source_target_pairs={{0,4},{4,8},{8,12},{12,0},{1,5},{5,9},{9,13},{13,1},{2,6},{6,10},{... | collective-permute-start | bytes 1228808 | tf_op jit(solution)/shard_map/ppermute | solution.py:393
  11.5 2.1 collective-permute-start
  14.4 9.4 %collective-permute-done.6.refs_1_ = bf16[320,640]{1,0:T(8,128)(2,1)S(1)} collective-permute-done((bf16[320,640]{1,0:T(8,128)(2,1)S(1)}, bf16[320,640]{1,0:T(8,128)(2,1)S(1)}, u32[]{:S(2)}, u32[]{:S(2)}) %collective-permute-start.6) | collective-permute-done | bytes 409632 | tf_op jit(solution)/shard_map/ppermute | solution.py:393
  23.9 1.8 collective-permute-start.9
  25.7 5.7 %collective-permute-done.refs_5_ = bf16[320,640]{1,0:T(8,128)(2,1)S(1)} collective-permute-done((bf16[320,640]{1,0:T(8,128)(2,1)S(1)}, bf16[320,640]{1,0:T(8,128)(2,1)S(1)}, u32[]{:S(2)}, u32[]{:S(2)}) %collective-permute-start) | collective-permute-done | bytes 409632 | tf_op jit(solution)/shard_map/ppermute | solution.py:393
  31.4 2.2 %collective-permute-start.1 = (bf16[320,640]{1,0:T(8,128)(2,1)S(1)}, bf16[320,640]{1,0:T(8,128)(2,1)S(1)}, u32[]{:S(2)}, u32[]{:S(2)}) collective-permute-start(bf16[320,640]{1,0:T(8,128)(2,1)S(1)} %constant_dynamic-slice_fusion.3), channel_id=1, source_target_pairs={{0,4},{4,8},{8,12},{12,0},{1,5},{5,9},{9,13},{13,1},{2,6},{6,10},{... | collective-permute-start | bytes 1228808 | tf_op jit(solution)/shard_map/ppermute | solution.py:393
  33.7 1.2 collective-permute-start.2
  34.9 8.3 %collective-permute-done.7.refs_3_ = bf16[320,640]{1,0:T(8,128)(2,1)} collective-permute-done((bf16[320,640]{1,0:T(8,128)(2,1)S(1)}, bf16[320,640]{1,0:T(8,128)(2,1)}, u32[]{:S(2)}, u32[]{:S(2)}) %collective-permute-start.7) | collective-permute-done | bytes 409632 | tf_op jit(solution)/shard_map/ppermute | solution.py:393
  43.2 1.9 collective-permute-start.8
  45.8 1.5 collective-permute-start.10
  47.3 1.7 fusion.2
  49.0 1.2 pad_maximum_fusion
  50.3 1.5 collective-permute-done.1.refs_1_
  51.7 0.8 copy-done.27
  52.5 1.5 collective-permute-start.3
  54.1 6.3 %norm_rows.1.x_ref = bf16[896,2560]{1,0:T(8,128)(2,1)} custom-call(bf16[4,896,640]{2,1,0:T(8,128)(2,1)} %bitcast.46), custom_call_target="tpu_custom_call" | custom-call | flops 18350080 | bytes 9175040 | tf_op jit(solution)/shard_map/norm_rows/pallas_call | solution.py:150
  60.3 1.0 collective-permute-start.4
  62.7 9.0 %project.4.k_ref = bf16[896,640]{1,0:T(8,128)(2,1)} custom-call(s32[5]{0:T(128)} %stack.92.place_ref, bf16[896,2560]{1,0:T(8,128)(2,1)} %norm_rows.1.x_ref, bf16[640,640]{1,0:T(8,128)(2,1)} %refs_0_.4, bf16[320,640]{1,0:T(8,128)(2,1)} %copy-done.22, bf16[320,640]{1,0:T(8,128)(2,1)} %copy-done.24, bf16[320,640]{1,0:T(8,128)(2,1)} %collective-permute-done.7.refs_3_, ...), custom_call_target="tpu_custom_call" | custom-call | flops 2936012800 | bytes 9011200 | tf_op jit(solution)/shard_map/project/pallas_call | solution.py:220
  72.2 3.7 %collective-permute-done.4.refs_3_ = bf16[320,640]{1,0:T(8,128)(2,1)S(1)} collective-permute-done((bf16[320,640]{1,0:T(8,128)(2,1)S(1)}, bf16[320,640]{1,0:T(8,128)(2,1)S(1)}, u32[]{:S(2)}, u32[]{:S(2)}) %collective-permute-start.4) | collective-permute-done | bytes 409632 | tf_op jit(solution)/shard_map/ppermute | solution.py:393
  76.5 6.0 %collective-permute-start.16 = (bf16[320,640]{1,0:T(8,128)(2,1)S(1)}, bf16[320,640]{1,0:T(8,128)(2,1)S(1)}, u32[]{:S(2)}, u32[]{:S(2)}) collective-permute-start(bf16[320,640]{1,0:T(8,128)(2,1)S(1)} %constant_dynamic-slice_fusion.1), channel_id=1, source_target_pairs={{0,12},{4,0},{8,4},{12,8},{1,13},{5,1},{9,5},{13,9},{2,14},{6,2},{... | collective-permute-start | bytes 1228808 | tf_op jit(solution)/shard_map/ppermute | solution.py:393
  82.5 6.9 %collective-permute-done.12.refs_1_ = bf16[320,640]{1,0:T(8,128)(2,1)S(1)} collective-permute-done((bf16[320,640]{1,0:T(8,128)(2,1)S(1)}, bf16[320,640]{1,0:T(8,128)(2,1)S(1)}, u32[]{:S(2)}, u32[]{:S(2)}) %collective-permute-start.12) | collective-permute-done | bytes 409632 | tf_op jit(solution)/shard_map/ppermute | solution.py:393
  89.4 0.8 collective-permute-start.13
  90.1 6.0 %collective-permute-start.14 = (bf16[320,640]{1,0:T(8,128)(2,1)S(1)}, bf16[320,640]{1,0:T(8,128)(2,1)}, u32[]{:S(2)}, u32[]{:S(2)}) collective-permute-start(bf16[320,640]{1,0:T(8,128)(2,1)S(1)} %collective-permute-done.12.refs_1_), channel_id=1, source_target_pairs={{0,4},{4,8},{8,12},{12,0},{1,5},{5,9},{9,13},{13,1},{2,6},{6,10},{... | collective-permute-start | bytes 1228808 | tf_op jit(solution)/shard_map/ppermute | solution.py:393
  97.0 1.0 collective-permute-start.17
  98.0 9.0 %project.3.q_ref = bf16[896,640]{1,0:T(8,128)(2,1)} custom-call(s32[5]{0:T(128)} %stack.92.place_ref, bf16[896,2560]{1,0:T(8,128)(2,1)} %norm_rows.1.x_ref, bf16[640,640]{1,0:T(8,128)(2,1)} %refs_0_.3, bf16[320,640]{1,0:T(8,128)(2,1)} %copy-done.20, bf16[320,640]{1,0:T(8,128)(2,1)} %copy-done.25, bf16[320,640]{1,0:T(8,128)(2,1)} %copy-done.26, ...), custom_call_target="tpu_custom_call" | custom-call | flops 2936012800 | bytes 9011200 | tf_op jit(solution)/shard_map/project/pallas_call | solution.py:220
  107.0 2.5 %collective-permute-start.18 = (bf16[320,640]{1,0:T(8,128)(2,1)S(1)}, bf16[320,640]{1,0:T(8,128)(2,1)S(1)}, u32[]{:S(2)}, u32[]{:S(2)}) collective-permute-start(bf16[320,640]{1,0:T(8,128)(2,1)S(1)} %constant_dynamic-slice_fusion), channel_id=1, source_target_pairs={{0,4},{4,8},{8,12},{12,0},{1,5},{5,9},{9,13},{13,1},{2,6},{6,10},{... | collective-permute-start | bytes 1228808 | tf_op jit(solution)/shard_map/ppermute | solution.py:393
  109.5 1.1 collective-permute-start.15
  110.6 1.3 collective-permute-start.21
  112.0 9.3 %collective-permute-done.18.refs_4_.refs_3_ = bf16[320,640]{1,0:T(8,128)(2,1)S(1)} collective-permute-done((bf16[320,640]{1,0:T(8,128)(2,1)S(1)}, bf16[320,640]{1,0:T(8,128)(2,1)S(1)}, u32[]{:S(2)}, u32[]{:S(2)}) %collective-permute-start.18) | collective-permute-done | bytes 409632 | tf_op jit(solution)/shard_map/ppermute | solution.py:393
  121.2 1.2 collective-permute-start.19
  123.8 8.5 %project.5.v_ref = bf16[896,640]{1,0:T(8,128)(2,1)} custom-call(s32[5]{0:T(128)} %stack.92.place_ref, bf16[896,2560]{1,0:T(8,128)(2,1)} %norm_rows.1.x_ref, bf16[640,640]{1,0:T(8,128)(2,1)} %refs_0_.5, bf16[320,640]{1,0:T(8,128)(2,1)} %copy-done.28, bf16[320,640]{1,0:T(8,128)(2,1)} %copy-done.30, bf16[320,640]{1,0:T(8,128)(2,1)} %collective-permute-done.14.refs_3_, ...), custom_call_target="tpu_custom_call" | custom-call | flops 2936012800 | bytes 9011200 | tf_op jit(solution)/shard_map/project/pallas_call | solution.py:220
  132.3 0.9 collective-permute-start.23
  133.2 8.9 %attention.2.refs_1_ = bf16[448,640]{1,0:T(8,128)(2,1)} custom-call(s32[2]{0:T(128)} %pad_add_fusion.1.place_ref, s32[3]{0:T(128)} %bitcast.59, bf16[896,640]{1,0:T(8,128)(2,1)} %project.3.q_ref, bf16[896,640]{1,0:T(8,128)(2,1)} %project.4.k_ref, bf16[896,640]{1,0:T(8,128)(2,1)} %project.5.v_ref), custom_call_target="tpu_custom_call" | custom-call | flops 1027604480 | bytes 3440640 | tf_op jit(solution)/shard_map/attention/pallas_call | solution.py:269
  143.5 8.8 %attention.3.refs_2_.refs_0_ = bf16[448,640]{1,0:T(8,128)(2,1)} custom-call(s32[2]{0:T(128)} %pad_add_fusion.place_ref, s32[3]{0:T(128)} %bitcast.60, bf16[896,640]{1,0:T(8,128)(2,1)} %project.3.q_ref, bf16[896,640]{1,0:T(8,128)(2,1)} %project.4.k_ref, bf16[896,640]{1,0:T(8,128)(2,1)} %project.5.v_ref), custom_call_target="tpu_custom_call" | custom-call | flops 1027604480 | bytes 3440640 | tf_op jit(solution)/shard_map/attention/pallas_call | solution.py:269
  153.5 6.6 %out_project.2 = (bf16[4,448,640]{2,1,0:T(8,128)(2,1)}, f32[4,8,640]{2,1,0:T(8,128)}) custom-call(s32[7]{0:T(128)} %stack.86.place_ref, s32[3]{0:T(128)} %get-tuple-element.55.refs_0_, bf16[448,640]{1,0:T(8,128)(2,1)} %attention.2.refs_1_, bf16[448,640]{1,0:T(8,128)(2,1)} %attention.3.refs_2_.refs_0_, bf16[640,640]{1,0:T(8,128)(2,1)} %refs_2_.1, ...), custom_call_target="tpu_custom_call" | custom-call | flops 1468006400 | bytes 6144000 | tf_op jit(solution)/shard_map/out_project/pallas_call | solution.py:365
  160.7 1.8 collective-permute-start.26
  162.9 3.0 %convolution_bitcast_fusion = f32[4,3,640]{2,1,0:T(4,128)S(1)} fusion(bf16[4,896,640]{2,1,0:T(8,128)(2,1)} %bitcast.47, s32[3]{0:T(128)S(1)} %copy-done.15), kind=kOutput, calls=%fused_computation.3 | convolution fusion | flops 13765248 | bytes 4618252 | tf_op jit(solution)/shard_map/sr,brw->bsw/dot_general | solution.py:451
  166.0 1.5 collective-permute-done.25
  167.6 4.5 %collective-permute-start.32 = (bf16[5,8,640]{2,1,0:T(8,128)(2,1)S(1)}, bf16[5,8,640]{2,1,0:T(8,128)(2,1)S(1)}, u32[]{:S(2)}, u32[]{:S(2)}) collective-permute-start(bf16[5,8,640]{2,1,0:T(8,128)(2,1)S(1)} %get-tuple-element.60), channel_id=1, source_target_pairs={{0,12},{4,0},{8,4},{12,8},{1,13},{5,1},{9,5},{13,9},{2,14},{6,2},{... | collective-permute-start | bytes 153608 | tf_op jit(solution)/shard_map/ppermute | solution.py:393
  172.5 1.9 collective-permute-start.30
  174.4 1.5 copy-done.2
  175.9 6.7 %out_project.3 = bf16[4,448,640]{2,1,0:T(8,128)(2,1)} custom-call(s32[7]{0:T(128)} %stack.86.place_ref, bf16[448,640]{1,0:T(8,128)(2,1)} %attention.3.refs_2_.refs_0_, bf16[4,448,640]{2,1,0:T(8,128)(2,1)} %copy-done.2, bf16[640,640]{1,0:T(8,128)(2,1)} %refs_2_.1, bf16[320,640]{1,0:T(8,128)(2,1)} %copy-done.4, bf16[320,640]{1,0:T(8,128)(2,1)} %copy-done.6, ...), custom_call_target="tpu_custom_call" | custom-call | flops 1468006400 | bytes 8437760 | tf_op jit(solution)/shard_map/out_project/pallas_call | solution.py:365
  182.7 2.5 %slice.37 = bf16[2,448,640]{2,1,0:T(8,128)(2,1)} slice(bf16[4,448,640]{2,1,0:T(8,128)(2,1)} %out_project.3), slice={[2:4], [0:448], [0:640]} | slice | bytes 2293760 | tf_op jit(solution)/shard_map/slice | solution.py:490
  185.2 1.1 collective-permute-start.28
  187.8 24.3 %collective-permute-done.28 = bf16[2,448,640]{2,1,0:T(8,128)(2,1)} collective-permute-done((bf16[2,448,640]{2,1,0:T(8,128)(2,1)}, bf16[2,448,640]{2,1,0:T(8,128)(2,1)}, u32[]{:S(2)}, u32[]{:S(2)}) %collective-permute-start.28) | collective-permute-done | bytes 1146912 | tf_op jit(solution)/shard_map/ppermute | solution.py:448
  212.1 2.0 fusion
  215.1 1.0 collective-permute-done.29
  216.1 1.4 maximum_select_fusion
  (143 shorter events, 13.8 us)
Async XLA Ops:
  7.2 180.2 %copy-start = (bf16[33,2560]{1,0:T(8,128)(2,1)S(1)}, bf16[33,2560]{1,0:T(8,128)(2,1)}, u32[]{:S(2)}) copy-start(bf16[33,2560]{1,0:T(8,128)(2,1)} %param.19) | copy-start | bytes 506884
  7.2 46.8 %all-gather.3.cloned.1.call-start = ((), (), s32[]{:S(2)}) async-start(), calls=%async_computation | async-start | bytes 5734400 | tf_op jit(solution)/shard_map/all_gather | solution.py:431
  8.4 15.4 %collective-permute-start.6 = (bf16[320,640]{1,0:T(8,128)(2,1)S(1)}, bf16[320,640]{1,0:T(8,128)(2,1)S(1)}, u32[]{:S(2)}, u32[]{:S(2)}) collective-permute-start(bf16[320,640]{1,0:T(8,128)(2,1)S(1)} %constant_dynamic-slice_fusion.2), channel_id=1, source_target_pairs={{0,4},{4,8},{8,12},{12,0},{1,5},{5,9},{9,13},{13,1},{2,6},{6,10},{... | collective-permute-start | bytes 1228808 | tf_op jit(solution)/shard_map/ppermute | solution.py:393
  11.5 19.9 %collective-permute-start = (bf16[320,640]{1,0:T(8,128)(2,1)S(1)}, bf16[320,640]{1,0:T(8,128)(2,1)S(1)}, u32[]{:S(2)}, u32[]{:S(2)}) collective-permute-start(bf16[320,640]{1,0:T(8,128)(2,1)S(1)} %constant_dynamic-slice_fusion.2), channel_id=1, source_target_pairs={{0,12},{4,0},{8,4},{12,8},{1,13},{5,1},{9,5},{13,9},{2,14},{6,2},{... | collective-permute-start | bytes 1228808 | tf_op jit(solution)/shard_map/ppermute | solution.py:393
  13.8 36.5 %copy-start.14 = (s32[3,1]{0,1:T(1,128)}, s32[3,1]{0,1:T(1,128)S(1)}, u32[]{:S(2)}) copy-start(s32[3,1]{0,1:T(1,128)S(1)} %reduce-window.8) | copy-start | bytes 40
  23.8 26.4 %copy-start.22 = (bf16[320,640]{1,0:T(8,128)(2,1)}, bf16[320,640]{1,0:T(8,128)(2,1)S(1)}, u32[]{:S(2)}) copy-start(bf16[320,640]{1,0:T(8,128)(2,1)S(1)} %collective-permute-done.6.refs_1_) | copy-start | bytes 1228804
  23.8 19.3 %collective-permute-start.7 = (bf16[320,640]{1,0:T(8,128)(2,1)S(1)}, bf16[320,640]{1,0:T(8,128)(2,1)}, u32[]{:S(2)}, u32[]{:S(2)}) collective-permute-start(bf16[320,640]{1,0:T(8,128)(2,1)S(1)} %collective-permute-done.6.refs_1_), channel_id=1, source_target_pairs={{0,4},{4,8},{8,12},{12,0},{1,5},{5,9},{9,13},{13,1},{2,6},{6,10},{... | collective-permute-start | bytes 1228808 | tf_op jit(solution)/shard_map/ppermute | solution.py:393
  23.9 21.2 %collective-permute-start.9 = (bf16[320,640]{1,0:T(8,128)(2,1)S(1)}, bf16[320,640]{1,0:T(8,128)(2,1)S(1)}, u32[]{:S(2)}, u32[]{:S(2)}) collective-permute-start(bf16[320,640]{1,0:T(8,128)(2,1)S(1)} %collective-permute-done.6.refs_1_), channel_id=1, source_target_pairs={{0,16},{16,0},{1,17},{17,1},{2,18},{18,2},{3,19},{19,3},{4,20},{20... | collective-permute-start | bytes 1228808 | tf_op jit(solution)/shard_map/ppermute | solution.py:405
  31.4 18.9 %copy-start.23 = (bf16[320,640]{1,0:T(8,128)(2,1)}, bf16[320,640]{1,0:T(8,128)(2,1)S(1)}, u32[]{:S(2)}) copy-start(bf16[320,640]{1,0:T(8,128)(2,1)S(1)} %collective-permute-done.refs_5_) | copy-start | bytes 1228804
  31.4 20.3 %collective-permute-start.1 = (bf16[320,640]{1,0:T(8,128)(2,1)S(1)}, bf16[320,640]{1,0:T(8,128)(2,1)S(1)}, u32[]{:S(2)}, u32[]{:S(2)}) collective-permute-start(bf16[320,640]{1,0:T(8,128)(2,1)S(1)} %constant_dynamic-slice_fusion.3), channel_id=1, source_target_pairs={{0,4},{4,8},{8,12},{12,0},{1,5},{5,9},{9,13},{13,1},{2,6},{6,10},{... | collective-permute-start | bytes 1228808 | tf_op jit(solution)/shard_map/ppermute | solution.py:393
  33.7 18.1 %collective-permute-start.2 = (bf16[320,640]{1,0:T(8,128)(2,1)S(1)}, bf16[320,640]{1,0:T(8,128)(2,1)S(1)}, u32[]{:S(2)}, u32[]{:S(2)}) collective-permute-start(bf16[320,640]{1,0:T(8,128)(2,1)S(1)} %collective-permute-done.refs_5_), channel_id=1, source_target_pairs={{0,16},{16,0},{1,17},{17,1},{2,18},{18,2},{3,19},{19,3},{4,20},{20... | collective-permute-start | bytes 1228808 | tf_op jit(solution)/shard_map/ppermute | solution.py:405
  43.2 18.8 %collective-permute-start.8 = (bf16[320,640]{1,0:T(8,128)(2,1)S(1)}, bf16[320,640]{1,0:T(8,128)(2,1)S(1)}, u32[]{:S(2)}, u32[]{:S(2)}) collective-permute-start(bf16[320,640]{1,0:T(8,128)(2,1)S(1)} %constant_dynamic-slice_fusion.3), channel_id=1, source_target_pairs={{0,12},{4,0},{8,4},{12,8},{1,13},{5,1},{9,5},{13,9},{2,14},{6,2},{... | collective-permute-start | bytes 1228808 | tf_op jit(solution)/shard_map/ppermute | solution.py:393
  45.8 16.2 %collective-permute-start.10 = (bf16[320,640]{1,0:T(8,128)(2,1)}, bf16[320,640]{1,0:T(8,128)(2,1)}, u32[]{:S(2)}, u32[]{:S(2)}) collective-permute-start(bf16[320,640]{1,0:T(8,128)(2,1)} %collective-permute-done.7.refs_3_), channel_id=1, source_target_pairs={{0,16},{16,0},{1,17},{17,1},{2,18},{18,2},{3,19},{19,3},{4,20},{20... | collective-permute-start | bytes 1228808 | tf_op jit(solution)/shard_map/ppermute | solution.py:405
  52.5 19.7 %collective-permute-start.3 = (bf16[320,640]{1,0:T(8,128)(2,1)S(1)}, bf16[320,640]{1,0:T(8,128)(2,1)S(1)}, u32[]{:S(2)}, u32[]{:S(2)}) collective-permute-start(bf16[320,640]{1,0:T(8,128)(2,1)S(1)} %collective-permute-done.1.refs_1_), channel_id=1, source_target_pairs={{0,16},{16,0},{1,17},{17,1},{2,18},{18,2},{3,19},{19,3},{4,20},{20... | collective-permute-start | bytes 1228808 | tf_op jit(solution)/shard_map/ppermute | solution.py:405
  60.3 15.6 %collective-permute-start.4 = (bf16[320,640]{1,0:T(8,128)(2,1)S(1)}, bf16[320,640]{1,0:T(8,128)(2,1)S(1)}, u32[]{:S(2)}, u32[]{:S(2)}) collective-permute-start(bf16[320,640]{1,0:T(8,128)(2,1)S(1)} %collective-permute-done.1.refs_1_), channel_id=1, source_target_pairs={{0,4},{4,8},{8,12},{12,0},{1,5},{5,9},{9,13},{13,1},{2,6},{6,10},{... | collective-permute-start | bytes 1228808 | tf_op jit(solution)/shard_map/ppermute | solution.py:393
  62.0 20.5 %collective-permute-start.11 = (bf16[320,640]{1,0:T(8,128)(2,1)S(1)}, bf16[320,640]{1,0:T(8,128)(2,1)S(1)}, u32[]{:S(2)}, u32[]{:S(2)}) collective-permute-start(bf16[320,640]{1,0:T(8,128)(2,1)S(1)} %collective-permute-done.8.refs_5_), channel_id=1, source_target_pairs={{0,16},{16,0},{1,17},{17,1},{2,18},{18,2},{3,19},{19,3},{4,20},{20... | collective-permute-start | bytes 1228808 | tf_op jit(solution)/shard_map/ppermute | solution.py:405
  62.7 33.4 %copy-start.3 = (bf16[640,640]{1,0:T(8,128)(2,1)S(1)}, bf16[640,640]{1,0:T(8,128)(2,1)}, u32[]{:S(2)}) copy-start(bf16[640,640]{1,0:T(8,128)(2,1)} %refs_2_.1) | copy-start | bytes 2457604
  71.8 17.6 %collective-permute-start.12 = (bf16[320,640]{1,0:T(8,128)(2,1)S(1)}, bf16[320,640]{1,0:T(8,128)(2,1)S(1)}, u32[]{:S(2)}, u32[]{:S(2)}) collective-permute-start(bf16[320,640]{1,0:T(8,128)(2,1)S(1)} %constant_dynamic-slice_fusion.1), channel_id=1, source_target_pairs={{0,4},{4,8},{8,12},{12,0},{1,5},{5,9},{9,13},{13,1},{2,6},{6,10},{... | collective-permute-start | bytes 1228808 | tf_op jit(solution)/shard_map/ppermute | solution.py:393
  72.2 25.7 %copy-start.25 = (bf16[320,640]{1,0:T(8,128)(2,1)}, bf16[320,640]{1,0:T(8,128)(2,1)S(1)}, u32[]{:S(2)}) copy-start(bf16[320,640]{1,0:T(8,128)(2,1)S(1)} %collective-permute-done.3.refs_2_) | copy-start | bytes 1228804
  76.0 22.0 %copy-start.26 = (bf16[320,640]{1,0:T(8,128)(2,1)}, bf16[320,640]{1,0:T(8,128)(2,1)S(1)}, u32[]{:S(2)}) copy-start(bf16[320,640]{1,0:T(8,128)(2,1)S(1)} %collective-permute-done.4.refs_3_) | copy-start | bytes 1228804
  76.0 20.2 %collective-permute-start.5 = (bf16[320,640]{1,0:T(8,128)(2,1)S(1)}, bf16[320,640]{1,0:T(8,128)(2,1)S(1)}, u32[]{:S(2)}, u32[]{:S(2)}) collective-permute-start(bf16[320,640]{1,0:T(8,128)(2,1)S(1)} %collective-permute-done.4.refs_3_), channel_id=1, source_target_pairs={{0,16},{16,0},{1,17},{17,1},{2,18},{18,2},{3,19},{19,3},{4,20},{20... | collective-permute-start | bytes 1228808 | tf_op jit(solution)/shard_map/ppermute | solution.py:405
  76.5 19.8 %collective-permute-start.16 = (bf16[320,640]{1,0:T(8,128)(2,1)S(1)}, bf16[320,640]{1,0:T(8,128)(2,1)S(1)}, u32[]{:S(2)}, u32[]{:S(2)}) collective-permute-start(bf16[320,640]{1,0:T(8,128)(2,1)S(1)} %constant_dynamic-slice_fusion.1), channel_id=1, source_target_pairs={{0,12},{4,0},{8,4},{12,8},{1,13},{5,1},{9,5},{13,9},{2,14},{6,2},{... | collective-permute-start | bytes 1228808 | tf_op jit(solution)/shard_map/ppermute | solution.py:393
  89.4 17.6 %copy-start.28 = (bf16[320,640]{1,0:T(8,128)(2,1)}, bf16[320,640]{1,0:T(8,128)(2,1)S(1)}, u32[]{:S(2)}) copy-start(bf16[320,640]{1,0:T(8,128)(2,1)S(1)} %collective-permute-done.12.refs_1_) | copy-start | bytes 1228804
  89.4 20.1 %collective-permute-start.13 = (bf16[320,640]{1,0:T(8,128)(2,1)S(1)}, bf16[320,640]{1,0:T(8,128)(2,1)S(1)}, u32[]{:S(2)}, u32[]{:S(2)}) collective-permute-start(bf16[320,640]{1,0:T(8,128)(2,1)S(1)} %collective-permute-done.12.refs_1_), channel_id=1, source_target_pairs={{0,16},{16,0},{1,17},{17,1},{2,18},{18,2},{3,19},{19,3},{4,20},{20... | collective-permute-start | bytes 1228808 | tf_op jit(solution)/shard_map/ppermute | solution.py:405
  90.1 19.4 %collective-permute-start.14 = (bf16[320,640]{1,0:T(8,128)(2,1)S(1)}, bf16[320,640]{1,0:T(8,128)(2,1)}, u32[]{:S(2)}, u32[]{:S(2)}) collective-permute-start(bf16[320,640]{1,0:T(8,128)(2,1)S(1)} %collective-permute-done.12.refs_1_), channel_id=1, source_target_pairs={{0,4},{4,8},{8,12},{12,0},{1,5},{5,9},{9,13},{13,1},{2,6},{6,10},{... | collective-permute-start | bytes 1228808 | tf_op jit(solution)/shard_map/ppermute | solution.py:393
  97.0 10.0 %copy-start.29 = (bf16[320,640]{1,0:T(8,128)(2,1)}, bf16[320,640]{1,0:T(8,128)(2,1)S(1)}, u32[]{:S(2)}) copy-start(bf16[320,640]{1,0:T(8,128)(2,1)S(1)} %collective-permute-done.16.refs_5_) | copy-start | bytes 1228804
  97.0 15.0 %collective-permute-start.17 = (bf16[320,640]{1,0:T(8,128)(2,1)S(1)}, bf16[320,640]{1,0:T(8,128)(2,1)}, u32[]{:S(2)}, u32[]{:S(2)}) collective-permute-start(bf16[320,640]{1,0:T(8,128)(2,1)S(1)} %collective-permute-done.16.refs_5_), channel_id=1, source_target_pairs={{0,16},{16,0},{1,17},{17,1},{2,18},{18,2},{3,19},{19,3},{4,20},{20... | collective-permute-start | bytes 1228808 | tf_op jit(solution)/shard_map/ppermute | solution.py:405
  107.0 14.3 %collective-permute-start.18 = (bf16[320,640]{1,0:T(8,128)(2,1)S(1)}, bf16[320,640]{1,0:T(8,128)(2,1)S(1)}, u32[]{:S(2)}, u32[]{:S(2)}) collective-permute-start(bf16[320,640]{1,0:T(8,128)(2,1)S(1)} %constant_dynamic-slice_fusion), channel_id=1, source_target_pairs={{0,4},{4,8},{8,12},{12,0},{1,5},{5,9},{9,13},{13,1},{2,6},{6,10},{... | collective-permute-start | bytes 1228808 | tf_op jit(solution)/shard_map/ppermute | solution.py:393
  109.5 13.5 %copy-start.30 = (bf16[320,640]{1,0:T(8,128)(2,1)}, bf16[320,640]{1,0:T(8,128)(2,1)S(1)}, u32[]{:S(2)}) copy-start(bf16[320,640]{1,0:T(8,128)(2,1)S(1)} %collective-permute-done.13.refs_2_) | copy-start | bytes 1228804
  109.5 13.5 %collective-permute-start.15 = (bf16[320,640]{1,0:T(8,128)(2,1)}, bf16[320,640]{1,0:T(8,128)(2,1)S(1)}, u32[]{:S(2)}, u32[]{:S(2)}) collective-permute-start(bf16[320,640]{1,0:T(8,128)(2,1)} %collective-permute-done.14.refs_3_), channel_id=1, source_target_pairs={{0,16},{16,0},{1,17},{17,1},{2,18},{18,2},{3,19},{19,3},{4,20},{20... | collective-permute-start | bytes 1228808 | tf_op jit(solution)/shard_map/ppermute | solution.py:405
  110.6 21.7 %collective-permute-start.21 = (bf16[320,640]{1,0:T(8,128)(2,1)S(1)}, bf16[320,640]{1,0:T(8,128)(2,1)S(1)}, u32[]{:S(2)}, u32[]{:S(2)}) collective-permute-start(bf16[320,640]{1,0:T(8,128)(2,1)S(1)} %constant_dynamic-slice_fusion), channel_id=1, source_target_pairs={{0,12},{4,0},{8,4},{12,8},{1,13},{5,1},{9,5},{13,9},{2,14},{6,2},{... | collective-permute-start | bytes 1228808 | tf_op jit(solution)/shard_map/ppermute | solution.py:393
  121.2 11.1 %copy-start.4 = (bf16[320,640]{1,0:T(8,128)(2,1)}, bf16[320,640]{1,0:T(8,128)(2,1)S(1)}, u32[]{:S(2)}) copy-start(bf16[320,640]{1,0:T(8,128)(2,1)S(1)} %collective-permute-done.18.refs_4_.refs_3_) | copy-start | bytes 1228804
  121.2 20.9 %collective-permute-start.19 = (bf16[320,640]{1,0:T(8,128)(2,1)S(1)}, bf16[320,640]{1,0:T(8,128)(2,1)S(1)}, u32[]{:S(2)}, u32[]{:S(2)}) collective-permute-start(bf16[320,640]{1,0:T(8,128)(2,1)S(1)} %collective-permute-done.18.refs_4_.refs_3_), channel_id=1, source_target_pairs={{0,16},{16,0},{1,17},{17,1},{2,18},{18,2},{3,19},{19,3},{4,20},{20... | collective-permute-start | bytes 1228808 | tf_op jit(solution)/shard_map/ppermute | solution.py:405
  123.0 29.4 %collective-permute-start.20 = (bf16[320,640]{1,0:T(8,128)(2,1)S(1)}, bf16[320,640]{1,0:T(8,128)(2,1)S(1)}, u32[]{:S(2)}, u32[]{:S(2)}) collective-permute-start(bf16[320,640]{1,0:T(8,128)(2,1)S(1)} %collective-permute-done.18.refs_4_.refs_3_), channel_id=1, source_target_pairs={{0,4},{4,8},{8,12},{12,0},{1,5},{5,9},{9,13},{13,1},{2,6},{6,10},{... | collective-permute-start | bytes 1228808 | tf_op jit(solution)/shard_map/ppermute | solution.py:393
  132.3 20.1 %collective-permute-start.23 = (bf16[320,640]{1,0:T(8,128)(2,1)S(1)}, bf16[320,640]{1,0:T(8,128)(2,1)S(1)}, u32[]{:S(2)}, u32[]{:S(2)}) collective-permute-start(bf16[320,640]{1,0:T(8,128)(2,1)S(1)} %collective-permute-done.21.refs_8_.refs_7_), channel_id=1, source_target_pairs={{0,16},{16,0},{1,17},{17,1},{2,18},{18,2},{3,19},{19,3},{4,20},{20... | collective-permute-start | bytes 1228808 | tf_op jit(solution)/shard_map/ppermute | solution.py:405
  142.1 10.3 %copy-start.6 = (bf16[320,640]{1,0:T(8,128)(2,1)}, bf16[320,640]{1,0:T(8,128)(2,1)S(1)}, u32[]{:S(2)}) copy-start(bf16[320,640]{1,0:T(8,128)(2,1)S(1)} %collective-permute-done.19.refs_5_.refs_4_) | copy-start | bytes 1228804
  142.1 10.3 %collective-permute-start.22 = (bf16[320,640]{1,0:T(8,128)(2,1)S(1)}, bf16[320,640]{1,0:T(8,128)(2,1)S(1)}, u32[]{:S(2)}, u32[]{:S(2)}) collective-permute-start(bf16[320,640]{1,0:T(8,128)(2,1)S(1)} %collective-permute-done.19.refs_5_.refs_4_), channel_id=1, source_target_pairs={{0,4},{4,8},{8,12},{12,0},{1,5},{5,9},{9,13},{13,1},{2,6},{6,10},{... | collective-permute-start | bytes 1228808 | tf_op jit(solution)/shard_map/ppermute | solution.py:393
  160.1 14.3 %collective-permute-start.27 = (bf16[4,448,640]{2,1,0:T(8,128)(2,1)}, bf16[4,448,640]{2,1,0:T(8,128)(2,1)S(1)}, u32[]{:S(2)}, u32[]{:S(2)}) collective-permute-start(bf16[4,448,640]{2,1,0:T(8,128)(2,1)} %get-tuple-element.50), channel_id=1, source_target_pairs={{0,1},{1,0},{2,3},{3,2},{4,5},{5,4},{6,7},{7,6},{8,9},{9,8},{10,11... | collective-permute-start | bytes 6881288 | tf_op jit(solution)/shard_map/ppermute | solution.py:448
  160.7 5.3 %collective-permute-start.26 = (f32[4,8,640]{2,1,0:T(8,128)}, f32[4,8,640]{2,1,0:T(8,128)S(1)}, u32[]{:S(2)}, u32[]{:S(2)}) collective-permute-start(f32[4,8,640]{2,1,0:T(8,128)} %get-tuple-element.48), channel_id=1, source_target_pairs={{0,3},{1,2},{2,1},{3,0},{4,7},{5,6},{6,5},{7,4},{8,11},{9,10},{10,... | collective-permute-start | bytes 245768 | tf_op jit(solution)/shard_map/ppermute | solution.py:448
  162.5 3.5 %collective-permute-start.24 = (f32[4,8,640]{2,1,0:T(8,128)}, f32[4,8,640]{2,1,0:T(8,128)S(1)}, u32[]{:S(2)}, u32[]{:S(2)}) collective-permute-start(f32[4,8,640]{2,1,0:T(8,128)} %get-tuple-element.48), channel_id=1, source_target_pairs={{0,1},{1,0},{2,3},{3,2},{4,5},{5,4},{6,7},{7,6},{8,9},{9,8},{10,11... | collective-permute-start | bytes 245768 | tf_op jit(solution)/shard_map/ppermute | solution.py:448
  162.5 5.0 %collective-permute-start.25 = (f32[4,8,640]{2,1,0:T(8,128)}, f32[4,8,640]{2,1,0:T(8,128)S(1)}, u32[]{:S(2)}, u32[]{:S(2)}) collective-permute-start(f32[4,8,640]{2,1,0:T(8,128)} %get-tuple-element.48), channel_id=1, source_target_pairs={{0,2},{1,3},{2,0},{3,1},{4,6},{5,7},{6,4},{7,5},{8,10},{9,11},{10,... | collective-permute-start | bytes 245768 | tf_op jit(solution)/shard_map/ppermute | solution.py:448
  167.6 18.7 %collective-permute-start.32 = (bf16[5,8,640]{2,1,0:T(8,128)(2,1)S(1)}, bf16[5,8,640]{2,1,0:T(8,128)(2,1)S(1)}, u32[]{:S(2)}, u32[]{:S(2)}) collective-permute-start(bf16[5,8,640]{2,1,0:T(8,128)(2,1)S(1)} %get-tuple-element.60), channel_id=1, source_target_pairs={{0,12},{4,0},{8,4},{12,8},{1,13},{5,1},{9,5},{13,9},{2,14},{6,2},{... | collective-permute-start | bytes 153608 | tf_op jit(solution)/shard_map/ppermute | solution.py:393
  172.1 14.3 %collective-permute-start.31 = (bf16[5,8,640]{2,1,0:T(8,128)(2,1)S(1)}, bf16[5,8,640]{2,1,0:T(8,128)(2,1)S(1)}, u32[]{:S(2)}, u32[]{:S(2)}) collective-permute-start(bf16[5,8,640]{2,1,0:T(8,128)(2,1)S(1)} %get-tuple-element.60), channel_id=1, source_target_pairs={{0,8},{4,12},{8,0},{12,4},{1,9},{5,13},{9,1},{13,5},{2,10},{6,14},... | collective-permute-start | bytes 153608 | tf_op jit(solution)/shard_map/ppermute | solution.py:393
  172.5 13.9 %collective-permute-start.30 = (bf16[5,8,640]{2,1,0:T(8,128)(2,1)S(1)}, bf16[5,8,640]{2,1,0:T(8,128)(2,1)S(1)}, u32[]{:S(2)}, u32[]{:S(2)}) collective-permute-start(bf16[5,8,640]{2,1,0:T(8,128)(2,1)S(1)} %get-tuple-element.60), channel_id=1, source_target_pairs={{0,4},{4,8},{8,12},{12,0},{1,5},{5,9},{9,13},{13,1},{2,6},{6,10},{... | collective-permute-start | bytes 153608 | tf_op jit(solution)/shard_map/ppermute | solution.py:393
  182.6 29.4 %copy-start.1 = (bf16[4,448,640]{2,1,0:T(8,128)(2,1)S(1)}, bf16[4,448,640]{2,1,0:T(8,128)(2,1)}, u32[]{:S(2)}) copy-start(bf16[4,448,640]{2,1,0:T(8,128)(2,1)} %out_project.3) | copy-start | bytes 6881284
  185.2 26.9 %collective-permute-start.28 = (bf16[2,448,640]{2,1,0:T(8,128)(2,1)}, bf16[2,448,640]{2,1,0:T(8,128)(2,1)}, u32[]{:S(2)}, u32[]{:S(2)}) collective-permute-start(bf16[2,448,640]{2,1,0:T(8,128)(2,1)} %slice.37), channel_id=1, source_target_pairs={{0,2},{1,3},{2,0},{3,1},{4,6},{5,7},{6,4},{7,5},{8,10},{9,11},{10,... | collective-permute-start | bytes 3440648 | tf_op jit(solution)/shard_map/ppermute | solution.py:448
  187.8 26.6 %copy-start.17 = (f32[3,33]{1,0:T(4,128)}, f32[3,33]{1,0:T(4,128)S(1)}, u32[]{:S(2)}) copy-start(f32[3,33]{1,0:T(4,128)S(1)} %get-tuple-element.67) | copy-start | bytes 1192
  214.1 2.0 collective-permute-start.29
  (21 other events, 98.8 us)
Sparse Core Ops, SparseCore 0:
  9.6 39.3 all-gather.2

commit v3 on v2

--- a/solution.py
+++ b/solution.py
@@ -127,15 +127,28 @@
 HBM_SPEC = pl.BlockSpec(memory_space=pltpu.HBM)
 
 
-def params(*semantics):
+def params(*semantics, limit=VMEM_LIMIT):
     return pltpu.CompilerParams(
-        vmem_limit_bytes=VMEM_LIMIT, dimension_semantics=semantics or None
-    )
-
-
-def norm_kernel(x_ref, out_ref):
-    blocks, _, width = x_ref.shape
+        vmem_limit_bytes=limit, dimension_semantics=semantics or None
+    )
+
+
+def norm_kernel(column_ref, picked_ref, x_ref, out_ref, rows_ref):
+    blocks, size, width = x_ref.shape
     count = blocks * width
+    base = pl.program_id(0) * size
+    slot = lax.broadcasted_iota(jnp.int32, (rows_ref.shape[1], size), 0)
+    row = lax.broadcasted_iota(jnp.int32, (rows_ref.shape[1], size), 1) + base
+    hit = sum(
+        ((slot == j) & (row == picked_ref[j])).astype(F32) for j in range(picked_ref.shape[0])
+    ).astype(BF16)
+
+    @pl.when(pl.program_id(0) == 0)
+    def _():
+        rows_ref[...] = jnp.zeros_like(rows_ref)
+
+    for b in range(blocks):
+        rows_ref[b ^ column_ref[0]] += jnp.dot(hit, x_ref[b], preferred_element_type=F32)
     values = [x_ref[b].astype(F32) for b in range(blocks)]
     average = sum(jnp.sum(v, -1, keepdims=True) for v in values) / count
     centred = [v - average for v in values]
@@ -145,20 +158,30 @@
         out_ref[:, b * width : (b + 1) * width] = (centred[b] * scale).astype(BF16)
 
 
-def norm_blocks(stack, row_block=224):
+def norm_blocks(column, picked, stack, row_block=224):
     blocks, rows, width = stack.shape
     return pl.pallas_call(
         norm_kernel,
         grid=(rows // row_block,),
-        in_specs=[pl.BlockSpec((blocks, row_block, width), lambda i: (0, i, 0))],
-        out_specs=pl.BlockSpec((row_block, blocks * width), lambda i: (i, 0)),
-        out_shape=jax.ShapeDtypeStruct((rows, blocks * width), BF16),
+        in_specs=[
+            SMEM_SPEC,
+            SMEM_SPEC,
+            pl.BlockSpec((blocks, row_block, width), lambda i: (0, i, 0)),
+        ],
+        out_specs=[
+            pl.BlockSpec((row_block, blocks * width), lambda i: (i, 0)),
+            pl.BlockSpec((blocks, 8, width), lambda i: (0, 0, 0)),
+        ],
+        out_shape=[
+            jax.ShapeDtypeStruct((rows, blocks * width), BF16),
+            jax.ShapeDtypeStruct((blocks, 8, width), F32),
+        ],
         compiler_params=params("arbitrary"),
         cost_estimate=pl.CostEstimate(
             flops=8 * stack.size, bytes_accessed=4 * stack.size, transcendentals=rows
         ),
         name="norm_rows",
-    )(stack)
+    )(column[None].astype(jnp.int32), picked, stack)
 
 
 def shard_parts(part, shard, half):
@@ -241,7 +264,6 @@
 
 def attend_kernel(place_ref, ends_ref, q_ref, k_ref, v_ref, out_ref, *, row_block):
     count = k_ref.shape[0]
-    keys, values = k_ref[...], v_ref[...]
     base = place_ref[1] * q_ref.shape[0]
     col = lax.broadcasted_iota(jnp.int32, (1, count), 1)
     sequences = ends_ref.shape[0]
@@ -250,33 +272,39 @@
         span = slice(r * row_block, (r + 1) * row_block)
         row = lax.broadcasted_iota(jnp.int32, (row_block, 1), 0) + (base + r * row_block)
         row_label = sum((row >= ends_ref[j]).astype(jnp.int32) for j in range(sequences - 1))
-        scores = lax.dot_general(
-            q_ref[span, :], keys, (((1,), (1,)), ((), ())), preferred_element_type=F32
-        )
-        scores = jnp.where(row_label == col_label, scores, -1e30)
-        top = jnp.max(scores, -1, keepdims=True)
-        raised = jnp.exp(scores - top)
-        weights = raised * (1.0 / jnp.sum(raised, -1, keepdims=True))
-        out_ref[span, :] = jnp.dot(
-            weights.astype(BF16), values, preferred_element_type=F32
-        ).astype(BF16)
-
-
-def attention(place, ends, queries, key_rows, value_rows, row_block=224):
+        for h in range(q_ref.shape[1] // HS):
+            head = slice(h * HS, (h + 1) * HS)
+            scores = lax.dot_general(
+                q_ref[span, head],
+                k_ref[:, head],
+                (((1,), (1,)), ((), ())),
+                preferred_element_type=F32,
+            )
+            scores = jnp.where(row_label == col_label, scores, -1e30)
+            top = jnp.max(scores, -1, keepdims=True)
+            raised = jnp.exp(scores - top)
+            weights = raised * (1.0 / jnp.sum(raised, -1, keepdims=True))
+            out_ref[span, head] = jnp.dot(
+                weights.astype(BF16), v_ref[:, head], preferred_element_type=F32
+            ).astype(BF16)
+
+
+def attention(place, ends, queries, key_rows, value_rows, row_block=448, group=5):
     rows, columns = queries.shape
     half = rows // 2
     heads = columns // HS
+    wide = group * HS
     return pl.pallas_call(
         functools.partial(attend_kernel, row_block=row_block),
         grid_spec=pltpu.PrefetchScalarGridSpec(
             num_scalar_prefetch=2,
-            grid=(heads,),
+            grid=(heads // group,),
             in_specs=[
-                pl.BlockSpec((half, HS), lambda h, place, ends: (place[1], h)),
-                pl.BlockSpec((rows, HS), lambda h, place, ends: (0, h)),
-                pl.BlockSpec((rows, HS), lambda h, place, ends: (0, h)),
+                pl.BlockSpec((half, wide), lambda h, place, ends: (place[1], h)),
+                pl.BlockSpec((rows, wide), lambda h, place, ends: (0, h)),
+                pl.BlockSpec((rows, wide), lambda h, place, ends: (0, h)),
             ],
-            out_specs=pl.BlockSpec((half, HS), lambda h, place, ends: (0, h)),
+            out_specs=pl.BlockSpec((half, wide), lambda h, place, ends: (0, h)),
         ),
         out_shape=jax.ShapeDtypeStruct((half, columns), BF16),
         compiler_params=params("arbitrary"),
@@ -289,7 +317,7 @@
     )(place, ends, queries, key_rows, value_rows)
 
 
-def out_kernel(adding, lengths, place_ref, *refs):
+def out_kernel(adding, base, lengths, place_ref, *refs):
     refs = list(refs)
     if adding:
         x_ref, come_ref = refs.pop(0), refs.pop(0)
@@ -302,24 +330,28 @@
     wbuf, sems = refs
     block = pl.program_id(0)
     half = wbuf.shape[1] // 2
-    part, core, column = place_ref[0], place_ref[5], place_ref[6]
+    part, core = place_ref[0], place_ref[5]
 
     @pl.when(block == 0)
     def _():
         for k, shard in enumerate(shards):
-            spot = place_ref[1 + k]
-            for j, (source, row) in enumerate(shard_parts(part, shard, half)):
-                pltpu.make_async_copy(
-                    source, wbuf.at[spot, pl.ds(row, half)], sems.at[spot, j]
-                ).start()
+            spot = place_ref[1 + k] - base
+
+            @pl.when((spot >= 0) & (spot < 2))
+            def _():
+                for j, (source, row) in enumerate(shard_parts(part, shard, half)):
+                    pltpu.make_async_copy(
+                        source, wbuf.at[spot, pl.ds(row, half)], sems.at[spot, j]
+                    ).start()
+
         if not adding:
             size = x_ref.shape[0]
             slot = lax.broadcasted_iota(jnp.int32, (marked.shape[0], size), 0)
             row = lax.broadcasted_iota(jnp.int32, (marked.shape[0], size), 1)
             total = None
-            for ref, base in ((x_ref, (1 - core) * size), (kept_ref, core * size)):
+            for ref, first in ((x_ref, (1 - core) * size), (kept_ref, core * size)):
                 hit = sum(
-                    ((slot == j) & (row + base == picked_ref[j])).astype(F32)
+                    ((slot == j) & (row + first == picked_ref[j])).astype(F32)
                     for j in range(picked_ref.shape[0])
                 )
                 term = jnp.dot(hit.astype(BF16), ref[...], preferred_element_type=F32)
@@ -336,13 +368,11 @@
     if adding:
         total = total + come_ref[...].astype(F32)
     else:
-        rows_ref[block ^ column] = jnp.dot(
-            marked[...], wbuf[block], preferred_element_type=F32
-        )
+        rows_ref[...] = jnp.dot(marked[...], wbuf[block], preferred_element_type=F32)
     out_ref[...] = total.astype(BF16)
 
 
-def out_project(place, context, shards, come=None, picked=None, kept=None):
+def out_project(place, context, shards, base, come=None, picked=None, kept=None):
     half, depth = context.shape
     width = shards[0][0].shape[1]
     flat = [ref for shard in shards for ref in shard]
@@ -351,28 +381,28 @@
     if adding:
         operands = [place, context, come]
         in_specs = [SMEM_SPEC, whole]
-        in_specs += [pl.BlockSpec((None, half, width), lambda j: (j ^ 1, 0, 0))]
+        in_specs += [pl.BlockSpec((None, half, width), lambda j: (1 - j, 0, 0))]
     else:
         operands = [place, picked, context, kept]
         in_specs = [SMEM_SPEC, SMEM_SPEC, whole, whole]
     out_specs = [pl.BlockSpec((None, half, width), lambda j: (j, 0, 0))]
-    out_shape = [jax.ShapeDtypeStruct((4, half, width), BF16)]
-    scratch = [pltpu.VMEM((4, depth, width), BF16), pltpu.SemaphoreType.DMA((4, 2))]
+    out_shape = [jax.ShapeDtypeStruct((2, half, width), BF16)]
+    scratch = [pltpu.VMEM((2, depth, width), BF16), pltpu.SemaphoreType.DMA((2, 2))]
     if not adding:
-        out_specs.append(pl.BlockSpec((4, 8, width), lambda j: (0, 0, 0)))
-        out_shape.append(jax.ShapeDtypeStruct((4, 8, width), F32))
+        out_specs.append(pl.BlockSpec((None, 8, width), lambda j: (j, 0, 0)))
+        out_shape.append(jax.ShapeDtypeStruct((2, 8, width), F32))
         scratch.append(pltpu.VMEM((8, depth), BF16))
     return pl.pallas_call(
-        functools.partial(out_kernel, adding, [len(shard) for shard in shards]),
-        grid=(4,),
+        functools.partial(out_kernel, adding, base, [len(shard) for shard in shards]),
+        grid=(2,),
         in_specs=in_specs + [HBM_SPEC] * len(flat),
         out_specs=out_specs,
         out_shape=out_shape,
         scratch_shapes=scratch,
-        compiler_params=params("arbitrary"),
+        compiler_params=params("arbitrary", limit=VMEM_LIMIT),
         cost_estimate=pl.CostEstimate(
-            flops=8 * half * depth * width,
-            bytes_accessed=2 * (half * depth + 4 * (depth + (1 + adding) * half) * width),
+            flops=4 * half * depth * width,
+            bytes_accessed=2 * (half * depth + 2 * (depth + (1 + adding) * half) * width),
             transcendentals=0,
         ),
         name="out_project",
@@ -442,14 +472,19 @@
     ends = jnp.cumsum(lengths)
     keep_place = jnp.stack([part, core]).astype(jnp.int32)
     send_place = jnp.stack([part, 1 - core]).astype(jnp.int32)
-    out_place = jnp.stack([part] + [s ^ column for s in ring_order] + [core, column]).astype(jnp.int32)
+    out_place = jnp.stack([part] + [s ^ column for s in ring_order] + [core]).astype(jnp.int32)
 
     def swap_by(value, mask):
         return lax.ppermute(value, "fsdp", [(i, i ^ mask) for i in range(fsdp)])
 
-    one_hot = chosen.astype(BF16)
-    hidden_rows = jnp.einsum("sr,brw->bsw", one_hot, stack, preferred_element_type=F32)
-    hidden_rows = jnp.pad(hidden_rows, ((0, 0), (0, 8 - sequences), (0, 0)))
+    def by_offset(blocks):
+        return jnp.stack(
+            [
+                lax.dynamic_index_in_dim(blocks, column ^ r, 0, keepdims=False)
+                for r in range(fsdp)
+            ]
+        )
+
     extra = jnp.stack([local_ids, assignment], 1).astype(BF16)
     extra = jnp.pad(extra, ((0, 8 - sequences), (0, width - 2)))[None]
 
@@ -461,37 +496,52 @@
     mine = ring.half(w_query)
     ring.step(mine, 1)
     ring.step(mine, -1)
-    normed = norm_blocks(stack)
-    ring.step(ring.along[3], 1, before=[normed])
+    normed, hidden_rows = norm_blocks(column, picked, stack)
+    ring.step(ring.along[3], 1)
     key_rows = project(place, normed, [(w_key,), *ring.pieces(0)], None, turn)
     mine = ring.half(w_value)
-    ring.step(mine, 1, before=[key_rows])
-    ring.step(mine, -1)
+    ring.step(mine, 1, before=[normed])
+    ring.step(mine, -1, before=[key_rows])
     ring.step(ring.along[6], 1)
     queries = project(place, normed, [(w_query,), *ring.pieces(1)], HS ** (-0.5), turn)
     mine = ring.half(w_out)
-    ring.step(mine, 1, before=[queries])
+    ring.step(mine, 1)
     value_rows = project(place, normed, [(w_value,), *ring.pieces(2)])
-    ring.step(mine, -1, before_swap=[value_rows])
+    ring.step(mine, -1, before=[queries], before_swap=[value_rows])
     context_sent = attention(send_place, ends, queries, key_rows, value_rows)
     last_along = ring.ring(tie(ring.along[9], ring.along[9]), 1)
     last_other = ring.ring(tie(ring.across[-2], ring.along[10], context_sent), 1)
     out_in = [(w_out,), ring.shards[9], (last_along, last_other), ring.shards[10]]
     context_kept = attention(keep_place, ends, queries, key_rows, tie(value_rows, context_sent))
 
-    sent, row_sum = out_project(out_place, context_sent, out_in, None, picked, context_kept)
-    arrived = swap_by(sent, 1)
-
-    row_sum = row_sum + sum(swap_by(row_sum, mask) for mask in range(1, fsdp))
+    def send(base, *before):
+        return out_project(
+            out_place, tie(context_sent, *before), out_in, base, None, picked, context_kept
+        )
+
+    sent_far, rows_far = send(2)
+    arrived_far = swap_by(sent_far, 1)
+    sent_near, rows_near = send(0, sent_far)
+    arrived_near = swap_by(sent_near, 1)
+    (chip_far,) = out_project(
+        out_place, tie(context_kept, sent_near), out_in, 2, arrived_far
+    )
+    crossed = swap_by(chip_far, 2)
+    (chip_near,) = out_project(
+        out_place, tie(context_kept, chip_far), out_in, 0, arrived_near
+    )
+
+    own_sum = jnp.concatenate([rows_near, rows_far], 0)
+    row_sum = own_sum
+    for mask in range(1, fsdp):
+        come = swap_by(own_sum, mask)
+        row_sum = row_sum + jnp.stack([come[r ^ mask] for r in range(fsdp)])
     full_rows = (hidden_rows + row_sum).astype(BF16)
     packet = jnp.concatenate([full_rows, extra], 0)
-
-    (chip,) = out_project(out_place, tie(context_kept, packet), out_in, arrived)
-    crossed = swap_by(chip[2:], 2)
-
     packets = [packet] + [ring.ring(packet, shift) for shift in range(1, dp)]
-    packets = jnp.stack(packets)[:, :, :sequences]
-    all_rows = packets[:, :dp].transpose(0, 2, 1, 3).reshape(dp * sequences, dp * width)
+    packets = tie(jnp.stack(packets), crossed)[:, :, :sequences]
+    all_rows = by_offset(packets[:, :dp].transpose(1, 0, 2, 3).reshape(dp, dp * sequences, width))
+    all_rows = all_rows.transpose(1, 0, 2).reshape(dp * sequences, dp * width)
     all_ids = packets[:, dp, :, 0].reshape(-1).astype(jnp.int32)
     all_owner = packets[:, dp, :, 1].reshape(-1).astype(jnp.int32)
     owned = group * sequences + jnp.arange(sequences, dtype=jnp.int32)
@@ -504,7 +554,7 @@
 
     def block_rows(index, place_in_chip):
         before = lax.dynamic_slice(stack, (index, core * half, 0), (1, half, width))[0]
-        summed = chip[place_in_chip].astype(F32) + crossed[place_in_chip].astype(F32)
+        summed = chip_near[place_in_chip].astype(F32) + crossed[place_in_chip].astype(F32)
         return (before.astype(F32) + summed).astype(BF16)
 
     other_rows = swap_by(block_rows(column ^ 1, 1), 1)

time: 225 us -> 211 us (0.938)
  starting transfers between devices: 49.4 us -> 41.4 us
  waiting for transfers between devices: 72.4 us -> 66.5 us
  Pallas kernels: 63.9 us -> 68.7 us
  matrix products: 3.69 us -> 0.66 us
  local copies, waits for them, and re-layouts: 10.3 us -> 7.71 us
    ppermute x6 -> x7, waiting for transfers between devices: 26.8 us -> 11.8 us  [swap_by(): return lax.ppermute(value, 'fsdp', [(i, i ^ mask) for i in range(fsdp)])]
    ppermute x16, starting transfers between devices: 33.7 us -> 22.8 us  [ring(): lax.ppermute(value, 'dp', [(i, (i + step) % self.dp) for i in range(self....]
    ppermute x16, waiting for transfers between devices: 44.9 us -> 53.9 us  [ring(): lax.ppermute(value, 'dp', [(i, (i + step) % self.dp) for i in range(self....]
    pallas_call x3 -> x5, Pallas kernels: 19.6 us -> 26 us  [the longest x4 19.6 us: out_project(): pl.pallas_call(functools.partial(out_kernel, adding, base, [len(shard) fo...]
    dot_general x1 -> x0, matrix products: 3.03 us -> none  [per_device(): jnp.einsum('sr,brw->bsw', one_hot, stack, preferred_element_type=F32)]
    ppermute x11, starting transfers between devices: 12.2 us -> 15 us  [step(): lax.ppermute(tie(self.along[i], *waits, *before_swap), 'parts', [(0, 1),...]
    slice x1 -> x3, local copies, waits for them, and re-layouts: 2.51 us -> 0.02 us  [per_device(): row_sum = row_sum + jnp.stack([come[r ^ mask] for r in range(fsdp)])]
    unnamed x72 -> x65, local copies, waits for them, and re-layouts: 6.05 us -> 5.72 us
  transfers between devices with their start and end apart: 34 -> 35, of which waited for: 11 -> 11; matrix products, arithmetic and copies ran while one was open for 7% -> 5% of each run, Pallas kernels for 26% -> 30%
where the time goes in v3:
time: 211 us; the launch traced here: 210 us
  Pallas kernels  68.7 us (33%)
  waiting for transfers between devices  66.5 us (32%)
  starting transfers between devices  41.4 us (20%)
  between operations  14.5 us (7%)
  other arithmetic  10.4 us (5%)
  local copies, waits for them, and re-layouts  7.71 us (4%)
    ppermute x16, waiting for transfers between devices, ring(): lax.ppermute(value, 'dp', [(i, (i + step) % self.dp) for i in range(self....  53.9 us
    pallas_call x3, Pallas kernels, project(): pl.pallas_call(functools.partial(project_kernel, scale, bool(turn), [len(...  26.5 us
    ppermute x16, starting transfers between devices, ring(): lax.ppermute(value, 'dp', [(i, (i + step) % self.dp) for i in range(self....  22.8 us
    pallas_call x4, Pallas kernels, out_project(): pl.pallas_call(functools.partial(out_kernel, adding, base, [len(shard) fo...  19.6 us
    pallas_call x2, Pallas kernels, attention(): pl.pallas_call(functools.partial(attend_kernel, row_block=row_block), gri...  16.2 us
    ppermute x11, starting transfers between devices, step(): lax.ppermute(tie(self.along[i], *waits, *before_swap), 'parts', [(0, 1),...  15 us
    ppermute x7, waiting for transfers between devices, swap_by(): return lax.ppermute(value, 'fsdp', [(i, i ^ mask) for i in range(fsdp)])  11.8 us
    pallas_call x1, Pallas kernels, norm_blocks(): pl.pallas_call(norm_kernel, grid=(rows // row_block,), in_specs=[SMEM_SPE...  6.44 us
  transfers between devices with their start and end apart: 35, of which 11 were waited for; matrix products, arithmetic and copies ran while one was open for 5% of the time, Pallas kernels for 30%

profile of v3, /device:TPU:0, one launch (start us, length us, event | category | flops | bytes accessed | tf_op | source)
XLA Modules:
  0.0 209.9 jit_solution(5960354047473889910)
XLA Ops:
  8.4 3.1 %collective-permute-start.6 = (bf16[320,640]{1,0:T(8,128)(2,1)S(1)}, bf16[320,640]{1,0:T(8,128)(2,1)}, u32[]{:S(2)}, u32[]{:S(2)}) collective-permute-start(bf16[320,640]{1,0:T(8,128)(2,1)S(1)} %constant_dynamic-slice_fusion.6), channel_id=1, source_target_pairs={{0,4},{4,8},{8,12},{12,0},{1,5},{5,9},{9,13},{13,1},{2,6},{6,10},{... | collective-permute-start | bytes 1228808 | tf_op jit(solution)/shard_map/ppermute | solution.py:423
  11.5 2.1 collective-permute-start
  14.4 9.6 %collective-permute-done.6.refs_1_ = bf16[320,640]{1,0:T(8,128)(2,1)} collective-permute-done((bf16[320,640]{1,0:T(8,128)(2,1)S(1)}, bf16[320,640]{1,0:T(8,128)(2,1)}, u32[]{:S(2)}, u32[]{:S(2)}) %collective-permute-start.6) | collective-permute-done | bytes 409632 | tf_op jit(solution)/shard_map/ppermute | solution.py:423
  24.0 1.8 collective-permute-start.9
  25.8 5.7 %collective-permute-done.refs_5_ = bf16[320,640]{1,0:T(8,128)(2,1)} collective-permute-done((bf16[320,640]{1,0:T(8,128)(2,1)S(1)}, bf16[320,640]{1,0:T(8,128)(2,1)}, u32[]{:S(2)}, u32[]{:S(2)}) %collective-permute-start) | collective-permute-done | bytes 409632 | tf_op jit(solution)/shard_map/ppermute | solution.py:423
  31.5 2.2 %collective-permute-start.1 = (bf16[320,640]{1,0:T(8,128)(2,1)S(1)}, bf16[320,640]{1,0:T(8,128)(2,1)S(1)}, u32[]{:S(2)}, u32[]{:S(2)}) collective-permute-start(bf16[320,640]{1,0:T(8,128)(2,1)S(1)} %constant_dynamic-slice_fusion.7), channel_id=1, source_target_pairs={{0,4},{4,8},{8,12},{12,0},{1,5},{5,9},{9,13},{13,1},{2,6},{6,10},{... | collective-permute-start | bytes 1228808 | tf_op jit(solution)/shard_map/ppermute | solution.py:423
  33.7 1.3 collective-permute-start.2
  35.1 8.4 %collective-permute-done.7.refs_3_ = bf16[320,640]{1,0:T(8,128)(2,1)} collective-permute-done((bf16[320,640]{1,0:T(8,128)(2,1)}, bf16[320,640]{1,0:T(8,128)(2,1)}, u32[]{:S(2)}, u32[]{:S(2)}) %collective-permute-start.7) | collective-permute-done | bytes 409632 | tf_op jit(solution)/shard_map/ppermute | solution.py:423
  43.5 1.9 collective-permute-start.8
  45.4 1.5 collective-permute-start.10
  46.9 5.1 %collective-permute-done.1.refs_1_ = bf16[320,640]{1,0:T(8,128)(2,1)S(1)} collective-permute-done((bf16[320,640]{1,0:T(8,128)(2,1)S(1)}, bf16[320,640]{1,0:T(8,128)(2,1)S(1)}, u32[]{:S(2)}, u32[]{:S(2)}) %collective-permute-start.1) | collective-permute-done | bytes 409632 | tf_op jit(solution)/shard_map/ppermute | solution.py:423
  52.1 1.6 collective-permute-start.3
  53.6 1.0 collective-permute-start.4
  54.7 1.7 fusion.2
  56.3 4.4 %collective-permute-done.8.refs_5_ = bf16[320,640]{1,0:T(8,128)(2,1)S(1)} collective-permute-done((bf16[320,640]{1,0:T(8,128)(2,1)S(1)}, bf16[320,640]{1,0:T(8,128)(2,1)S(1)}, u32[]{:S(2)}, u32[]{:S(2)}) %collective-permute-start.8) | collective-permute-done | bytes 409632 | tf_op jit(solution)/shard_map/ppermute | solution.py:423
  60.7 1.5 collective-permute-start.11
  62.3 6.4 %norm_rows.1 = (bf16[896,2560]{1,0:T(8,128)(2,1)}, f32[4,8,640]{2,1,0:T(8,128)}) custom-call(s32[1]{0:T(128)} %bitcast.13.column_ref, s32[3]{0:T(128)} %get-tuple-element.69.picked_ref.refs_0_, bf16[4,896,640]{2,1,0:T(8,128)(2,1)} %bitcast.42), custom_call_target="tpu_custom_call" | custom-call | flops 18350080 | bytes 9175040 | tf_op jit(solution)/shard_map/norm_rows/pallas_call | solution.py:163
  68.7 1.3 collective-permute-start.12
  70.0 1.2 pad_maximum_fusion
  72.6 9.0 %project.4.k_ref = bf16[896,640]{1,0:T(8,128)(2,1)} custom-call(s32[5]{0:T(128)} %stack.105.place_ref, bf16[896,2560]{1,0:T(8,128)(2,1)} %get-tuple-element.34.x_ref, bf16[640,640]{1,0:T(8,128)(2,1)} %refs_0_.4, bf16[320,640]{1,0:T(8,128)(2,1)} %collective-permute-done.6.refs_1_, bf16[320,640]{1,0:T(8,128)(2,1)} %copy-done.24, ...), custom_call_target="tpu_custom_call" | custom-call | flops 2936012800 | bytes 9011200 | tf_op jit(solution)/shard_map/project/pallas_call | solution.py:243
  81.6 2.5 %collective-permute-start.16 = (bf16[320,640]{1,0:T(8,128)(2,1)S(1)}, bf16[320,640]{1,0:T(8,128)(2,1)S(1)}, u32[]{:S(2)}, u32[]{:S(2)}) collective-permute-start(bf16[320,640]{1,0:T(8,128)(2,1)S(1)} %constant_dynamic-slice_fusion.5), channel_id=1, source_target_pairs={{0,12},{4,0},{8,4},{12,8},{1,13},{5,1},{9,5},{13,9},{2,14},{6,2},{... | collective-permute-start | bytes 1228808 | tf_op jit(solution)/shard_map/ppermute | solution.py:423
  84.1 1.6 collective-permute-start.13
  85.7 8.3 %collective-permute-done.16.refs_5_ = bf16[320,640]{1,0:T(8,128)(2,1)S(1)} collective-permute-done((bf16[320,640]{1,0:T(8,128)(2,1)S(1)}, bf16[320,640]{1,0:T(8,128)(2,1)S(1)}, u32[]{:S(2)}, u32[]{:S(2)}) %collective-permute-start.16) | collective-permute-done | bytes 409632 | tf_op jit(solution)/shard_map/ppermute | solution.py:423
  94.0 1.5 collective-permute-start.17
  95.7 8.4 %collective-permute-done.14.refs_3_ = bf16[320,640]{1,0:T(8,128)(2,1)} collective-permute-done((bf16[320,640]{1,0:T(8,128)(2,1)S(1)}, bf16[320,640]{1,0:T(8,128)(2,1)}, u32[]{:S(2)}, u32[]{:S(2)}) %collective-permute-start.14) | collective-permute-done | bytes 409632 | tf_op jit(solution)/shard_map/ppermute | solution.py:423
  104.9 9.0 %project.3.q_ref = bf16[896,640]{1,0:T(8,128)(2,1)} custom-call(s32[5]{0:T(128)} %stack.105.place_ref, bf16[896,2560]{1,0:T(8,128)(2,1)} %get-tuple-element.34.x_ref, bf16[640,640]{1,0:T(8,128)(2,1)} %refs_0_.3, bf16[320,640]{1,0:T(8,128)(2,1)} %copy-done.21, bf16[320,640]{1,0:T(8,128)(2,1)} %collective-permute-done.3.refs_2_, ...), custom_call_target="tpu_custom_call" | custom-call | flops 2936012800 | bytes 9011200 | tf_op jit(solution)/shard_map/project/pallas_call | solution.py:243
  114.7 1.2 collective-permute-start.19
  115.9 1.3 collective-permute-start.21
  118.6 8.5 %project.5.v_ref = bf16[896,640]{1,0:T(8,128)(2,1)} custom-call(s32[5]{0:T(128)} %stack.105.place_ref, bf16[896,2560]{1,0:T(8,128)(2,1)} %get-tuple-element.34.x_ref, bf16[640,640]{1,0:T(8,128)(2,1)} %refs_0_.5, bf16[320,640]{1,0:T(8,128)(2,1)} %copy-done.23, bf16[320,640]{1,0:T(8,128)(2,1)} %copy-done.27, bf16[320,640]{1,0:T(8,128)(2,1)} %collective-permute-done.14.refs_3_, ...), custom_call_target="tpu_custom_call" | custom-call | flops 2936012800 | bytes 9011200 | tf_op jit(solution)/shard_map/project/pallas_call | solution.py:243
  127.1 8.1 %attention.2.refs_1_ = bf16[448,640]{1,0:T(8,128)(2,1)} custom-call(s32[2]{0:T(128)} %pad_add_fusion.1.place_ref, s32[3]{0:T(128)} %bitcast.51, bf16[896,640]{1,0:T(8,128)(2,1)} %project.3.q_ref, bf16[896,640]{1,0:T(8,128)(2,1)} %project.4.k_ref, bf16[896,640]{1,0:T(8,128)(2,1)} %project.5.v_ref), custom_call_target="tpu_custom_call" | custom-call | flops 1027604480 | bytes 3440640 | tf_op jit(solution)/shard_map/attention/pallas_call | solution.py:297
  135.2 1.6 collective-permute-start.22
  136.8 1.5 collective-permute-start.23
  139.5 8.1 %attention.3.refs_2_.refs_0_ = bf16[448,640]{1,0:T(8,128)(2,1)} custom-call(s32[2]{0:T(128)} %pad_add_fusion.place_ref, s32[3]{0:T(128)} %bitcast.52, bf16[896,640]{1,0:T(8,128)(2,1)} %project.3.q_ref, bf16[896,640]{1,0:T(8,128)(2,1)} %project.4.k_ref, bf16[896,640]{1,0:T(8,128)(2,1)} %project.5.v_ref), custom_call_target="tpu_custom_call" | custom-call | flops 1027604480 | bytes 3440640 | tf_op jit(solution)/shard_map/attention/pallas_call | solution.py:297
  149.3 5.1 %out_project.4 = (bf16[2,448,640]{2,1,0:T(8,128)(2,1)}, f32[2,8,640]{2,1,0:T(8,128)}) custom-call(s32[6]{0:T(128)} %stack.99.place_ref, s32[3]{0:T(128)} %get-tuple-element.69.picked_ref.refs_0_, bf16[448,640]{1,0:T(8,128)(2,1)} %attention.2.refs_1_, bf16[448,640]{1,0:T(8,128)(2,1)} %attention.3.refs_2_.refs_0_, bf16[640,640]{1,0:T(8,128)(2,1)} %refs_2_.3, ...), custom_call_target="tpu_custom_call" | custom-call | flops 734003200 | bytes 3358720 | tf_op jit(solution)/shard_map/out_project/pallas_call | solution.py:395
  154.9 4.9 %out_project.5 = (bf16[2,448,640]{2,1,0:T(8,128)(2,1)}, f32[2,8,640]{2,1,0:T(8,128)}) custom-call(s32[6]{0:T(128)} %stack.99.place_ref, s32[3]{0:T(128)} %get-tuple-element.69.picked_ref.refs_0_, bf16[448,640]{1,0:T(8,128)(2,1)} %attention.2.refs_1_, bf16[448,640]{1,0:T(8,128)(2,1)} %attention.3.refs_2_.refs_0_, bf16[640,640]{1,0:T(8,128)(2,1)} %refs_2_.3, ...), custom_call_target="tpu_custom_call" | custom-call | flops 734003200 | bytes 3358720 | tf_op jit(solution)/shard_map/out_project/pallas_call | solution.py:395
  160.6 0.8 collective-permute-start.28
  161.5 1.2 collective-permute-start.29
  163.3 1.0 copy-done.9
  164.3 5.0 %out_project.6 = bf16[2,448,640]{2,1,0:T(8,128)(2,1)} custom-call(s32[6]{0:T(128)} %stack.99.place_ref, bf16[448,640]{1,0:T(8,128)(2,1)} %attention.3.refs_2_.refs_0_, bf16[2,448,640]{2,1,0:T(8,128)(2,1)} %copy-done.9, bf16[640,640]{1,0:T(8,128)(2,1)} %refs_2_.3, bf16[320,640]{1,0:T(8,128)(2,1)} %copy-done.2, bf16[320,640]{1,0:T(8,128)(2,1)} %copy-done.3, ...), custom_call_target="tpu_custom_call" | custom-call | flops 734003200 | bytes 4505600 | tf_op jit(solution)/shard_map/out_project/pallas_call | solution.py:395
  170.2 2.4 %collective-permute-start.33 = (bf16[5,8,640]{2,1,0:T(8,128)(2,1)S(1)}, bf16[5,8,640]{2,1,0:T(8,128)(2,1)S(1)}, u32[]{:S(2)}, u32[]{:S(2)}) collective-permute-start(bf16[5,8,640]{2,1,0:T(8,128)(2,1)S(1)} %get-tuple-element.88), channel_id=1, source_target_pairs={{0,12},{4,0},{8,4},{12,8},{1,13},{5,1},{9,5},{13,9},{2,14},{6,2},{... | collective-permute-start | bytes 153608 | tf_op jit(solution)/shard_map/ppermute | solution.py:423
  172.6 0.8 collective-permute-start.32
  173.4 1.9 collective-permute-start.31
  175.4 3.2 %collective-permute-done.32 = bf16[5,8,640]{2,1,0:T(8,128)(2,1)S(1)} collective-permute-done((bf16[5,8,640]{2,1,0:T(8,128)(2,1)S(1)}, bf16[5,8,640]{2,1,0:T(8,128)(2,1)S(1)}, u32[]{:S(2)}, u32[]{:S(2)}) %collective-permute-start.32) | collective-permute-done | bytes 51232 | tf_op jit(solution)/shard_map/ppermute | solution.py:423
  179.4 1.0 copy-done.8
  180.4 4.7 %out_project.7 = bf16[2,448,640]{2,1,0:T(8,128)(2,1)} custom-call(s32[6]{0:T(128)} %stack.99.place_ref, bf16[448,640]{1,0:T(8,128)(2,1)} %attention.3.refs_2_.refs_0_, bf16[2,448,640]{2,1,0:T(8,128)(2,1)} %copy-done.8, bf16[640,640]{1,0:T(8,128)(2,1)} %refs_2_.3, bf16[320,640]{1,0:T(8,128)(2,1)} %copy-done.2, bf16[320,640]{1,0:T(8,128)(2,1)} %copy-done.3, ...), custom_call_target="tpu_custom_call" | custom-call | flops 734003200 | bytes 4505600 | tf_op jit(solution)/shard_map/out_project/pallas_call | solution.py:395
  185.1 11.7 %collective-permute-done.26 = bf16[2,448,640]{2,1,0:T(8,128)(2,1)S(1)} collective-permute-done((bf16[2,448,640]{2,1,0:T(8,128)(2,1)}, bf16[2,448,640]{2,1,0:T(8,128)(2,1)S(1)}, u32[]{:S(2)}, u32[]{:S(2)}) %collective-permute-start.26) | collective-permute-done | bytes 1146912 | tf_op jit(solution)/shard_map/ppermute | solution.py:478
  197.1 2.0 fusion
  201.6 1.5 maximum_select_fusion
  (145 shorter events, 15.9 us)
Async XLA Ops:
  7.2 193.1 %copy-start = (bf16[33,2560]{1,0:T(8,128)(2,1)S(1)}, bf16[33,2560]{1,0:T(8,128)(2,1)}, u32[]{:S(2)}) copy-start(bf16[33,2560]{1,0:T(8,128)(2,1)} %param.19) | copy-start | bytes 506884
  7.2 18.5 %copy-start.11 = (bf16[640,640]{1,0:T(8,128)(2,1)S(1)}, bf16[640,640]{1,0:T(8,128)(2,1)}, u32[]{:S(2)}) copy-start(bf16[640,640]{1,0:T(8,128)(2,1)} %refs_0_.3) | copy-start | bytes 2457604
  7.2 39.7 %copy-start.12 = (bf16[640,640]{1,0:T(8,128)(2,1)S(1)}, bf16[640,640]{1,0:T(8,128)(2,1)}, u32[]{:S(2)}) copy-start(bf16[640,640]{1,0:T(8,128)(2,1)} %refs_0_.5) | copy-start | bytes 2457604
  7.2 55.0 %all-gather.3.cloned.1.call-start = ((), (), s32[]{:S(2)}) async-start(), calls=%async_computation | async-start | bytes 5734400 | tf_op jit(solution)/shard_map/all_gather | solution.py:461
  8.4 15.6 %collective-permute-start.6 = (bf16[320,640]{1,0:T(8,128)(2,1)S(1)}, bf16[320,640]{1,0:T(8,128)(2,1)}, u32[]{:S(2)}, u32[]{:S(2)}) collective-permute-start(bf16[320,640]{1,0:T(8,128)(2,1)S(1)} %constant_dynamic-slice_fusion.6), channel_id=1, source_target_pairs={{0,4},{4,8},{8,12},{12,0},{1,5},{5,9},{9,13},{13,1},{2,6},{6,10},{... | collective-permute-start | bytes 1228808 | tf_op jit(solution)/shard_map/ppermute | solution.py:423
  11.5 20.0 %collective-permute-start = (bf16[320,640]{1,0:T(8,128)(2,1)S(1)}, bf16[320,640]{1,0:T(8,128)(2,1)}, u32[]{:S(2)}, u32[]{:S(2)}) collective-permute-start(bf16[320,640]{1,0:T(8,128)(2,1)S(1)} %constant_dynamic-slice_fusion.6), channel_id=1, source_target_pairs={{0,12},{4,0},{8,4},{12,8},{1,13},{5,1},{9,5},{13,9},{2,14},{6,2},{... | collective-permute-start | bytes 1228808 | tf_op jit(solution)/shard_map/ppermute | solution.py:423
  13.8 42.6 %copy-start.16 = (s32[3,1]{0,1:T(1,128)}, s32[3,1]{0,1:T(1,128)S(1)}, u32[]{:S(2)}) copy-start(s32[3,1]{0,1:T(1,128)S(1)} %reduce-window.8) | copy-start | bytes 40
  24.0 19.5 %collective-permute-start.7 = (bf16[320,640]{1,0:T(8,128)(2,1)}, bf16[320,640]{1,0:T(8,128)(2,1)}, u32[]{:S(2)}, u32[]{:S(2)}) collective-permute-start(bf16[320,640]{1,0:T(8,128)(2,1)} %collective-permute-done.6.refs_1_), channel_id=1, source_target_pairs={{0,4},{4,8},{8,12},{12,0},{1,5},{5,9},{9,13},{13,1},{2,6},{6,10},{... | collective-permute-start | bytes 1228808 | tf_op jit(solution)/shard_map/ppermute | solution.py:423
  24.0 21.4 %collective-permute-start.9 = (bf16[320,640]{1,0:T(8,128)(2,1)}, bf16[320,640]{1,0:T(8,128)(2,1)S(1)}, u32[]{:S(2)}, u32[]{:S(2)}) collective-permute-start(bf16[320,640]{1,0:T(8,128)(2,1)} %collective-permute-done.6.refs_1_), channel_id=1, source_target_pairs={{0,16},{16,0},{1,17},{17,1},{2,18},{18,2},{3,19},{19,3},{4,20},{20... | collective-permute-start | bytes 1228808 | tf_op jit(solution)/shard_map/ppermute | solution.py:435
  31.5 20.5 %collective-permute-start.1 = (bf16[320,640]{1,0:T(8,128)(2,1)S(1)}, bf16[320,640]{1,0:T(8,128)(2,1)S(1)}, u32[]{:S(2)}, u32[]{:S(2)}) collective-permute-start(bf16[320,640]{1,0:T(8,128)(2,1)S(1)} %constant_dynamic-slice_fusion.7), channel_id=1, source_target_pairs={{0,4},{4,8},{8,12},{12,0},{1,5},{5,9},{9,13},{13,1},{2,6},{6,10},{... | collective-permute-start | bytes 1228808 | tf_op jit(solution)/shard_map/ppermute | solution.py:423
  33.7 18.4 %collective-permute-start.2 = (bf16[320,640]{1,0:T(8,128)(2,1)}, bf16[320,640]{1,0:T(8,128)(2,1)S(1)}, u32[]{:S(2)}, u32[]{:S(2)}) collective-permute-start(bf16[320,640]{1,0:T(8,128)(2,1)} %collective-permute-done.refs_5_), channel_id=1, source_target_pairs={{0,16},{16,0},{1,17},{17,1},{2,18},{18,2},{3,19},{19,3},{4,20},{20... | collective-permute-start | bytes 1228808 | tf_op jit(solution)/shard_map/ppermute | solution.py:435
  43.5 17.3 %collective-permute-start.8 = (bf16[320,640]{1,0:T(8,128)(2,1)S(1)}, bf16[320,640]{1,0:T(8,128)(2,1)S(1)}, u32[]{:S(2)}, u32[]{:S(2)}) collective-permute-start(bf16[320,640]{1,0:T(8,128)(2,1)S(1)} %constant_dynamic-slice_fusion.7), channel_id=1, source_target_pairs={{0,12},{4,0},{8,4},{12,8},{1,13},{5,1},{9,5},{13,9},{2,14},{6,2},{... | collective-permute-start | bytes 1228808 | tf_op jit(solution)/shard_map/ppermute | solution.py:423
  45.4 15.4 %collective-permute-start.10 = (bf16[320,640]{1,0:T(8,128)(2,1)}, bf16[320,640]{1,0:T(8,128)(2,1)}, u32[]{:S(2)}, u32[]{:S(2)}) collective-permute-start(bf16[320,640]{1,0:T(8,128)(2,1)} %collective-permute-done.7.refs_3_), channel_id=1, source_target_pairs={{0,16},{16,0},{1,17},{17,1},{2,18},{18,2},{3,19},{19,3},{4,20},{20... | collective-permute-start | bytes 1228808 | tf_op jit(solution)/shard_map/ppermute | solution.py:435
  52.0 16.7 %copy-start.21 = (bf16[320,640]{1,0:T(8,128)(2,1)}, bf16[320,640]{1,0:T(8,128)(2,1)S(1)}, u32[]{:S(2)}) copy-start(bf16[320,640]{1,0:T(8,128)(2,1)S(1)} %collective-permute-done.1.refs_1_) | copy-start | bytes 1228804
  52.1 19.9 %collective-permute-start.3 = (bf16[320,640]{1,0:T(8,128)(2,1)S(1)}, bf16[320,640]{1,0:T(8,128)(2,1)}, u32[]{:S(2)}, u32[]{:S(2)}) collective-permute-start(bf16[320,640]{1,0:T(8,128)(2,1)S(1)} %collective-permute-done.1.refs_1_), channel_id=1, source_target_pairs={{0,16},{16,0},{1,17},{17,1},{2,18},{18,2},{3,19},{19,3},{4,20},{20... | collective-permute-start | bytes 1228808 | tf_op jit(solution)/shard_map/ppermute | solution.py:435
  53.6 18.3 %collective-permute-start.4 = (bf16[320,640]{1,0:T(8,128)(2,1)S(1)}, bf16[320,640]{1,0:T(8,128)(2,1)}, u32[]{:S(2)}, u32[]{:S(2)}) collective-permute-start(bf16[320,640]{1,0:T(8,128)(2,1)S(1)} %collective-permute-done.1.refs_1_), channel_id=1, source_target_pairs={{0,4},{4,8},{8,12},{12,0},{1,5},{5,9},{9,13},{13,1},{2,6},{6,10},{... | collective-permute-start | bytes 1228808 | tf_op jit(solution)/shard_map/ppermute | solution.py:423
  60.7 23.3 %collective-permute-start.11 = (bf16[320,640]{1,0:T(8,128)(2,1)S(1)}, bf16[320,640]{1,0:T(8,128)(2,1)}, u32[]{:S(2)}, u32[]{:S(2)}) collective-permute-start(bf16[320,640]{1,0:T(8,128)(2,1)S(1)} %collective-permute-done.8.refs_5_), channel_id=1, source_target_pairs={{0,16},{16,0},{1,17},{17,1},{2,18},{18,2},{3,19},{19,3},{4,20},{20... | collective-permute-start | bytes 1228808 | tf_op jit(solution)/shard_map/ppermute | solution.py:435
  68.7 15.4 %collective-permute-start.12 = (bf16[320,640]{1,0:T(8,128)(2,1)S(1)}, bf16[320,640]{1,0:T(8,128)(2,1)S(1)}, u32[]{:S(2)}, u32[]{:S(2)}) collective-permute-start(bf16[320,640]{1,0:T(8,128)(2,1)S(1)} %constant_dynamic-slice_fusion.5), channel_id=1, source_target_pairs={{0,4},{4,8},{8,12},{12,0},{1,5},{5,9},{9,13},{13,1},{2,6},{6,10},{... | collective-permute-start | bytes 1228808 | tf_op jit(solution)/shard_map/ppermute | solution.py:423
  71.9 13.8 %collective-permute-start.5 = (bf16[320,640]{1,0:T(8,128)(2,1)}, bf16[320,640]{1,0:T(8,128)(2,1)S(1)}, u32[]{:S(2)}, u32[]{:S(2)}) collective-permute-start(bf16[320,640]{1,0:T(8,128)(2,1)} %collective-permute-done.4.refs_3_), channel_id=1, source_target_pairs={{0,16},{16,0},{1,17},{17,1},{2,18},{18,2},{3,19},{19,3},{4,20},{20... | collective-permute-start | bytes 1228808 | tf_op jit(solution)/shard_map/ppermute | solution.py:435
  72.6 13.1 %copy-start.1 = (bf16[640,640]{1,0:T(8,128)(2,1)S(1)}, bf16[640,640]{1,0:T(8,128)(2,1)}, u32[]{:S(2)}) copy-start(bf16[640,640]{1,0:T(8,128)(2,1)} %refs_2_.3) | copy-start | bytes 2457604
  81.6 12.4 %collective-permute-start.16 = (bf16[320,640]{1,0:T(8,128)(2,1)S(1)}, bf16[320,640]{1,0:T(8,128)(2,1)S(1)}, u32[]{:S(2)}, u32[]{:S(2)}) collective-permute-start(bf16[320,640]{1,0:T(8,128)(2,1)S(1)} %constant_dynamic-slice_fusion.5), channel_id=1, source_target_pairs={{0,12},{4,0},{8,4},{12,8},{1,13},{5,1},{9,5},{13,9},{2,14},{6,2},{... | collective-permute-start | bytes 1228808 | tf_op jit(solution)/shard_map/ppermute | solution.py:423
  84.1 29.8 %copy-start.23 = (bf16[320,640]{1,0:T(8,128)(2,1)}, bf16[320,640]{1,0:T(8,128)(2,1)S(1)}, u32[]{:S(2)}) copy-start(bf16[320,640]{1,0:T(8,128)(2,1)S(1)} %collective-permute-done.12.refs_1_) | copy-start | bytes 1228804
  84.1 11.6 %collective-permute-start.13 = (bf16[320,640]{1,0:T(8,128)(2,1)S(1)}, bf16[320,640]{1,0:T(8,128)(2,1)S(1)}, u32[]{:S(2)}, u32[]{:S(2)}) collective-permute-start(bf16[320,640]{1,0:T(8,128)(2,1)S(1)} %collective-permute-done.12.refs_1_), channel_id=1, source_target_pairs={{0,16},{16,0},{1,17},{17,1},{2,18},{18,2},{3,19},{19,3},{4,20},{20... | collective-permute-start | bytes 1228808 | tf_op jit(solution)/shard_map/ppermute | solution.py:435
  85.7 18.4 %collective-permute-start.14 = (bf16[320,640]{1,0:T(8,128)(2,1)S(1)}, bf16[320,640]{1,0:T(8,128)(2,1)}, u32[]{:S(2)}, u32[]{:S(2)}) collective-permute-start(bf16[320,640]{1,0:T(8,128)(2,1)S(1)} %collective-permute-done.12.refs_1_), channel_id=1, source_target_pairs={{0,4},{4,8},{8,12},{12,0},{1,5},{5,9},{9,13},{13,1},{2,6},{6,10},{... | collective-permute-start | bytes 1228808 | tf_op jit(solution)/shard_map/ppermute | solution.py:423
  85.7 19.1 %copy-start.28 = (bf16[320,640]{1,0:T(8,128)(2,1)}, bf16[320,640]{1,0:T(8,128)(2,1)S(1)}, u32[]{:S(2)}) copy-start(bf16[320,640]{1,0:T(8,128)(2,1)S(1)} %collective-permute-done.5.refs_4_) | copy-start | bytes 1228804
  94.0 19.8 %copy-start.26 = (bf16[320,640]{1,0:T(8,128)(2,1)}, bf16[320,640]{1,0:T(8,128)(2,1)S(1)}, u32[]{:S(2)}) copy-start(bf16[320,640]{1,0:T(8,128)(2,1)S(1)} %collective-permute-done.16.refs_5_) | copy-start | bytes 1228804
  94.0 19.9 %collective-permute-start.17 = (bf16[320,640]{1,0:T(8,128)(2,1)S(1)}, bf16[320,640]{1,0:T(8,128)(2,1)S(1)}, u32[]{:S(2)}, u32[]{:S(2)}) collective-permute-start(bf16[320,640]{1,0:T(8,128)(2,1)S(1)} %collective-permute-done.16.refs_5_), channel_id=1, source_target_pairs={{0,16},{16,0},{1,17},{17,1},{2,18},{18,2},{3,19},{19,3},{4,20},{20... | collective-permute-start | bytes 1228808 | tf_op jit(solution)/shard_map/ppermute | solution.py:435
  95.5 19.1 %collective-permute-start.18 = (bf16[320,640]{1,0:T(8,128)(2,1)S(1)}, bf16[320,640]{1,0:T(8,128)(2,1)S(1)}, u32[]{:S(2)}, u32[]{:S(2)}) collective-permute-start(bf16[320,640]{1,0:T(8,128)(2,1)S(1)} %constant_dynamic-slice_fusion.4), channel_id=1, source_target_pairs={{0,4},{4,8},{8,12},{12,0},{1,5},{5,9},{9,13},{13,1},{2,6},{6,10},{... | collective-permute-start | bytes 1228808 | tf_op jit(solution)/shard_map/ppermute | solution.py:423
  95.7 18.2 %copy-start.27 = (bf16[320,640]{1,0:T(8,128)(2,1)}, bf16[320,640]{1,0:T(8,128)(2,1)S(1)}, u32[]{:S(2)}) copy-start(bf16[320,640]{1,0:T(8,128)(2,1)S(1)} %collective-permute-done.13.refs_2_) | copy-start | bytes 1228804
  104.1 14.5 %collective-permute-start.15 = (bf16[320,640]{1,0:T(8,128)(2,1)}, bf16[320,640]{1,0:T(8,128)(2,1)}, u32[]{:S(2)}, u32[]{:S(2)}) collective-permute-start(bf16[320,640]{1,0:T(8,128)(2,1)} %collective-permute-done.14.refs_3_), channel_id=1, source_target_pairs={{0,16},{16,0},{1,17},{17,1},{2,18},{18,2},{3,19},{19,3},{4,20},{20... | collective-permute-start | bytes 1228808 | tf_op jit(solution)/shard_map/ppermute | solution.py:435
  114.7 12.4 %copy-start.2 = (bf16[320,640]{1,0:T(8,128)(2,1)}, bf16[320,640]{1,0:T(8,128)(2,1)S(1)}, u32[]{:S(2)}) copy-start(bf16[320,640]{1,0:T(8,128)(2,1)S(1)} %collective-permute-done.18.refs_4_.refs_3_) | copy-start | bytes 1228804
  114.7 20.6 %collective-permute-start.19 = (bf16[320,640]{1,0:T(8,128)(2,1)S(1)}, bf16[320,640]{1,0:T(8,128)(2,1)S(1)}, u32[]{:S(2)}, u32[]{:S(2)}) collective-permute-start(bf16[320,640]{1,0:T(8,128)(2,1)S(1)} %collective-permute-done.18.refs_4_.refs_3_), channel_id=1, source_target_pairs={{0,16},{16,0},{1,17},{17,1},{2,18},{18,2},{3,19},{19,3},{4,20},{20... | collective-permute-start | bytes 1228808 | tf_op jit(solution)/shard_map/ppermute | solution.py:435
  115.9 19.3 %collective-permute-start.21 = (bf16[320,640]{1,0:T(8,128)(2,1)S(1)}, bf16[320,640]{1,0:T(8,128)(2,1)S(1)}, u32[]{:S(2)}, u32[]{:S(2)}) collective-permute-start(bf16[320,640]{1,0:T(8,128)(2,1)S(1)} %constant_dynamic-slice_fusion.4), channel_id=1, source_target_pairs={{0,12},{4,0},{8,4},{12,8},{1,13},{5,1},{9,5},{13,9},{2,14},{6,2},{... | collective-permute-start | bytes 1228808 | tf_op jit(solution)/shard_map/ppermute | solution.py:423
  117.8 29.8 %collective-permute-start.20 = (bf16[320,640]{1,0:T(8,128)(2,1)S(1)}, bf16[320,640]{1,0:T(8,128)(2,1)S(1)}, u32[]{:S(2)}, u32[]{:S(2)}) collective-permute-start(bf16[320,640]{1,0:T(8,128)(2,1)S(1)} %collective-permute-done.18.refs_4_.refs_3_), channel_id=1, source_target_pairs={{0,4},{4,8},{8,12},{12,0},{1,5},{5,9},{9,13},{13,1},{2,6},{6,10},{... | collective-permute-start | bytes 1228808 | tf_op jit(solution)/shard_map/ppermute | solution.py:423
  135.2 12.3 %copy-start.3 = (bf16[320,640]{1,0:T(8,128)(2,1)}, bf16[320,640]{1,0:T(8,128)(2,1)S(1)}, u32[]{:S(2)}) copy-start(bf16[320,640]{1,0:T(8,128)(2,1)S(1)} %collective-permute-done.19.refs_5_.refs_4_) | copy-start | bytes 1228804
  135.2 12.3 %copy-start.4 = (bf16[320,640]{1,0:T(8,128)(2,1)}, bf16[320,640]{1,0:T(8,128)(2,1)S(1)}, u32[]{:S(2)}) copy-start(bf16[320,640]{1,0:T(8,128)(2,1)S(1)} %collective-permute-done.21.refs_8_.refs_7_) | copy-start | bytes 1228804
  135.2 12.4 %collective-permute-start.22 = (bf16[320,640]{1,0:T(8,128)(2,1)S(1)}, bf16[320,640]{1,0:T(8,128)(2,1)S(1)}, u32[]{:S(2)}, u32[]{:S(2)}) collective-permute-start(bf16[320,640]{1,0:T(8,128)(2,1)S(1)} %collective-permute-done.19.refs_5_.refs_4_), channel_id=1, source_target_pairs={{0,4},{4,8},{8,12},{12,0},{1,5},{5,9},{9,13},{13,1},{2,6},{6,10},{... | collective-permute-start | bytes 1228808 | tf_op jit(solution)/shard_map/ppermute | solution.py:423
  136.8 10.8 %collective-permute-start.23 = (bf16[320,640]{1,0:T(8,128)(2,1)S(1)}, bf16[320,640]{1,0:T(8,128)(2,1)S(1)}, u32[]{:S(2)}, u32[]{:S(2)}) collective-permute-start(bf16[320,640]{1,0:T(8,128)(2,1)S(1)} %collective-permute-done.21.refs_8_.refs_7_), channel_id=1, source_target_pairs={{0,16},{16,0},{1,17},{17,1},{2,18},{18,2},{3,19},{19,3},{4,20},{20... | collective-permute-start | bytes 1228808 | tf_op jit(solution)/shard_map/ppermute | solution.py:435
  154.4 9.0 %collective-permute-start.24 = (bf16[2,448,640]{2,1,0:T(8,128)(2,1)}, bf16[2,448,640]{2,1,0:T(8,128)(2,1)S(1)}, u32[]{:S(2)}, u32[]{:S(2)}) collective-permute-start(bf16[2,448,640]{2,1,0:T(8,128)(2,1)} %get-tuple-element.56), channel_id=1, source_target_pairs={{0,1},{1,0},{2,3},{3,2},{4,5},{5,4},{6,7},{7,6},{8,9},{9,8},{10,11... | collective-permute-start | bytes 3440648 | tf_op jit(solution)/shard_map/ppermute | solution.py:478
  160.6 9.5 %collective-permute-start.28 = (f32[4,8,640]{2,1,0:T(8,128)S(1)}, f32[4,8,640]{2,1,0:T(8,128)S(1)}, u32[]{:S(2)}, u32[]{:S(2)}) collective-permute-start(f32[4,8,640]{2,1,0:T(8,128)S(1)} %constant_dynamic-update-slice_fusion), channel_id=1, source_target_pairs={{0,1},{1,0},{2,3},{3,2},{4,5},{5,4},{6,7},{7,6},{8,9},{9,8},{10,11... | collective-permute-start | bytes 245768 | tf_op jit(solution)/shard_map/ppermute | solution.py:478
  161.4 18.0 %collective-permute-start.25 = (bf16[2,448,640]{2,1,0:T(8,128)(2,1)}, bf16[2,448,640]{2,1,0:T(8,128)(2,1)S(1)}, u32[]{:S(2)}, u32[]{:S(2)}) collective-permute-start(bf16[2,448,640]{2,1,0:T(8,128)(2,1)} %get-tuple-element.58), channel_id=1, source_target_pairs={{0,1},{1,0},{2,3},{3,2},{4,5},{5,4},{6,7},{7,6},{8,9},{9,8},{10,11... | collective-permute-start | bytes 3440648 | tf_op jit(solution)/shard_map/ppermute | solution.py:478
  161.5 8.7 %collective-permute-start.29 = (f32[4,8,640]{2,1,0:T(8,128)S(1)}, f32[4,8,640]{2,1,0:T(8,128)S(1)}, u32[]{:S(2)}, u32[]{:S(2)}) collective-permute-start(f32[4,8,640]{2,1,0:T(8,128)S(1)} %constant_dynamic-update-slice_fusion), channel_id=1, source_target_pairs={{0,2},{1,3},{2,0},{3,1},{4,6},{5,7},{6,4},{7,5},{8,10},{9,11},{10,... | collective-permute-start | bytes 245768 | tf_op jit(solution)/shard_map/ppermute | solution.py:478
  162.7 7.4 %collective-permute-start.30 = (f32[4,8,640]{2,1,0:T(8,128)S(1)}, f32[4,8,640]{2,1,0:T(8,128)S(1)}, u32[]{:S(2)}, u32[]{:S(2)}) collective-permute-start(f32[4,8,640]{2,1,0:T(8,128)S(1)} %constant_dynamic-update-slice_fusion), channel_id=1, source_target_pairs={{0,3},{1,2},{2,1},{3,0},{4,7},{5,6},{6,5},{7,4},{8,11},{9,10},{10,... | collective-permute-start | bytes 245768 | tf_op jit(solution)/shard_map/ppermute | solution.py:478
  169.3 27.5 %collective-permute-start.26 = (bf16[2,448,640]{2,1,0:T(8,128)(2,1)}, bf16[2,448,640]{2,1,0:T(8,128)(2,1)S(1)}, u32[]{:S(2)}, u32[]{:S(2)}) collective-permute-start(bf16[2,448,640]{2,1,0:T(8,128)(2,1)} %out_project.6), channel_id=1, source_target_pairs={{0,2},{1,3},{2,0},{3,1},{4,6},{5,7},{6,4},{7,5},{8,10},{9,11},{10,... | collective-permute-start | bytes 3440648 | tf_op jit(solution)/shard_map/ppermute | solution.py:478
  170.2 5.2 %collective-permute-start.33 = (bf16[5,8,640]{2,1,0:T(8,128)(2,1)S(1)}, bf16[5,8,640]{2,1,0:T(8,128)(2,1)S(1)}, u32[]{:S(2)}, u32[]{:S(2)}) collective-permute-start(bf16[5,8,640]{2,1,0:T(8,128)(2,1)S(1)} %get-tuple-element.88), channel_id=1, source_target_pairs={{0,12},{4,0},{8,4},{12,8},{1,13},{5,1},{9,5},{13,9},{2,14},{6,2},{... | collective-permute-start | bytes 153608 | tf_op jit(solution)/shard_map/ppermute | solution.py:423
  172.6 5.9 %collective-permute-start.32 = (bf16[5,8,640]{2,1,0:T(8,128)(2,1)S(1)}, bf16[5,8,640]{2,1,0:T(8,128)(2,1)S(1)}, u32[]{:S(2)}, u32[]{:S(2)}) collective-permute-start(bf16[5,8,640]{2,1,0:T(8,128)(2,1)S(1)} %get-tuple-element.88), channel_id=1, source_target_pairs={{0,8},{4,12},{8,0},{12,4},{1,9},{5,13},{9,1},{13,5},{2,10},{6,14},... | collective-permute-start | bytes 153608 | tf_op jit(solution)/shard_map/ppermute | solution.py:423
  173.4 5.9 %collective-permute-start.31 = (bf16[5,8,640]{2,1,0:T(8,128)(2,1)S(1)}, bf16[5,8,640]{2,1,0:T(8,128)(2,1)S(1)}, u32[]{:S(2)}, u32[]{:S(2)}) collective-permute-start(bf16[5,8,640]{2,1,0:T(8,128)(2,1)S(1)} %get-tuple-element.88), channel_id=1, source_target_pairs={{0,4},{4,8},{8,12},{12,0},{1,5},{5,9},{9,13},{13,1},{2,6},{6,10},{... | collective-permute-start | bytes 153608 | tf_op jit(solution)/shard_map/ppermute | solution.py:423
  199.1 2.5 %collective-permute-start.27 = (bf16[448,640]{1,0:T(8,128)(2,1)S(1)}, bf16[448,640]{1,0:T(8,128)(2,1)S(1)}, u32[]{:S(2)}, u32[]{:S(2)}) collective-permute-start(bf16[448,640]{1,0:T(8,128)(2,1)S(1)} %get-tuple-element.72), channel_id=1, source_target_pairs={{0,1},{1,0},{2,3},{3,2},{4,5},{5,4},{6,7},{7,6},{8,9},{9,8},{10,11... | collective-permute-start | bytes 1720328 | tf_op jit(solution)/shard_map/ppermute | solution.py:478
  (18 other events, 75.9 us)
Sparse Core Ops, SparseCore 0:
  9.6 39.3 all-gather.2

commit v4 on v3

--- a/solution.py
+++ b/solution.py
@@ -501,9 +501,9 @@
     key_rows = project(place, normed, [(w_key,), *ring.pieces(0)], None, turn)
     mine = ring.half(w_value)
     ring.step(mine, 1, before=[normed])
-    ring.step(mine, -1, before=[key_rows])
+    queries = project(place, normed, [(w_query,), *ring.pieces(1)], HS ** (-0.5), turn)
+    ring.step(mine, -1, before=[key_rows], before_swap=[queries])
     ring.step(ring.along[6], 1)
-    queries = project(place, normed, [(w_query,), *ring.pieces(1)], HS ** (-0.5), turn)
     mine = ring.half(w_out)
     ring.step(mine, 1)
     value_rows = project(place, normed, [(w_value,), *ring.pieces(2)])

time: 211 us -> 207 us (0.981)
  waiting for transfers between devices: 66.5 us -> 59.4 us
    ppermute x16, waiting for transfers between devices: 53.9 us -> 43.7 us  [ring(): lax.ppermute(value, 'dp', [(i, (i + step) % self.dp) for i in range(self....]
    ppermute x11, waiting for transfers between devices: 0.19 us -> 4.59 us  [step(): lax.ppermute(tie(self.along[i], *waits, *before_swap), 'parts', [(0, 1),...]
    unnamed x65 -> x69, local copies, waits for them, and re-layouts: 5.72 us -> 7.21 us
  transfers between devices with their start and end apart: 35 -> 35, of which waited for: 11 -> 12; matrix products, arithmetic and copies ran while one was open for 5% -> 5% of each run, Pallas kernels for 30% -> 31%
where the time goes in v4:
time: 207 us; the launch traced here: 206 us
  Pallas kernels  68.7 us (33%)
  waiting for transfers between devices  59.4 us (29%)
  starting transfers between devices  43.5 us (21%)
  between operations  14.6 us (7%)
  other arithmetic  10.3 us (5%)
  local copies, waits for them, and re-layouts  9.15 us (4%)
    ppermute x16, waiting for transfers between devices, ring(): lax.ppermute(value, 'dp', [(i, (i + step) % self.dp) for i in range(self....  43.7 us
    pallas_call x3, Pallas kernels, project(): pl.pallas_call(functools.partial(project_kernel, scale, bool(turn), [len(...  26.5 us
    ppermute x16, starting transfers between devices, ring(): lax.ppermute(value, 'dp', [(i, (i + step) % self.dp) for i in range(self....  23.7 us
    pallas_call x4, Pallas kernels, out_project(): pl.pallas_call(functools.partial(out_kernel, adding, base, [len(shard) fo...  19.6 us
    pallas_call x2, Pallas kernels, attention(): pl.pallas_call(functools.partial(attend_kernel, row_block=row_block), gri...  16.2 us
    ppermute x11, starting transfers between devices, step(): lax.ppermute(tie(self.along[i], *waits, *before_swap), 'parts', [(0, 1),...  16.1 us
    ppermute x7, waiting for transfers between devices, swap_by(): return lax.ppermute(value, 'fsdp', [(i, i ^ mask) for i in range(fsdp)])  10.4 us
    unnamed x69, local copies, waits for them, and re-layouts  7.21 us
  transfers between devices with their start and end apart: 35, of which 12 were waited for; matrix products, arithmetic and copies ran while one was open for 5% of the time, Pallas kernels for 31%

profile of v4, /device:TPU:0, one launch (start us, length us, event | category | flops | bytes accessed | tf_op | source)
XLA Modules:
  0.0 206.3 jit_solution(12326951194654551370)
XLA Ops:
  8.4 3.1 %collective-permute-start.6 = (bf16[320,640]{1,0:T(8,128)(2,1)S(1)}, bf16[320,640]{1,0:T(8,128)(2,1)S(1)}, u32[]{:S(2)}, u32[]{:S(2)}) collective-permute-start(bf16[320,640]{1,0:T(8,128)(2,1)S(1)} %constant_dynamic-slice_fusion.6), channel_id=1, source_target_pairs={{0,4},{4,8},{8,12},{12,0},{1,5},{5,9},{9,13},{13,1},{2,6},{6,10},{... | collective-permute-start | bytes 1228808 | tf_op jit(solution)/shard_map/ppermute | solution.py:423
  11.5 2.1 %collective-permute-start = (bf16[320,640]{1,0:T(8,128)(2,1)S(1)}, bf16[320,640]{1,0:T(8,128)(2,1)}, u32[]{:S(2)}, u32[]{:S(2)}) collective-permute-start(bf16[320,640]{1,0:T(8,128)(2,1)S(1)} %constant_dynamic-slice_fusion.6), channel_id=1, source_target_pairs={{0,12},{4,0},{8,4},{12,8},{1,13},{5,1},{9,5},{13,9},{2,14},{6,2},{... | collective-permute-start | bytes 1228808 | tf_op jit(solution)/shard_map/ppermute | solution.py:423
  14.3 9.5 %collective-permute-done.6.refs_1_ = bf16[320,640]{1,0:T(8,128)(2,1)S(1)} collective-permute-done((bf16[320,640]{1,0:T(8,128)(2,1)S(1)}, bf16[320,640]{1,0:T(8,128)(2,1)S(1)}, u32[]{:S(2)}, u32[]{:S(2)}) %collective-permute-start.6) | collective-permute-done | bytes 409632 | tf_op jit(solution)/shard_map/ppermute | solution.py:423
  23.9 1.8 collective-permute-start.9
  25.7 5.8 %collective-permute-done.refs_5_ = bf16[320,640]{1,0:T(8,128)(2,1)} collective-permute-done((bf16[320,640]{1,0:T(8,128)(2,1)S(1)}, bf16[320,640]{1,0:T(8,128)(2,1)}, u32[]{:S(2)}, u32[]{:S(2)}) %collective-permute-start) | collective-permute-done | bytes 409632 | tf_op jit(solution)/shard_map/ppermute | solution.py:423
  31.5 2.1 %collective-permute-start.1 = (bf16[320,640]{1,0:T(8,128)(2,1)S(1)}, bf16[320,640]{1,0:T(8,128)(2,1)S(1)}, u32[]{:S(2)}, u32[]{:S(2)}) collective-permute-start(bf16[320,640]{1,0:T(8,128)(2,1)S(1)} %constant_dynamic-slice_fusion.7), channel_id=1, source_target_pairs={{0,4},{4,8},{8,12},{12,0},{1,5},{5,9},{9,13},{13,1},{2,6},{6,10},{... | collective-permute-start | bytes 1228808 | tf_op jit(solution)/shard_map/ppermute | solution.py:423
  33.6 1.4 collective-permute-start.2
  35.1 8.1 %collective-permute-done.7.refs_3_ = bf16[320,640]{1,0:T(8,128)(2,1)} collective-permute-done((bf16[320,640]{1,0:T(8,128)(2,1)S(1)}, bf16[320,640]{1,0:T(8,128)(2,1)}, u32[]{:S(2)}, u32[]{:S(2)}) %collective-permute-start.7) | collective-permute-done | bytes 409632 | tf_op jit(solution)/shard_map/ppermute | solution.py:423
  43.2 1.9 collective-permute-start.8
  45.0 1.5 collective-permute-start.10
  46.6 5.1 %collective-permute-done.1.refs_1_ = bf16[320,640]{1,0:T(8,128)(2,1)S(1)} collective-permute-done((bf16[320,640]{1,0:T(8,128)(2,1)S(1)}, bf16[320,640]{1,0:T(8,128)(2,1)S(1)}, u32[]{:S(2)}, u32[]{:S(2)}) %collective-permute-start.1) | collective-permute-done | bytes 409632 | tf_op jit(solution)/shard_map/ppermute | solution.py:423
  51.7 1.6 collective-permute-start.3
  54.6 1.7 fusion.2
  56.3 4.2 %collective-permute-done.8.refs_5_ = bf16[320,640]{1,0:T(8,128)(2,1)} collective-permute-done((bf16[320,640]{1,0:T(8,128)(2,1)S(1)}, bf16[320,640]{1,0:T(8,128)(2,1)}, u32[]{:S(2)}, u32[]{:S(2)}) %collective-permute-start.8) | collective-permute-done | bytes 409632 | tf_op jit(solution)/shard_map/ppermute | solution.py:423
  60.5 1.5 collective-permute-start.11
  62.1 6.4 %norm_rows.1 = (bf16[896,2560]{1,0:T(8,128)(2,1)}, f32[4,8,640]{2,1,0:T(8,128)}) custom-call(s32[1]{0:T(128)} %bitcast.13.column_ref, s32[3]{0:T(128)} %get-tuple-element.69.picked_ref.refs_0_, bf16[4,896,640]{2,1,0:T(8,128)(2,1)} %bitcast.42), custom_call_target="tpu_custom_call" | custom-call | flops 18350080 | bytes 9175040 | tf_op jit(solution)/shard_map/norm_rows/pallas_call | solution.py:163
  69.3 1.2 pad_maximum_fusion
  70.5 1.8 collective-permute-start.5
  72.3 9.0 %project.4.k_ref = bf16[896,640]{1,0:T(8,128)(2,1)} custom-call(s32[5]{0:T(128)} %stack.105.place_ref, bf16[896,2560]{1,0:T(8,128)(2,1)} %get-tuple-element.34.x_ref, bf16[640,640]{1,0:T(8,128)(2,1)} %refs_0_.4, bf16[320,640]{1,0:T(8,128)(2,1)} %copy-done.22, bf16[320,640]{1,0:T(8,128)(2,1)} %copy-done.23, bf16[320,640]{1,0:T(8,128)(2,1)} %collective-permute-done.7.refs_3_, ...), custom_call_target="tpu_custom_call" | custom-call | flops 2936012800 | bytes 9011200 | tf_op jit(solution)/shard_map/project/pallas_call | solution.py:243
  81.3 1.8 collective-permute-start.16
  83.1 1.6 collective-permute-start.13
  85.6 9.0 %project.3.q_ref = bf16[896,640]{1,0:T(8,128)(2,1)} custom-call(s32[5]{0:T(128)} %stack.105.place_ref, bf16[896,2560]{1,0:T(8,128)(2,1)} %get-tuple-element.34.x_ref, bf16[640,640]{1,0:T(8,128)(2,1)} %refs_0_.3, bf16[320,640]{1,0:T(8,128)(2,1)} %copy-done.21, bf16[320,640]{1,0:T(8,128)(2,1)} %collective-permute-done.3.refs_2_, ...), custom_call_target="tpu_custom_call" | custom-call | flops 2936012800 | bytes 9011200 | tf_op jit(solution)/shard_map/project/pallas_call | solution.py:243
  94.5 0.9 collective-permute-start.17
  95.5 2.0 collective-permute-start.18
  97.5 5.5 %collective-permute-done.14.refs_3_ = bf16[320,640]{1,0:T(8,128)(2,1)} collective-permute-done((bf16[320,640]{1,0:T(8,128)(2,1)S(1)}, bf16[320,640]{1,0:T(8,128)(2,1)}, u32[]{:S(2)}, u32[]{:S(2)}) %collective-permute-start.14) | collective-permute-done | bytes 409632 | tf_op jit(solution)/shard_map/ppermute | solution.py:423
  102.9 1.4 collective-permute-start.15
  104.3 2.7 %collective-permute-done.17.refs_6_ = bf16[320,640]{1,0:T(8,128)(2,1)S(1)} collective-permute-done((bf16[320,640]{1,0:T(8,128)(2,1)S(1)}, bf16[320,640]{1,0:T(8,128)(2,1)S(1)}, u32[]{:S(2)}, u32[]{:S(2)}) %collective-permute-start.17) | collective-permute-done | bytes 409632 | tf_op jit(solution)/shard_map/ppermute | solution.py:435
  107.8 1.5 collective-permute-done.18.refs_4_.refs_3_
  109.3 1.5 collective-permute-start.19
  110.8 2.5 %collective-permute-start.21 = (bf16[320,640]{1,0:T(8,128)(2,1)S(1)}, bf16[320,640]{1,0:T(8,128)(2,1)S(1)}, u32[]{:S(2)}, u32[]{:S(2)}) collective-permute-start(bf16[320,640]{1,0:T(8,128)(2,1)S(1)} %constant_dynamic-slice_fusion.4), channel_id=1, source_target_pairs={{0,12},{4,0},{8,4},{12,8},{1,13},{5,1},{9,5},{13,9},{2,14},{6,2},{... | collective-permute-start | bytes 1228808 | tf_op jit(solution)/shard_map/ppermute | solution.py:423
  113.9 1.9 collective-permute-done.15.refs_4_
  116.6 8.5 %project.5.v_ref = bf16[896,640]{1,0:T(8,128)(2,1)} custom-call(s32[5]{0:T(128)} %stack.105.place_ref, bf16[896,2560]{1,0:T(8,128)(2,1)} %get-tuple-element.34.x_ref, bf16[640,640]{1,0:T(8,128)(2,1)} %refs_0_.5, bf16[320,640]{1,0:T(8,128)(2,1)} %copy-done.25, bf16[320,640]{1,0:T(8,128)(2,1)} %copy-done.27, bf16[320,640]{1,0:T(8,128)(2,1)} %collective-permute-done.14.refs_3_, ...), custom_call_target="tpu_custom_call" | custom-call | flops 2936012800 | bytes 9011200 | tf_op jit(solution)/shard_map/project/pallas_call | solution.py:243
  125.1 8.1 %attention.2.refs_1_ = bf16[448,640]{1,0:T(8,128)(2,1)} custom-call(s32[2]{0:T(128)} %pad_add_fusion.1.place_ref, s32[3]{0:T(128)} %bitcast.51, bf16[896,640]{1,0:T(8,128)(2,1)} %project.3.q_ref, bf16[896,640]{1,0:T(8,128)(2,1)} %project.4.k_ref, bf16[896,640]{1,0:T(8,128)(2,1)} %project.5.v_ref), custom_call_target="tpu_custom_call" | custom-call | flops 1027604480 | bytes 3440640 | tf_op jit(solution)/shard_map/attention/pallas_call | solution.py:297
  133.5 1.2 collective-permute-start.23
  135.9 8.1 %attention.3.refs_2_.refs_0_ = bf16[448,640]{1,0:T(8,128)(2,1)} custom-call(s32[2]{0:T(128)} %pad_add_fusion.place_ref, s32[3]{0:T(128)} %bitcast.52, bf16[896,640]{1,0:T(8,128)(2,1)} %project.3.q_ref, bf16[896,640]{1,0:T(8,128)(2,1)} %project.4.k_ref, bf16[896,640]{1,0:T(8,128)(2,1)} %project.5.v_ref), custom_call_target="tpu_custom_call" | custom-call | flops 1027604480 | bytes 3440640 | tf_op jit(solution)/shard_map/attention/pallas_call | solution.py:297
  145.7 5.1 %out_project.4 = (bf16[2,448,640]{2,1,0:T(8,128)(2,1)}, f32[2,8,640]{2,1,0:T(8,128)}) custom-call(s32[6]{0:T(128)} %stack.99.place_ref, s32[3]{0:T(128)} %get-tuple-element.69.picked_ref.refs_0_, bf16[448,640]{1,0:T(8,128)(2,1)} %attention.2.refs_1_, bf16[448,640]{1,0:T(8,128)(2,1)} %attention.3.refs_2_.refs_0_, bf16[640,640]{1,0:T(8,128)(2,1)} %refs_2_.3, ...), custom_call_target="tpu_custom_call" | custom-call | flops 734003200 | bytes 3358720 | tf_op jit(solution)/shard_map/out_project/pallas_call | solution.py:395
  151.3 4.9 %out_project.5 = (bf16[2,448,640]{2,1,0:T(8,128)(2,1)}, f32[2,8,640]{2,1,0:T(8,128)}) custom-call(s32[6]{0:T(128)} %stack.99.place_ref, s32[3]{0:T(128)} %get-tuple-element.69.picked_ref.refs_0_, bf16[448,640]{1,0:T(8,128)(2,1)} %attention.2.refs_1_, bf16[448,640]{1,0:T(8,128)(2,1)} %attention.3.refs_2_.refs_0_, bf16[640,640]{1,0:T(8,128)(2,1)} %refs_2_.3, ...), custom_call_target="tpu_custom_call" | custom-call | flops 734003200 | bytes 3358720 | tf_op jit(solution)/shard_map/out_project/pallas_call | solution.py:395
  157.9 1.2 collective-permute-start.29
  159.7 1.0 copy-done.9
  160.7 5.0 %out_project.6 = bf16[2,448,640]{2,1,0:T(8,128)(2,1)} custom-call(s32[6]{0:T(128)} %stack.99.place_ref, bf16[448,640]{1,0:T(8,128)(2,1)} %attention.3.refs_2_.refs_0_, bf16[2,448,640]{2,1,0:T(8,128)(2,1)} %copy-done.9, bf16[640,640]{1,0:T(8,128)(2,1)} %refs_2_.3, bf16[320,640]{1,0:T(8,128)(2,1)} %copy-done.2, bf16[320,640]{1,0:T(8,128)(2,1)} %copy-done.3, ...), custom_call_target="tpu_custom_call" | custom-call | flops 734003200 | bytes 4505600 | tf_op jit(solution)/shard_map/out_project/pallas_call | solution.py:395
  166.6 4.3 %collective-permute-start.33 = (bf16[5,8,640]{2,1,0:T(8,128)(2,1)S(1)}, bf16[5,8,640]{2,1,0:T(8,128)(2,1)S(1)}, u32[]{:S(2)}, u32[]{:S(2)}) collective-permute-start(bf16[5,8,640]{2,1,0:T(8,128)(2,1)S(1)} %get-tuple-element.88), channel_id=1, source_target_pairs={{0,12},{4,0},{8,4},{12,8},{1,13},{5,1},{9,5},{13,9},{2,14},{6,2},{... | collective-permute-start | bytes 153608 | tf_op jit(solution)/shard_map/ppermute | solution.py:423
  171.2 1.9 collective-permute-start.31
  173.1 3.2 %collective-permute-done.32 = bf16[5,8,640]{2,1,0:T(8,128)(2,1)S(1)} collective-permute-done((bf16[5,8,640]{2,1,0:T(8,128)(2,1)S(1)}, bf16[5,8,640]{2,1,0:T(8,128)(2,1)S(1)}, u32[]{:S(2)}, u32[]{:S(2)}) %collective-permute-start.32) | collective-permute-done | bytes 51232 | tf_op jit(solution)/shard_map/ppermute | solution.py:423
  177.1 1.0 copy-done.8
  178.1 4.7 %out_project.7 = bf16[2,448,640]{2,1,0:T(8,128)(2,1)} custom-call(s32[6]{0:T(128)} %stack.99.place_ref, bf16[448,640]{1,0:T(8,128)(2,1)} %attention.3.refs_2_.refs_0_, bf16[2,448,640]{2,1,0:T(8,128)(2,1)} %copy-done.8, bf16[640,640]{1,0:T(8,128)(2,1)} %refs_2_.3, bf16[320,640]{1,0:T(8,128)(2,1)} %copy-done.2, bf16[320,640]{1,0:T(8,128)(2,1)} %copy-done.3, ...), custom_call_target="tpu_custom_call" | custom-call | flops 734003200 | bytes 4505600 | tf_op jit(solution)/shard_map/out_project/pallas_call | solution.py:395
  182.8 10.4 %collective-permute-done.26 = bf16[2,448,640]{2,1,0:T(8,128)(2,1)S(1)} collective-permute-done((bf16[2,448,640]{2,1,0:T(8,128)(2,1)}, bf16[2,448,640]{2,1,0:T(8,128)(2,1)S(1)}, u32[]{:S(2)}, u32[]{:S(2)}) %collective-permute-start.26) | collective-permute-done | bytes 1146912 | tf_op jit(solution)/shard_map/ppermute | solution.py:478
  193.5 2.0 fusion
  198.0 1.5 maximum_select_fusion
  (149 shorter events, 17.6 us)
Async XLA Ops:
  7.2 189.5 %copy-start = (bf16[33,2560]{1,0:T(8,128)(2,1)S(1)}, bf16[33,2560]{1,0:T(8,128)(2,1)}, u32[]{:S(2)}) copy-start(bf16[33,2560]{1,0:T(8,128)(2,1)} %param.19) | copy-start | bytes 506884
  7.2 18.4 %copy-start.11 = (bf16[640,640]{1,0:T(8,128)(2,1)S(1)}, bf16[640,640]{1,0:T(8,128)(2,1)}, u32[]{:S(2)}) copy-start(bf16[640,640]{1,0:T(8,128)(2,1)} %refs_0_.3) | copy-start | bytes 2457604
  7.2 39.3 %copy-start.12 = (bf16[640,640]{1,0:T(8,128)(2,1)S(1)}, bf16[640,640]{1,0:T(8,128)(2,1)}, u32[]{:S(2)}) copy-start(bf16[640,640]{1,0:T(8,128)(2,1)} %refs_0_.5) | copy-start | bytes 2457604
  7.2 54.8 %all-gather.3.cloned.1.call-start = ((), (), s32[]{:S(2)}) async-start(), calls=%async_computation | async-start | bytes 5734400 | tf_op jit(solution)/shard_map/all_gather | solution.py:461
  8.4 15.4 %collective-permute-start.6 = (bf16[320,640]{1,0:T(8,128)(2,1)S(1)}, bf16[320,640]{1,0:T(8,128)(2,1)S(1)}, u32[]{:S(2)}, u32[]{:S(2)}) collective-permute-start(bf16[320,640]{1,0:T(8,128)(2,1)S(1)} %constant_dynamic-slice_fusion.6), channel_id=1, source_target_pairs={{0,4},{4,8},{8,12},{12,0},{1,5},{5,9},{9,13},{13,1},{2,6},{6,10},{... | collective-permute-start | bytes 1228808 | tf_op jit(solution)/shard_map/ppermute | solution.py:423
  11.5 20.0 %collective-permute-start = (bf16[320,640]{1,0:T(8,128)(2,1)S(1)}, bf16[320,640]{1,0:T(8,128)(2,1)}, u32[]{:S(2)}, u32[]{:S(2)}) collective-permute-start(bf16[320,640]{1,0:T(8,128)(2,1)S(1)} %constant_dynamic-slice_fusion.6), channel_id=1, source_target_pairs={{0,12},{4,0},{8,4},{12,8},{1,13},{5,1},{9,5},{13,9},{2,14},{6,2},{... | collective-permute-start | bytes 1228808 | tf_op jit(solution)/shard_map/ppermute | solution.py:423
  13.8 42.6 %copy-start.16 = (s32[3,1]{0,1:T(1,128)}, s32[3,1]{0,1:T(1,128)S(1)}, u32[]{:S(2)}) copy-start(s32[3,1]{0,1:T(1,128)S(1)} %reduce-window.8) | copy-start | bytes 40
  23.8 32.5 %copy-start.22 = (bf16[320,640]{1,0:T(8,128)(2,1)}, bf16[320,640]{1,0:T(8,128)(2,1)S(1)}, u32[]{:S(2)}) copy-start(bf16[320,640]{1,0:T(8,128)(2,1)S(1)} %collective-permute-done.6.refs_1_) | copy-start | bytes 1228804
  23.8 19.3 %collective-permute-start.7 = (bf16[320,640]{1,0:T(8,128)(2,1)S(1)}, bf16[320,640]{1,0:T(8,128)(2,1)}, u32[]{:S(2)}, u32[]{:S(2)}) collective-permute-start(bf16[320,640]{1,0:T(8,128)(2,1)S(1)} %collective-permute-done.6.refs_1_), channel_id=1, source_target_pairs={{0,4},{4,8},{8,12},{12,0},{1,5},{5,9},{9,13},{13,1},{2,6},{6,10},{... | collective-permute-start | bytes 1228808 | tf_op jit(solution)/shard_map/ppermute | solution.py:423
  23.9 21.2 %collective-permute-start.9 = (bf16[320,640]{1,0:T(8,128)(2,1)S(1)}, bf16[320,640]{1,0:T(8,128)(2,1)S(1)}, u32[]{:S(2)}, u32[]{:S(2)}) collective-permute-start(bf16[320,640]{1,0:T(8,128)(2,1)S(1)} %collective-permute-done.6.refs_1_), channel_id=1, source_target_pairs={{0,16},{16,0},{1,17},{17,1},{2,18},{18,2},{3,19},{19,3},{4,20},{20... | collective-permute-start | bytes 1228808 | tf_op jit(solution)/shard_map/ppermute | solution.py:435
  31.5 20.2 %collective-permute-start.1 = (bf16[320,640]{1,0:T(8,128)(2,1)S(1)}, bf16[320,640]{1,0:T(8,128)(2,1)S(1)}, u32[]{:S(2)}, u32[]{:S(2)}) collective-permute-start(bf16[320,640]{1,0:T(8,128)(2,1)S(1)} %constant_dynamic-slice_fusion.7), channel_id=1, source_target_pairs={{0,4},{4,8},{8,12},{12,0},{1,5},{5,9},{9,13},{13,1},{2,6},{6,10},{... | collective-permute-start | bytes 1228808 | tf_op jit(solution)/shard_map/ppermute | solution.py:423
  33.6 18.1 %collective-permute-start.2 = (bf16[320,640]{1,0:T(8,128)(2,1)}, bf16[320,640]{1,0:T(8,128)(2,1)S(1)}, u32[]{:S(2)}, u32[]{:S(2)}) collective-permute-start(bf16[320,640]{1,0:T(8,128)(2,1)} %collective-permute-done.refs_5_), channel_id=1, source_target_pairs={{0,16},{16,0},{1,17},{17,1},{2,18},{18,2},{3,19},{19,3},{4,20},{20... | collective-permute-start | bytes 1228808 | tf_op jit(solution)/shard_map/ppermute | solution.py:435
  43.2 17.4 %collective-permute-start.8 = (bf16[320,640]{1,0:T(8,128)(2,1)S(1)}, bf16[320,640]{1,0:T(8,128)(2,1)}, u32[]{:S(2)}, u32[]{:S(2)}) collective-permute-start(bf16[320,640]{1,0:T(8,128)(2,1)S(1)} %constant_dynamic-slice_fusion.7), channel_id=1, source_target_pairs={{0,12},{4,0},{8,4},{12,8},{1,13},{5,1},{9,5},{13,9},{2,14},{6,2},{... | collective-permute-start | bytes 1228808 | tf_op jit(solution)/shard_map/ppermute | solution.py:423
  45.0 15.5 %collective-permute-start.10 = (bf16[320,640]{1,0:T(8,128)(2,1)}, bf16[320,640]{1,0:T(8,128)(2,1)}, u32[]{:S(2)}, u32[]{:S(2)}) collective-permute-start(bf16[320,640]{1,0:T(8,128)(2,1)} %collective-permute-done.7.refs_3_), channel_id=1, source_target_pairs={{0,16},{16,0},{1,17},{17,1},{2,18},{18,2},{3,19},{19,3},{4,20},{20... | collective-permute-start | bytes 1228808 | tf_op jit(solution)/shard_map/ppermute | solution.py:435
  51.7 16.7 %copy-start.21 = (bf16[320,640]{1,0:T(8,128)(2,1)}, bf16[320,640]{1,0:T(8,128)(2,1)S(1)}, u32[]{:S(2)}) copy-start(bf16[320,640]{1,0:T(8,128)(2,1)S(1)} %collective-permute-done.1.refs_1_) | copy-start | bytes 1228804
  51.7 18.8 %collective-permute-start.3 = (bf16[320,640]{1,0:T(8,128)(2,1)S(1)}, bf16[320,640]{1,0:T(8,128)(2,1)}, u32[]{:S(2)}, u32[]{:S(2)}) collective-permute-start(bf16[320,640]{1,0:T(8,128)(2,1)S(1)} %collective-permute-done.1.refs_1_), channel_id=1, source_target_pairs={{0,16},{16,0},{1,17},{17,1},{2,18},{18,2},{3,19},{19,3},{4,20},{20... | collective-permute-start | bytes 1228808 | tf_op jit(solution)/shard_map/ppermute | solution.py:435
  53.3 17.2 %collective-permute-start.4 = (bf16[320,640]{1,0:T(8,128)(2,1)S(1)}, bf16[320,640]{1,0:T(8,128)(2,1)}, u32[]{:S(2)}, u32[]{:S(2)}) collective-permute-start(bf16[320,640]{1,0:T(8,128)(2,1)S(1)} %collective-permute-done.1.refs_1_), channel_id=1, source_target_pairs={{0,4},{4,8},{8,12},{12,0},{1,5},{5,9},{9,13},{13,1},{2,6},{6,10},{... | collective-permute-start | bytes 1228808 | tf_op jit(solution)/shard_map/ppermute | solution.py:423
  60.5 22.6 %collective-permute-start.11 = (bf16[320,640]{1,0:T(8,128)(2,1)}, bf16[320,640]{1,0:T(8,128)(2,1)S(1)}, u32[]{:S(2)}, u32[]{:S(2)}) collective-permute-start(bf16[320,640]{1,0:T(8,128)(2,1)} %collective-permute-done.8.refs_5_), channel_id=1, source_target_pairs={{0,16},{16,0},{1,17},{17,1},{2,18},{18,2},{3,19},{19,3},{4,20},{20... | collective-permute-start | bytes 1228808 | tf_op jit(solution)/shard_map/ppermute | solution.py:435
  68.5 14.6 %collective-permute-start.12 = (bf16[320,640]{1,0:T(8,128)(2,1)S(1)}, bf16[320,640]{1,0:T(8,128)(2,1)S(1)}, u32[]{:S(2)}, u32[]{:S(2)}) collective-permute-start(bf16[320,640]{1,0:T(8,128)(2,1)S(1)} %constant_dynamic-slice_fusion.5), channel_id=1, source_target_pairs={{0,4},{4,8},{8,12},{12,0},{1,5},{5,9},{9,13},{13,1},{2,6},{6,10},{... | collective-permute-start | bytes 1228808 | tf_op jit(solution)/shard_map/ppermute | solution.py:423
  70.5 14.3 %collective-permute-start.5 = (bf16[320,640]{1,0:T(8,128)(2,1)}, bf16[320,640]{1,0:T(8,128)(2,1)S(1)}, u32[]{:S(2)}, u32[]{:S(2)}) collective-permute-start(bf16[320,640]{1,0:T(8,128)(2,1)} %collective-permute-done.4.refs_3_), channel_id=1, source_target_pairs={{0,16},{16,0},{1,17},{17,1},{2,18},{18,2},{3,19},{19,3},{4,20},{20... | collective-permute-start | bytes 1228808 | tf_op jit(solution)/shard_map/ppermute | solution.py:435
  72.3 12.4 %copy-start.1 = (bf16[640,640]{1,0:T(8,128)(2,1)S(1)}, bf16[640,640]{1,0:T(8,128)(2,1)}, u32[]{:S(2)}) copy-start(bf16[640,640]{1,0:T(8,128)(2,1)} %refs_2_.3) | copy-start | bytes 2457604
  81.3 13.2 %collective-permute-start.16 = (bf16[320,640]{1,0:T(8,128)(2,1)S(1)}, bf16[320,640]{1,0:T(8,128)(2,1)S(1)}, u32[]{:S(2)}, u32[]{:S(2)}) collective-permute-start(bf16[320,640]{1,0:T(8,128)(2,1)S(1)} %constant_dynamic-slice_fusion.5), channel_id=1, source_target_pairs={{0,12},{4,0},{8,4},{12,8},{1,13},{5,1},{9,5},{13,9},{2,14},{6,2},{... | collective-permute-start | bytes 1228808 | tf_op jit(solution)/shard_map/ppermute | solution.py:423
  83.1 11.4 %copy-start.25 = (bf16[320,640]{1,0:T(8,128)(2,1)}, bf16[320,640]{1,0:T(8,128)(2,1)S(1)}, u32[]{:S(2)}) copy-start(bf16[320,640]{1,0:T(8,128)(2,1)S(1)} %collective-permute-done.12.refs_1_) | copy-start | bytes 1228804
  83.1 14.3 %collective-permute-start.13 = (bf16[320,640]{1,0:T(8,128)(2,1)S(1)}, bf16[320,640]{1,0:T(8,128)(2,1)S(1)}, u32[]{:S(2)}, u32[]{:S(2)}) collective-permute-start(bf16[320,640]{1,0:T(8,128)(2,1)S(1)} %collective-permute-done.12.refs_1_), channel_id=1, source_target_pairs={{0,16},{16,0},{1,17},{17,1},{2,18},{18,2},{3,19},{19,3},{4,20},{20... | collective-permute-start | bytes 1228808 | tf_op jit(solution)/shard_map/ppermute | solution.py:435
  84.7 18.2 %collective-permute-start.14 = (bf16[320,640]{1,0:T(8,128)(2,1)S(1)}, bf16[320,640]{1,0:T(8,128)(2,1)}, u32[]{:S(2)}, u32[]{:S(2)}) collective-permute-start(bf16[320,640]{1,0:T(8,128)(2,1)S(1)} %collective-permute-done.12.refs_1_), channel_id=1, source_target_pairs={{0,4},{4,8},{8,12},{12,0},{1,5},{5,9},{9,13},{13,1},{2,6},{6,10},{... | collective-permute-start | bytes 1228808 | tf_op jit(solution)/shard_map/ppermute | solution.py:423
  94.5 21.3 %copy-start.26 = (bf16[320,640]{1,0:T(8,128)(2,1)}, bf16[320,640]{1,0:T(8,128)(2,1)S(1)}, u32[]{:S(2)}) copy-start(bf16[320,640]{1,0:T(8,128)(2,1)S(1)} %collective-permute-done.16.refs_5_) | copy-start | bytes 1228804
  94.5 12.5 %collective-permute-start.17 = (bf16[320,640]{1,0:T(8,128)(2,1)S(1)}, bf16[320,640]{1,0:T(8,128)(2,1)S(1)}, u32[]{:S(2)}, u32[]{:S(2)}) collective-permute-start(bf16[320,640]{1,0:T(8,128)(2,1)S(1)} %collective-permute-done.16.refs_5_), channel_id=1, source_target_pairs={{0,16},{16,0},{1,17},{17,1},{2,18},{18,2},{3,19},{19,3},{4,20},{20... | collective-permute-start | bytes 1228808 | tf_op jit(solution)/shard_map/ppermute | solution.py:435
  95.5 13.8 %collective-permute-start.18 = (bf16[320,640]{1,0:T(8,128)(2,1)S(1)}, bf16[320,640]{1,0:T(8,128)(2,1)S(1)}, u32[]{:S(2)}, u32[]{:S(2)}) collective-permute-start(bf16[320,640]{1,0:T(8,128)(2,1)S(1)} %constant_dynamic-slice_fusion.4), channel_id=1, source_target_pairs={{0,4},{4,8},{8,12},{12,0},{1,5},{5,9},{9,13},{13,1},{2,6},{6,10},{... | collective-permute-start | bytes 1228808 | tf_op jit(solution)/shard_map/ppermute | solution.py:423
  97.5 15.9 %copy-start.27 = (bf16[320,640]{1,0:T(8,128)(2,1)}, bf16[320,640]{1,0:T(8,128)(2,1)S(1)}, u32[]{:S(2)}) copy-start(bf16[320,640]{1,0:T(8,128)(2,1)S(1)} %collective-permute-done.13.refs_2_) | copy-start | bytes 1228804
  102.9 12.9 %collective-permute-start.15 = (bf16[320,640]{1,0:T(8,128)(2,1)}, bf16[320,640]{1,0:T(8,128)(2,1)S(1)}, u32[]{:S(2)}, u32[]{:S(2)}) collective-permute-start(bf16[320,640]{1,0:T(8,128)(2,1)} %collective-permute-done.14.refs_3_), channel_id=1, source_target_pairs={{0,16},{16,0},{1,17},{17,1},{2,18},{18,2},{3,19},{19,3},{4,20},{20... | collective-permute-start | bytes 1228808 | tf_op jit(solution)/shard_map/ppermute | solution.py:435
  109.3 15.8 %copy-start.2 = (bf16[320,640]{1,0:T(8,128)(2,1)}, bf16[320,640]{1,0:T(8,128)(2,1)S(1)}, u32[]{:S(2)}) copy-start(bf16[320,640]{1,0:T(8,128)(2,1)S(1)} %collective-permute-done.18.refs_4_.refs_3_) | copy-start | bytes 1228804
  109.3 23.9 %collective-permute-start.19 = (bf16[320,640]{1,0:T(8,128)(2,1)S(1)}, bf16[320,640]{1,0:T(8,128)(2,1)S(1)}, u32[]{:S(2)}, u32[]{:S(2)}) collective-permute-start(bf16[320,640]{1,0:T(8,128)(2,1)S(1)} %collective-permute-done.18.refs_4_.refs_3_), channel_id=1, source_target_pairs={{0,16},{16,0},{1,17},{17,1},{2,18},{18,2},{3,19},{19,3},{4,20},{20... | collective-permute-start | bytes 1228808 | tf_op jit(solution)/shard_map/ppermute | solution.py:435
  110.8 22.4 %collective-permute-start.21 = (bf16[320,640]{1,0:T(8,128)(2,1)S(1)}, bf16[320,640]{1,0:T(8,128)(2,1)S(1)}, u32[]{:S(2)}, u32[]{:S(2)}) collective-permute-start(bf16[320,640]{1,0:T(8,128)(2,1)S(1)} %constant_dynamic-slice_fusion.4), channel_id=1, source_target_pairs={{0,12},{4,0},{8,4},{12,8},{1,13},{5,1},{9,5},{13,9},{2,14},{6,2},{... | collective-permute-start | bytes 1228808 | tf_op jit(solution)/shard_map/ppermute | solution.py:423
  113.9 30.1 %collective-permute-start.20 = (bf16[320,640]{1,0:T(8,128)(2,1)S(1)}, bf16[320,640]{1,0:T(8,128)(2,1)S(1)}, u32[]{:S(2)}, u32[]{:S(2)}) collective-permute-start(bf16[320,640]{1,0:T(8,128)(2,1)S(1)} %collective-permute-done.18.refs_4_.refs_3_), channel_id=1, source_target_pairs={{0,4},{4,8},{8,12},{12,0},{1,5},{5,9},{9,13},{13,1},{2,6},{6,10},{... | collective-permute-start | bytes 1228808 | tf_op jit(solution)/shard_map/ppermute | solution.py:423
  133.2 10.7 %copy-start.3 = (bf16[320,640]{1,0:T(8,128)(2,1)}, bf16[320,640]{1,0:T(8,128)(2,1)S(1)}, u32[]{:S(2)}) copy-start(bf16[320,640]{1,0:T(8,128)(2,1)S(1)} %collective-permute-done.19.refs_5_.refs_4_) | copy-start | bytes 1228804
  133.2 10.7 %copy-start.4 = (bf16[320,640]{1,0:T(8,128)(2,1)}, bf16[320,640]{1,0:T(8,128)(2,1)S(1)}, u32[]{:S(2)}) copy-start(bf16[320,640]{1,0:T(8,128)(2,1)S(1)} %collective-permute-done.21.refs_8_.refs_7_) | copy-start | bytes 1228804
  133.2 10.8 %collective-permute-start.22 = (bf16[320,640]{1,0:T(8,128)(2,1)S(1)}, bf16[320,640]{1,0:T(8,128)(2,1)S(1)}, u32[]{:S(2)}, u32[]{:S(2)}) collective-permute-start(bf16[320,640]{1,0:T(8,128)(2,1)S(1)} %collective-permute-done.19.refs_5_.refs_4_), channel_id=1, source_target_pairs={{0,4},{4,8},{8,12},{12,0},{1,5},{5,9},{9,13},{13,1},{2,6},{6,10},{... | collective-permute-start | bytes 1228808 | tf_op jit(solution)/shard_map/ppermute | solution.py:423
  133.5 10.5 %collective-permute-start.23 = (bf16[320,640]{1,0:T(8,128)(2,1)S(1)}, bf16[320,640]{1,0:T(8,128)(2,1)S(1)}, u32[]{:S(2)}, u32[]{:S(2)}) collective-permute-start(bf16[320,640]{1,0:T(8,128)(2,1)S(1)} %collective-permute-done.21.refs_8_.refs_7_), channel_id=1, source_target_pairs={{0,16},{16,0},{1,17},{17,1},{2,18},{18,2},{3,19},{19,3},{4,20},{20... | collective-permute-start | bytes 1228808 | tf_op jit(solution)/shard_map/ppermute | solution.py:435
  150.8 9.0 %collective-permute-start.24 = (bf16[2,448,640]{2,1,0:T(8,128)(2,1)}, bf16[2,448,640]{2,1,0:T(8,128)(2,1)S(1)}, u32[]{:S(2)}, u32[]{:S(2)}) collective-permute-start(bf16[2,448,640]{2,1,0:T(8,128)(2,1)} %get-tuple-element.56), channel_id=1, source_target_pairs={{0,1},{1,0},{2,3},{3,2},{4,5},{5,4},{6,7},{7,6},{8,9},{9,8},{10,11... | collective-permute-start | bytes 3440648 | tf_op jit(solution)/shard_map/ppermute | solution.py:478
  156.9 9.5 %collective-permute-start.28 = (f32[4,8,640]{2,1,0:T(8,128)S(1)}, f32[4,8,640]{2,1,0:T(8,128)S(1)}, u32[]{:S(2)}, u32[]{:S(2)}) collective-permute-start(f32[4,8,640]{2,1,0:T(8,128)S(1)} %constant_dynamic-update-slice_fusion), channel_id=1, source_target_pairs={{0,1},{1,0},{2,3},{3,2},{4,5},{5,4},{6,7},{7,6},{8,9},{9,8},{10,11... | collective-permute-start | bytes 245768 | tf_op jit(solution)/shard_map/ppermute | solution.py:478
  157.8 19.3 %collective-permute-start.25 = (bf16[2,448,640]{2,1,0:T(8,128)(2,1)}, bf16[2,448,640]{2,1,0:T(8,128)(2,1)S(1)}, u32[]{:S(2)}, u32[]{:S(2)}) collective-permute-start(bf16[2,448,640]{2,1,0:T(8,128)(2,1)} %get-tuple-element.58), channel_id=1, source_target_pairs={{0,1},{1,0},{2,3},{3,2},{4,5},{5,4},{6,7},{7,6},{8,9},{9,8},{10,11... | collective-permute-start | bytes 3440648 | tf_op jit(solution)/shard_map/ppermute | solution.py:478
  157.9 8.7 %collective-permute-start.29 = (f32[4,8,640]{2,1,0:T(8,128)S(1)}, f32[4,8,640]{2,1,0:T(8,128)S(1)}, u32[]{:S(2)}, u32[]{:S(2)}) collective-permute-start(f32[4,8,640]{2,1,0:T(8,128)S(1)} %constant_dynamic-update-slice_fusion), channel_id=1, source_target_pairs={{0,2},{1,3},{2,0},{3,1},{4,6},{5,7},{6,4},{7,5},{8,10},{9,11},{10,... | collective-permute-start | bytes 245768 | tf_op jit(solution)/shard_map/ppermute | solution.py:478
  159.1 7.4 %collective-permute-start.30 = (f32[4,8,640]{2,1,0:T(8,128)S(1)}, f32[4,8,640]{2,1,0:T(8,128)S(1)}, u32[]{:S(2)}, u32[]{:S(2)}) collective-permute-start(f32[4,8,640]{2,1,0:T(8,128)S(1)} %constant_dynamic-update-slice_fusion), channel_id=1, source_target_pairs={{0,3},{1,2},{2,1},{3,0},{4,7},{5,6},{6,5},{7,4},{8,11},{9,10},{10,... | collective-permute-start | bytes 245768 | tf_op jit(solution)/shard_map/ppermute | solution.py:478
  165.7 27.5 %collective-permute-start.26 = (bf16[2,448,640]{2,1,0:T(8,128)(2,1)}, bf16[2,448,640]{2,1,0:T(8,128)(2,1)S(1)}, u32[]{:S(2)}, u32[]{:S(2)}) collective-permute-start(bf16[2,448,640]{2,1,0:T(8,128)(2,1)} %out_project.6), channel_id=1, source_target_pairs={{0,2},{1,3},{2,0},{3,1},{4,6},{5,7},{6,4},{7,5},{8,10},{9,11},{10,... | collective-permute-start | bytes 3440648 | tf_op jit(solution)/shard_map/ppermute | solution.py:478
  166.6 6.5 %collective-permute-start.33 = (bf16[5,8,640]{2,1,0:T(8,128)(2,1)S(1)}, bf16[5,8,640]{2,1,0:T(8,128)(2,1)S(1)}, u32[]{:S(2)}, u32[]{:S(2)}) collective-permute-start(bf16[5,8,640]{2,1,0:T(8,128)(2,1)S(1)} %get-tuple-element.88), channel_id=1, source_target_pairs={{0,12},{4,0},{8,4},{12,8},{1,13},{5,1},{9,5},{13,9},{2,14},{6,2},{... | collective-permute-start | bytes 153608 | tf_op jit(solution)/shard_map/ppermute | solution.py:423
  170.9 5.4 %collective-permute-start.32 = (bf16[5,8,640]{2,1,0:T(8,128)(2,1)S(1)}, bf16[5,8,640]{2,1,0:T(8,128)(2,1)S(1)}, u32[]{:S(2)}, u32[]{:S(2)}) collective-permute-start(bf16[5,8,640]{2,1,0:T(8,128)(2,1)S(1)} %get-tuple-element.88), channel_id=1, source_target_pairs={{0,8},{4,12},{8,0},{12,4},{1,9},{5,13},{9,1},{13,5},{2,10},{6,14},... | collective-permute-start | bytes 153608 | tf_op jit(solution)/shard_map/ppermute | solution.py:423
  171.2 5.9 %collective-permute-start.31 = (bf16[5,8,640]{2,1,0:T(8,128)(2,1)S(1)}, bf16[5,8,640]{2,1,0:T(8,128)(2,1)S(1)}, u32[]{:S(2)}, u32[]{:S(2)}) collective-permute-start(bf16[5,8,640]{2,1,0:T(8,128)(2,1)S(1)} %get-tuple-element.88), channel_id=1, source_target_pairs={{0,4},{4,8},{8,12},{12,0},{1,5},{5,9},{9,13},{13,1},{2,6},{6,10},{... | collective-permute-start | bytes 153608 | tf_op jit(solution)/shard_map/ppermute | solution.py:423
  195.5 2.5 %collective-permute-start.27 = (bf16[448,640]{1,0:T(8,128)(2,1)S(1)}, bf16[448,640]{1,0:T(8,128)(2,1)S(1)}, u32[]{:S(2)}, u32[]{:S(2)}) collective-permute-start(bf16[448,640]{1,0:T(8,128)(2,1)S(1)} %get-tuple-element.72), channel_id=1, source_target_pairs={{0,1},{1,0},{2,3},{3,2},{4,5},{5,4},{6,7},{7,6},{8,9},{9,8},{10,11... | collective-permute-start | bytes 1720328 | tf_op jit(solution)/shard_map/ppermute | solution.py:478
  (20 other events, 70.7 us)
Sparse Core Ops, SparseCore 0:
  9.6 39.3 all-gather.2

commit v5 on v4

--- a/solution.py
+++ b/solution.py
@@ -262,49 +262,114 @@
     )(place, normed, *flat, *turn)
 
 
-def attend_kernel(place_ref, ends_ref, q_ref, k_ref, v_ref, out_ref, *, row_block):
-    count = k_ref.shape[0]
+def attend_rows(base, ends_ref, q_ref, k_ref, v_ref, out_ref):
+    size, count = q_ref.shape[0], k_ref.shape[0]
+    sequences = ends_ref.shape[0]
+    col = lax.broadcasted_iota(jnp.int32, (1, count), 1)
+    col_label = sum((col >= ends_ref[j]).astype(jnp.int32) for j in range(sequences - 1))
+    row = lax.broadcasted_iota(jnp.int32, (size, 1), 0) + base
+    row_label = sum((row >= ends_ref[j]).astype(jnp.int32) for j in range(sequences - 1))
+    for h in range(q_ref.shape[1] // HS):
+        head = slice(h * HS, (h + 1) * HS)
+        scores = lax.dot_general(
+            q_ref[:, head],
+            k_ref[:, head],
+            (((1,), (1,)), ((), ())),
+            preferred_element_type=F32,
+        )
+        scores = jnp.where(row_label == col_label, scores, -1e30)
+        top = jnp.max(scores, -1, keepdims=True)
+        raised = jnp.exp(scores - top)
+        weights = raised * (1.0 / jnp.sum(raised, -1, keepdims=True))
+        out_ref[:, head] = jnp.dot(
+            weights.astype(BF16), v_ref[:, head], preferred_element_type=F32
+        ).astype(BF16)
+
+
+def attend_kernel(place_ref, ends_ref, q_ref, k_ref, v_ref, out_ref):
     base = place_ref[1] * q_ref.shape[0]
-    col = lax.broadcasted_iota(jnp.int32, (1, count), 1)
-    sequences = ends_ref.shape[0]
-    col_label = sum((col >= ends_ref[j]).astype(jnp.int32) for j in range(sequences - 1))
-    for r in range(q_ref.shape[0] // row_block):
-        span = slice(r * row_block, (r + 1) * row_block)
-        row = lax.broadcasted_iota(jnp.int32, (row_block, 1), 0) + (base + r * row_block)
-        row_label = sum((row >= ends_ref[j]).astype(jnp.int32) for j in range(sequences - 1))
-        for h in range(q_ref.shape[1] // HS):
-            head = slice(h * HS, (h + 1) * HS)
-            scores = lax.dot_general(
-                q_ref[span, head],
-                k_ref[:, head],
-                (((1,), (1,)), ((), ())),
-                preferred_element_type=F32,
+    attend_rows(base, ends_ref, q_ref, k_ref, v_ref, out_ref)
+
+
+def value_attend_kernel(lengths, place_ref, half_ref, ends_ref, x_ref, q_ref, k_ref, *refs):
+    refs = list(refs)
+    shards = take_shards(refs, lengths)
+    value_ref, out_ref, wbuf, xbuf, qbuf, kbuf, vbuf, w_sems, sems = refs
+    depth = shards[0][0].shape[0]
+    half = depth // 2
+    copies = [pltpu.make_async_copy(x_ref, xbuf, sems.at[0])]
+    for k, shard in enumerate(shards):
+        for j, (source, row) in enumerate(shard_parts(place_ref[0], shard, half)):
+            row = pl.multiple_of(place_ref[1 + k] * depth + row, half)
+            copies.append(
+                pltpu.make_async_copy(source, wbuf.at[pl.ds(row, half)], w_sems.at[k, j])
             )
-            scores = jnp.where(row_label == col_label, scores, -1e30)
-            top = jnp.max(scores, -1, keepdims=True)
-            raised = jnp.exp(scores - top)
-            weights = raised * (1.0 / jnp.sum(raised, -1, keepdims=True))
-            out_ref[span, head] = jnp.dot(
-                weights.astype(BF16), v_ref[:, head], preferred_element_type=F32
-            ).astype(BF16)
-
-
-def attention(place, ends, queries, key_rows, value_rows, row_block=448, group=5):
+    size = qbuf.shape[0]
+    base = pl.multiple_of(half_ref[1] * size, size)
+    later = [
+        pltpu.make_async_copy(k_ref, kbuf, sems.at[1]),
+        pltpu.make_async_copy(q_ref.at[pl.ds(base, size)], qbuf, sems.at[2]),
+    ]
+    for copy in copies + later:
+        copy.start()
+    for copy in copies:
+        copy.wait()
+    vbuf[...] = jnp.dot(xbuf[...], wbuf[...], preferred_element_type=F32).astype(BF16)
+    store = pltpu.make_async_copy(vbuf, value_ref, sems.at[3])
+    store.start()
+    for copy in later:
+        copy.wait()
+    attend_rows(base, ends_ref, qbuf, kbuf, vbuf, out_ref)
+    store.wait()
+
+
+def value_attend(place, half_place, ends, normed, queries, key_rows, shards):
+    rows, features = normed.shape
+    columns = queries.shape[1]
+    half = rows // 2
+    flat = [ref for shard in shards for ref in shard]
+    return pl.pallas_call(
+        functools.partial(value_attend_kernel, [len(shard) for shard in shards]),
+        in_specs=[SMEM_SPEC] * 3 + [HBM_SPEC] * (3 + len(flat)),
+        out_specs=[HBM_SPEC, pl.BlockSpec(memory_space=pltpu.VMEM)],
+        out_shape=[
+            jax.ShapeDtypeStruct((rows, columns), BF16),
+            jax.ShapeDtypeStruct((half, columns), BF16),
+        ],
+        scratch_shapes=[
+            pltpu.VMEM((features, columns), BF16),
+            pltpu.VMEM((rows, features), BF16),
+            pltpu.VMEM((half, columns), BF16),
+            pltpu.VMEM((rows, columns), BF16),
+            pltpu.VMEM((rows, columns), BF16),
+            pltpu.SemaphoreType.DMA((4, 2)),
+            pltpu.SemaphoreType.DMA((4,)),
+        ],
+        compiler_params=params(),
+        cost_estimate=pl.CostEstimate(
+            flops=2 * rows * columns * (features + rows),
+            bytes_accessed=2 * (normed.size + (features + 4 * rows) * columns),
+            transcendentals=half * rows * columns // HS,
+        ),
+        name="value_attend",
+    )(place, half_place, ends, normed, queries, key_rows, *flat)
+
+
+def attention(place, ends, queries, key_rows, value_rows):
     rows, columns = queries.shape
     half = rows // 2
     heads = columns // HS
-    wide = group * HS
     return pl.pallas_call(
-        functools.partial(attend_kernel, row_block=row_block),
+        attend_kernel,
         grid_spec=pltpu.PrefetchScalarGridSpec(
             num_scalar_prefetch=2,
-            grid=(heads // group,),
+            grid=(1,),
             in_specs=[
-                pl.BlockSpec((half, wide), lambda h, place, ends: (place[1], h)),
-                pl.BlockSpec((rows, wide), lambda h, place, ends: (0, h)),
-                pl.BlockSpec((rows, wide), lambda h, place, ends: (0, h)),
+                pl.BlockSpec((half, columns), lambda h, place, ends: (place[1], h)),
+                pl.BlockSpec((rows, columns), lambda h, place, ends: (0, h)),
+                pl.BlockSpec((rows, columns), lambda h, place, ends: (0, h)),
             ],
-            out_specs=pl.BlockSpec((half, wide), lambda h, place, ends: (0, h)),
+            out_specs=pl.BlockSpec((half, columns), lambda h, place, ends: (0, h)),
         ),
         out_shape=jax.ShapeDtypeStruct((half, columns), BF16),
         compiler_params=params("arbitrary"),
@@ -399,7 +464,7 @@
         out_specs=out_specs,
         out_shape=out_shape,
         scratch_shapes=scratch,
-        compiler_params=params("arbitrary", limit=VMEM_LIMIT),
+        compiler_params=params("arbitrary", limit=24 * 1024 * 1024),
         cost_estimate=pl.CostEstimate(
             flops=4 * half * depth * width,
             bytes_accessed=2 * (half * depth + 2 * (depth + (1 + adding) * half) * width),
@@ -506,9 +571,10 @@
     ring.step(ring.along[6], 1)
     mine = ring.half(w_out)
     ring.step(mine, 1)
-    value_rows = project(place, normed, [(w_value,), *ring.pieces(2)])
-    ring.step(mine, -1, before=[queries], before_swap=[value_rows])
-    context_sent = attention(send_place, ends, queries, key_rows, value_rows)
+    value_rows, context_sent = value_attend(
+        place, send_place, ends, normed, queries, key_rows, [(w_value,), *ring.pieces(2)]
+    )
+    ring.step(mine, -1, before=[queries], before_swap=[context_sent])
     last_along = ring.ring(tie(ring.along[9], ring.along[9]), 1)
     last_other = ring.ring(tie(ring.across[-2], ring.along[10], context_sent), 1)
     out_in = [(w_out,), ring.shards[9], (last_along, last_other), ring.shards[10]]

time: 207 us -> 206 us (level)
  waiting for transfers between devices: 59.4 us -> 64.4 us
  Pallas kernels: 68.7 us -> 63.9 us
  starting transfers between devices: 43.5 us -> 41.2 us
    pallas_call x3 -> x2, Pallas kernels: 26.5 us -> 18 us  [project(): pl.pallas_call(functools.partial(project_kernel, scale, bool(turn), [len(...]
    pallas_call x2, Pallas kernels: 16.2 us -> 24.2 us  [the longest x1 16 us: value_attend(): pl.pallas_call(functools.partial(value_attend_kernel, [len(shard) for sha...]
    pallas_call x4, Pallas kernels: 19.6 us -> 15.3 us  [out_project(): pl.pallas_call(functools.partial(out_kernel, adding, base, [len(shard) fo...]
    ppermute x16, waiting for transfers between devices: 43.7 us -> 46.5 us  [ring(): lax.ppermute(value, 'dp', [(i, (i + step) % self.dp) for i in range(self....]
    unnamed x69 -> x67, local copies, waits for them, and re-layouts: 7.21 us -> 9.29 us
  transfers between devices with their start and end apart: 35 -> 35, of which waited for: 12 -> 14; matrix products, arithmetic and copies ran while one was open for 5% -> 4% of each run, Pallas kernels for 31% -> 29%
where the time goes in v5:
time: 206 us
  waiting for transfers between devices  64.4 us (31%)
  Pallas kernels  63.9 us (31%)
  starting transfers between devices  41.2 us (20%)
  between operations  14.5 us (7%)
  local copies, waits for them, and re-layouts  10.8 us (5%)
  other arithmetic  10.3 us (5%)
    ppermute x16, waiting for transfers between devices, ring(): lax.ppermute(value, 'dp', [(i, (i + step) % self.dp) for i in range(self....  46.5 us
    ppermute x16, starting transfers between devices, ring(): lax.ppermute(value, 'dp', [(i, (i + step) % self.dp) for i in range(self....  22.6 us
    pallas_call x2, Pallas kernels, project(): pl.pallas_call(functools.partial(project_kernel, scale, bool(turn), [len(...  18 us
    pallas_call x1, Pallas kernels, value_attend(): pl.pallas_call(functools.partial(value_attend_kernel, [len(shard) for sha...  16 us
    pallas_call x4, Pallas kernels, out_project(): pl.pallas_call(functools.partial(out_kernel, adding, base, [len(shard) fo...  15.3 us
    ppermute x11, starting transfers between devices, step(): lax.ppermute(tie(self.along[i], *waits, *before_swap), 'parts', [(0, 1),...  14.3 us
    ppermute x7, waiting for transfers between devices, swap_by(): return lax.ppermute(value, 'fsdp', [(i, i ^ mask) for i in range(fsdp)])  11.8 us
    unnamed x67, local copies, waits for them, and re-layouts  9.29 us
  transfers between devices with their start and end apart: 35, of which 14 were waited for; matrix products, arithmetic and copies ran while one was open for 4% of the time, Pallas kernels for 29%

profile of v5, /device:TPU:0, one launch (start us, length us, event | category | flops | bytes accessed | tf_op | source)
XLA Modules:
  0.0 205.7 jit_solution(1393031741334869545)
XLA Ops:
  8.4 3.1 %collective-permute-start.6 = (bf16[320,640]{1,0:T(8,128)(2,1)S(1)}, bf16[320,640]{1,0:T(8,128)(2,1)S(1)}, u32[]{:S(2)}, u32[]{:S(2)}) collective-permute-start(bf16[320,640]{1,0:T(8,128)(2,1)S(1)} %constant_dynamic-slice_fusion.6), channel_id=1, source_target_pairs={{0,4},{4,8},{8,12},{12,0},{1,5},{5,9},{9,13},{13,1},{2,6},{6,10},{... | collective-permute-start | bytes 1228808 | tf_op jit(solution)/shard_map/ppermute | solution.py:488
  11.5 2.1 %collective-permute-start = (bf16[320,640]{1,0:T(8,128)(2,1)S(1)}, bf16[320,640]{1,0:T(8,128)(2,1)}, u32[]{:S(2)}, u32[]{:S(2)}) collective-permute-start(bf16[320,640]{1,0:T(8,128)(2,1)S(1)} %constant_dynamic-slice_fusion.6), channel_id=1, source_target_pairs={{0,12},{4,0},{8,4},{12,8},{1,13},{5,1},{9,5},{13,9},{2,14},{6,2},{... | collective-permute-start | bytes 1228808 | tf_op jit(solution)/shard_map/ppermute | solution.py:488
  14.3 9.6 %collective-permute-done.6.refs_1_ = bf16[320,640]{1,0:T(8,128)(2,1)S(1)} collective-permute-done((bf16[320,640]{1,0:T(8,128)(2,1)S(1)}, bf16[320,640]{1,0:T(8,128)(2,1)S(1)}, u32[]{:S(2)}, u32[]{:S(2)}) %collective-permute-start.6) | collective-permute-done | bytes 409632 | tf_op jit(solution)/shard_map/ppermute | solution.py:488
  23.9 1.8 collective-permute-start.9
  25.7 5.8 %collective-permute-done.refs_5_ = bf16[320,640]{1,0:T(8,128)(2,1)} collective-permute-done((bf16[320,640]{1,0:T(8,128)(2,1)S(1)}, bf16[320,640]{1,0:T(8,128)(2,1)}, u32[]{:S(2)}, u32[]{:S(2)}) %collective-permute-start) | collective-permute-done | bytes 409632 | tf_op jit(solution)/shard_map/ppermute | solution.py:488
  31.5 2.1 %collective-permute-start.1 = (bf16[320,640]{1,0:T(8,128)(2,1)S(1)}, bf16[320,640]{1,0:T(8,128)(2,1)}, u32[]{:S(2)}, u32[]{:S(2)}) collective-permute-start(bf16[320,640]{1,0:T(8,128)(2,1)S(1)} %constant_dynamic-slice_fusion.7), channel_id=1, source_target_pairs={{0,4},{4,8},{8,12},{12,0},{1,5},{5,9},{9,13},{13,1},{2,6},{6,10},{... | collective-permute-start | bytes 1228808 | tf_op jit(solution)/shard_map/ppermute | solution.py:488
  33.6 1.4 collective-permute-start.2
  35.1 8.1 %collective-permute-done.7.refs_3_ = bf16[320,640]{1,0:T(8,128)(2,1)} collective-permute-done((bf16[320,640]{1,0:T(8,128)(2,1)S(1)}, bf16[320,640]{1,0:T(8,128)(2,1)}, u32[]{:S(2)}, u32[]{:S(2)}) %collective-permute-start.7) | collective-permute-done | bytes 409632 | tf_op jit(solution)/shard_map/ppermute | solution.py:488
  43.2 1.9 collective-permute-start.8
  45.0 1.5 collective-permute-start.10
  46.6 5.2 %collective-permute-done.1.refs_1_ = bf16[320,640]{1,0:T(8,128)(2,1)} collective-permute-done((bf16[320,640]{1,0:T(8,128)(2,1)S(1)}, bf16[320,640]{1,0:T(8,128)(2,1)}, u32[]{:S(2)}, u32[]{:S(2)}) %collective-permute-start.1) | collective-permute-done | bytes 409632 | tf_op jit(solution)/shard_map/ppermute | solution.py:488
  51.8 1.5 collective-permute-start.3
  54.7 1.7 fusion.2
  56.3 4.2 %collective-permute-done.8.refs_5_ = bf16[320,640]{1,0:T(8,128)(2,1)} collective-permute-done((bf16[320,640]{1,0:T(8,128)(2,1)S(1)}, bf16[320,640]{1,0:T(8,128)(2,1)}, u32[]{:S(2)}, u32[]{:S(2)}) %collective-permute-start.8) | collective-permute-done | bytes 409632 | tf_op jit(solution)/shard_map/ppermute | solution.py:488
  60.5 1.5 collective-permute-start.11
  62.1 6.4 %norm_rows.1 = (bf16[896,2560]{1,0:T(8,128)(2,1)}, f32[4,8,640]{2,1,0:T(8,128)}) custom-call(s32[1]{0:T(128)} %bitcast.13.column_ref, s32[3]{0:T(128)} %get-tuple-element.72.picked_ref.refs_0_, bf16[4,896,640]{2,1,0:T(8,128)(2,1)} %bitcast.42), custom_call_target="tpu_custom_call" | custom-call | flops 18350080 | bytes 9175040 | tf_op jit(solution)/shard_map/norm_rows/pallas_call | solution.py:163
  69.3 1.2 pad_maximum_fusion
  70.5 1.7 collective-permute-start.5
  72.2 9.0 %project.3.k_ref = bf16[896,640]{1,0:T(8,128)(2,1)} custom-call(s32[5]{0:T(128)} %stack.105.place_ref, bf16[896,2560]{1,0:T(8,128)(2,1)} %get-tuple-element.36.x_ref, bf16[640,640]{1,0:T(8,128)(2,1)} %refs_0_.4, bf16[320,640]{1,0:T(8,128)(2,1)} %copy-done.22, bf16[320,640]{1,0:T(8,128)(2,1)} %copy-done.23, bf16[320,640]{1,0:T(8,128)(2,1)} %collective-permute-done.7.refs_3_, ...), custom_call_target="tpu_custom_call" | custom-call | flops 2936012800 | bytes 9011200 | tf_op jit(solution)/shard_map/project/pallas_call | solution.py:243
  81.3 1.9 collective-permute-start.16
  83.2 1.6 collective-permute-start.13
  85.6 9.0 %project.2.q_ref = bf16[896,640]{1,0:T(8,128)(2,1)} custom-call(s32[5]{0:T(128)} %stack.105.place_ref, bf16[896,2560]{1,0:T(8,128)(2,1)} %get-tuple-element.36.x_ref, bf16[640,640]{1,0:T(8,128)(2,1)} %refs_0_.3, bf16[320,640]{1,0:T(8,128)(2,1)} %collective-permute-done.1.refs_1_, bf16[320,640]{1,0:T(8,128)(2,1)} %copy-done.25, ...), custom_call_target="tpu_custom_call" | custom-call | flops 2936012800 | bytes 9011200 | tf_op jit(solution)/shard_map/project/pallas_call | solution.py:243
  95.5 2.0 collective-permute-start.18
  97.5 6.0 %collective-permute-done.14.refs_3_ = bf16[320,640]{1,0:T(8,128)(2,1)} collective-permute-done((bf16[320,640]{1,0:T(8,128)(2,1)S(1)}, bf16[320,640]{1,0:T(8,128)(2,1)}, u32[]{:S(2)}, u32[]{:S(2)}) %collective-permute-start.14) | collective-permute-done | bytes 409632 | tf_op jit(solution)/shard_map/ppermute | solution.py:488
  104.3 2.8 %collective-permute-done.17.refs_6_ = bf16[320,640]{1,0:T(8,128)(2,1)S(1)} collective-permute-done((bf16[320,640]{1,0:T(8,128)(2,1)S(1)}, bf16[320,640]{1,0:T(8,128)(2,1)S(1)}, u32[]{:S(2)}, u32[]{:S(2)}) %collective-permute-start.17) | collective-permute-done | bytes 409632 | tf_op jit(solution)/shard_map/ppermute | solution.py:500
  107.1 2.3 %collective-permute-done.18.refs_4_.refs_3_ = bf16[320,640]{1,0:T(8,128)(2,1)S(1)} collective-permute-done((bf16[320,640]{1,0:T(8,128)(2,1)S(1)}, bf16[320,640]{1,0:T(8,128)(2,1)S(1)}, u32[]{:S(2)}, u32[]{:S(2)}) %collective-permute-start.18) | collective-permute-done | bytes 409632 | tf_op jit(solution)/shard_map/ppermute | solution.py:488
  109.3 1.5 collective-permute-start.19
  110.9 2.1 %collective-permute-start.21 = (bf16[320,640]{1,0:T(8,128)(2,1)S(1)}, bf16[320,640]{1,0:T(8,128)(2,1)S(1)}, u32[]{:S(2)}, u32[]{:S(2)}) collective-permute-start(bf16[320,640]{1,0:T(8,128)(2,1)S(1)} %constant_dynamic-slice_fusion.4), channel_id=1, source_target_pairs={{0,12},{4,0},{8,4},{12,8},{1,13},{5,1},{9,5},{13,9},{2,14},{6,2},{... | collective-permute-start | bytes 1228808 | tf_op jit(solution)/shard_map/ppermute | solution.py:488
  113.6 2.6 %collective-permute-done.15.refs_4_ = bf16[320,640]{1,0:T(8,128)(2,1)} collective-permute-done((bf16[320,640]{1,0:T(8,128)(2,1)}, bf16[320,640]{1,0:T(8,128)(2,1)}, u32[]{:S(2)}, u32[]{:S(2)}) %collective-permute-start.15) | collective-permute-done | bytes 409632 | tf_op jit(solution)/shard_map/ppermute | solution.py:500
  116.2 16.0 %value_attend.1 = (bf16[896,640]{1,0:T(8,128)(2,1)}, bf16[448,640]{1,0:T(8,128)(2,1)}) custom-call(s32[5]{0:T(128)} %stack.105.place_ref, s32[2]{0:T(128)} %pad_add_fusion.1.half_ref, s32[3]{0:T(128)} %bitcast.51, bf16[896,2560]{1,0:T(8,128)(2,1)} %get-tuple-element.36.x_ref, bf16[896,640]{1,0:T(8,128)(2,1)} %project.2.q_ref, ...), custom_call_target="tpu_custom_call" | custom-call | flops 3963617280 | bytes 12451840 | tf_op jit(solution)/shard_map/value_attend/pallas_call | solution.py:331
  133.3 8.2 %attention.1.refs_2_.refs_0_ = bf16[448,640]{1,0:T(8,128)(2,1)} custom-call(s32[2]{0:T(128)} %pad_add_fusion.place_ref, s32[3]{0:T(128)} %bitcast.52, bf16[896,640]{1,0:T(8,128)(2,1)} %project.2.q_ref, bf16[896,640]{1,0:T(8,128)(2,1)} %project.3.k_ref, bf16[896,640]{1,0:T(8,128)(2,1)} %get-tuple-element.51.v_ref), custom_call_target="tpu_custom_call" | custom-call | flops 1027604480 | bytes 3440640 | tf_op jit(solution)/shard_map/attention/pallas_call | solution.py:362
  143.0 1.1 copy-done.2
  145.1 4.1 %out_project.4 = (bf16[2,448,640]{2,1,0:T(8,128)(2,1)}, f32[2,8,640]{2,1,0:T(8,128)S(1)}) custom-call(s32[6]{0:T(128)S(1)} %stack.99.place_ref, s32[3]{0:T(128)S(1)} %copy-done.11, bf16[448,640]{1,0:T(8,128)(2,1)S(1)} %copy-done.9, bf16[448,640]{1,0:T(8,128)(2,1)S(1)} %copy-done.2, bf16[640,640]{1,0:T(8,128)(2,1)S(1)} %copy-done.1, ...), custom_call_target="tpu_custom_call" | custom-call | flops 734003200 | bytes 3358720 | tf_op jit(solution)/shard_map/out_project/pallas_call | solution.py:460
  149.8 1.0 copy-done.6
  150.8 1.1 copy-done.10
  151.8 3.2 %out_project.5 = (bf16[2,448,640]{2,1,0:T(8,128)(2,1)S(1)}, f32[2,8,640]{2,1,0:T(8,128)S(1)}) custom-call(s32[6]{0:T(128)S(1)} %stack.99.place_ref, s32[3]{0:T(128)S(1)} %copy-done.11, bf16[448,640]{1,0:T(8,128)(2,1)S(1)} %copy-done.10, bf16[448,640]{1,0:T(8,128)(2,1)S(1)} %copy-done.3, bf16[640,640]{1,0:T(8,128)(2,1)S(1)} %copy-done.1, ...), custom_call_target="tpu_custom_call" | custom-call | flops 734003200 | bytes 3358720 | tf_op jit(solution)/shard_map/out_project/pallas_call | solution.py:460
  155.0 1.1 copy-done.12
  156.1 1.3 collective-permute-start.28
  158.3 1.0 collective-permute-start.30
  159.4 1.0 copy-done.7
  160.4 4.4 %out_project.6 = bf16[2,448,640]{2,1,0:T(8,128)(2,1)} custom-call(s32[6]{0:T(128)S(1)} %stack.99.place_ref, bf16[448,640]{1,0:T(8,128)(2,1)S(1)} %copy-done.3, bf16[2,448,640]{2,1,0:T(8,128)(2,1)} %collective-permute-done.24.refs_1_, bf16[640,640]{1,0:T(8,128)(2,1)S(1)} %copy-done.1, bf16[320,640]{1,0:T(8,128)(2,1)S(1)} %collective-permute-done.18.refs_4_.refs_3_, ...), custom_call_target="tpu_custom_call" | custom-call | flops 734003200 | bytes 4505600 | tf_op jit(solution)/shard_map/out_project/pallas_call | solution.py:460
  165.8 4.5 %collective-permute-start.33 = (bf16[5,8,640]{2,1,0:T(8,128)(2,1)S(1)}, bf16[5,8,640]{2,1,0:T(8,128)(2,1)S(1)}, u32[]{:S(2)}, u32[]{:S(2)}) collective-permute-start(bf16[5,8,640]{2,1,0:T(8,128)(2,1)S(1)} %get-tuple-element.91), channel_id=1, source_target_pairs={{0,12},{4,0},{8,4},{12,8},{1,13},{5,1},{9,5},{13,9},{2,14},{6,2},{... | collective-permute-start | bytes 153608 | tf_op jit(solution)/shard_map/ppermute | solution.py:488
  170.2 1.3 collective-permute-start.31
  172.3 3.0 %collective-permute-done.32 = bf16[5,8,640]{2,1,0:T(8,128)(2,1)S(1)} collective-permute-done((bf16[5,8,640]{2,1,0:T(8,128)(2,1)S(1)}, bf16[5,8,640]{2,1,0:T(8,128)(2,1)S(1)}, u32[]{:S(2)}, u32[]{:S(2)}) %collective-permute-start.32) | collective-permute-done | bytes 51232 | tf_op jit(solution)/shard_map/ppermute | solution.py:488
  177.2 3.6 %out_project.7 = bf16[2,448,640]{2,1,0:T(8,128)(2,1)S(1)} custom-call(s32[6]{0:T(128)S(1)} %stack.99.place_ref, bf16[448,640]{1,0:T(8,128)(2,1)S(1)} %copy-done.3, bf16[2,448,640]{2,1,0:T(8,128)(2,1)} %collective-permute-done.25.refs_1_, bf16[640,640]{1,0:T(8,128)(2,1)S(1)} %copy-done.1, bf16[320,640]{1,0:T(8,128)(2,1)S(1)} %collective-permute-done.18.refs_4_.refs_3_, ...), custom_call_target="tpu_custom_call" | custom-call | flops 734003200 | bytes 4505600 | tf_op jit(solution)/shard_map/out_project/pallas_call | solution.py:460
  180.8 11.8 %collective-permute-done.26 = bf16[2,448,640]{2,1,0:T(8,128)(2,1)} collective-permute-done((bf16[2,448,640]{2,1,0:T(8,128)(2,1)}, bf16[2,448,640]{2,1,0:T(8,128)(2,1)}, u32[]{:S(2)}, u32[]{:S(2)}) %collective-permute-start.26) | collective-permute-done | bytes 1146912 | tf_op jit(solution)/shard_map/ppermute | solution.py:543
  192.9 2.0 fusion
  197.4 1.5 maximum_select_fusion
  (146 shorter events, 18.7 us)
Async XLA Ops:
  7.2 188.9 %copy-start = (bf16[33,2560]{1,0:T(8,128)(2,1)S(1)}, bf16[33,2560]{1,0:T(8,128)(2,1)}, u32[]{:S(2)}) copy-start(bf16[33,2560]{1,0:T(8,128)(2,1)} %param.19) | copy-start | bytes 506884
  7.2 18.4 %copy-start.14 = (bf16[640,640]{1,0:T(8,128)(2,1)S(1)}, bf16[640,640]{1,0:T(8,128)(2,1)}, u32[]{:S(2)}) copy-start(bf16[640,640]{1,0:T(8,128)(2,1)} %refs_0_.3) | copy-start | bytes 2457604
  7.2 39.3 %copy-start.15 = (bf16[640,640]{1,0:T(8,128)(2,1)S(1)}, bf16[640,640]{1,0:T(8,128)(2,1)}, u32[]{:S(2)}) copy-start(bf16[640,640]{1,0:T(8,128)(2,1)} %refs_0_.5) | copy-start | bytes 2457604
  7.2 54.8 %all-gather.3.cloned.1.call-start = ((), (), s32[]{:S(2)}) async-start(), calls=%async_computation | async-start | bytes 5734400 | tf_op jit(solution)/shard_map/all_gather | solution.py:526
  8.4 15.4 %collective-permute-start.6 = (bf16[320,640]{1,0:T(8,128)(2,1)S(1)}, bf16[320,640]{1,0:T(8,128)(2,1)S(1)}, u32[]{:S(2)}, u32[]{:S(2)}) collective-permute-start(bf16[320,640]{1,0:T(8,128)(2,1)S(1)} %constant_dynamic-slice_fusion.6), channel_id=1, source_target_pairs={{0,4},{4,8},{8,12},{12,0},{1,5},{5,9},{9,13},{13,1},{2,6},{6,10},{... | collective-permute-start | bytes 1228808 | tf_op jit(solution)/shard_map/ppermute | solution.py:488
  11.5 20.0 %collective-permute-start = (bf16[320,640]{1,0:T(8,128)(2,1)S(1)}, bf16[320,640]{1,0:T(8,128)(2,1)}, u32[]{:S(2)}, u32[]{:S(2)}) collective-permute-start(bf16[320,640]{1,0:T(8,128)(2,1)S(1)} %constant_dynamic-slice_fusion.6), channel_id=1, source_target_pairs={{0,12},{4,0},{8,4},{12,8},{1,13},{5,1},{9,5},{13,9},{2,14},{6,2},{... | collective-permute-start | bytes 1228808 | tf_op jit(solution)/shard_map/ppermute | solution.py:488
  13.8 42.6 %copy-start.17 = (s32[3,1]{0,1:T(1,128)}, s32[3,1]{0,1:T(1,128)S(1)}, u32[]{:S(2)}) copy-start(s32[3,1]{0,1:T(1,128)S(1)} %reduce-window.8) | copy-start | bytes 40
  23.8 30.2 %copy-start.22 = (bf16[320,640]{1,0:T(8,128)(2,1)}, bf16[320,640]{1,0:T(8,128)(2,1)S(1)}, u32[]{:S(2)}) copy-start(bf16[320,640]{1,0:T(8,128)(2,1)S(1)} %collective-permute-done.6.refs_1_) | copy-start | bytes 1228804
  23.8 19.3 %collective-permute-start.7 = (bf16[320,640]{1,0:T(8,128)(2,1)S(1)}, bf16[320,640]{1,0:T(8,128)(2,1)}, u32[]{:S(2)}, u32[]{:S(2)}) collective-permute-start(bf16[320,640]{1,0:T(8,128)(2,1)S(1)} %collective-permute-done.6.refs_1_), channel_id=1, source_target_pairs={{0,4},{4,8},{8,12},{12,0},{1,5},{5,9},{9,13},{13,1},{2,6},{6,10},{... | collective-permute-start | bytes 1228808 | tf_op jit(solution)/shard_map/ppermute | solution.py:488
  23.9 21.2 %collective-permute-start.9 = (bf16[320,640]{1,0:T(8,128)(2,1)S(1)}, bf16[320,640]{1,0:T(8,128)(2,1)S(1)}, u32[]{:S(2)}, u32[]{:S(2)}) collective-permute-start(bf16[320,640]{1,0:T(8,128)(2,1)S(1)} %collective-permute-done.6.refs_1_), channel_id=1, source_target_pairs={{0,16},{16,0},{1,17},{17,1},{2,18},{18,2},{3,19},{19,3},{4,20},{20... | collective-permute-start | bytes 1228808 | tf_op jit(solution)/shard_map/ppermute | solution.py:500
  31.5 20.3 %collective-permute-start.1 = (bf16[320,640]{1,0:T(8,128)(2,1)S(1)}, bf16[320,640]{1,0:T(8,128)(2,1)}, u32[]{:S(2)}, u32[]{:S(2)}) collective-permute-start(bf16[320,640]{1,0:T(8,128)(2,1)S(1)} %constant_dynamic-slice_fusion.7), channel_id=1, source_target_pairs={{0,4},{4,8},{8,12},{12,0},{1,5},{5,9},{9,13},{13,1},{2,6},{6,10},{... | collective-permute-start | bytes 1228808 | tf_op jit(solution)/shard_map/ppermute | solution.py:488
  33.6 18.3 %collective-permute-start.2 = (bf16[320,640]{1,0:T(8,128)(2,1)}, bf16[320,640]{1,0:T(8,128)(2,1)S(1)}, u32[]{:S(2)}, u32[]{:S(2)}) collective-permute-start(bf16[320,640]{1,0:T(8,128)(2,1)} %collective-permute-done.refs_5_), channel_id=1, source_target_pairs={{0,16},{16,0},{1,17},{17,1},{2,18},{18,2},{3,19},{19,3},{4,20},{20... | collective-permute-start | bytes 1228808 | tf_op jit(solution)/shard_map/ppermute | solution.py:500
  43.2 17.4 %collective-permute-start.8 = (bf16[320,640]{1,0:T(8,128)(2,1)S(1)}, bf16[320,640]{1,0:T(8,128)(2,1)}, u32[]{:S(2)}, u32[]{:S(2)}) collective-permute-start(bf16[320,640]{1,0:T(8,128)(2,1)S(1)} %constant_dynamic-slice_fusion.7), channel_id=1, source_target_pairs={{0,12},{4,0},{8,4},{12,8},{1,13},{5,1},{9,5},{13,9},{2,14},{6,2},{... | collective-permute-start | bytes 1228808 | tf_op jit(solution)/shard_map/ppermute | solution.py:488
  45.0 15.5 %collective-permute-start.10 = (bf16[320,640]{1,0:T(8,128)(2,1)}, bf16[320,640]{1,0:T(8,128)(2,1)}, u32[]{:S(2)}, u32[]{:S(2)}) collective-permute-start(bf16[320,640]{1,0:T(8,128)(2,1)} %collective-permute-done.7.refs_3_), channel_id=1, source_target_pairs={{0,16},{16,0},{1,17},{17,1},{2,18},{18,2},{3,19},{19,3},{4,20},{20... | collective-permute-start | bytes 1228808 | tf_op jit(solution)/shard_map/ppermute | solution.py:500
  51.8 18.7 %collective-permute-start.3 = (bf16[320,640]{1,0:T(8,128)(2,1)}, bf16[320,640]{1,0:T(8,128)(2,1)S(1)}, u32[]{:S(2)}, u32[]{:S(2)}) collective-permute-start(bf16[320,640]{1,0:T(8,128)(2,1)} %collective-permute-done.1.refs_1_), channel_id=1, source_target_pairs={{0,16},{16,0},{1,17},{17,1},{2,18},{18,2},{3,19},{19,3},{4,20},{20... | collective-permute-start | bytes 1228808 | tf_op jit(solution)/shard_map/ppermute | solution.py:500
  53.4 17.2 %collective-permute-start.4 = (bf16[320,640]{1,0:T(8,128)(2,1)}, bf16[320,640]{1,0:T(8,128)(2,1)}, u32[]{:S(2)}, u32[]{:S(2)}) collective-permute-start(bf16[320,640]{1,0:T(8,128)(2,1)} %collective-permute-done.1.refs_1_), channel_id=1, source_target_pairs={{0,4},{4,8},{8,12},{12,0},{1,5},{5,9},{9,13},{13,1},{2,6},{6,10},{... | collective-permute-start | bytes 1228808 | tf_op jit(solution)/shard_map/ppermute | solution.py:488
  60.5 22.7 %collective-permute-start.11 = (bf16[320,640]{1,0:T(8,128)(2,1)}, bf16[320,640]{1,0:T(8,128)(2,1)}, u32[]{:S(2)}, u32[]{:S(2)}) collective-permute-start(bf16[320,640]{1,0:T(8,128)(2,1)} %collective-permute-done.8.refs_5_), channel_id=1, source_target_pairs={{0,16},{16,0},{1,17},{17,1},{2,18},{18,2},{3,19},{19,3},{4,20},{20... | collective-permute-start | bytes 1228808 | tf_op jit(solution)/shard_map/ppermute | solution.py:500
  68.5 14.7 %collective-permute-start.12 = (bf16[320,640]{1,0:T(8,128)(2,1)S(1)}, bf16[320,640]{1,0:T(8,128)(2,1)S(1)}, u32[]{:S(2)}, u32[]{:S(2)}) collective-permute-start(bf16[320,640]{1,0:T(8,128)(2,1)S(1)} %constant_dynamic-slice_fusion.5), channel_id=1, source_target_pairs={{0,4},{4,8},{8,12},{12,0},{1,5},{5,9},{9,13},{13,1},{2,6},{6,10},{... | collective-permute-start | bytes 1228808 | tf_op jit(solution)/shard_map/ppermute | solution.py:488
  70.5 10.8 %copy-start.25 = (bf16[320,640]{1,0:T(8,128)(2,1)}, bf16[320,640]{1,0:T(8,128)(2,1)S(1)}, u32[]{:S(2)}) copy-start(bf16[320,640]{1,0:T(8,128)(2,1)S(1)} %collective-permute-done.3.refs_2_) | copy-start | bytes 1228804
  70.5 14.3 %collective-permute-start.5 = (bf16[320,640]{1,0:T(8,128)(2,1)}, bf16[320,640]{1,0:T(8,128)(2,1)S(1)}, u32[]{:S(2)}, u32[]{:S(2)}) collective-permute-start(bf16[320,640]{1,0:T(8,128)(2,1)} %collective-permute-done.4.refs_3_), channel_id=1, source_target_pairs={{0,16},{16,0},{1,17},{17,1},{2,18},{18,2},{3,19},{19,3},{4,20},{20... | collective-permute-start | bytes 1228808 | tf_op jit(solution)/shard_map/ppermute | solution.py:500
  72.2 12.6 %copy-start.1 = (bf16[640,640]{1,0:T(8,128)(2,1)S(1)}, bf16[640,640]{1,0:T(8,128)(2,1)}, u32[]{:S(2)}) copy-start(bf16[640,640]{1,0:T(8,128)(2,1)} %refs_2_.3) | copy-start | bytes 2457604
  81.3 13.3 %collective-permute-start.16 = (bf16[320,640]{1,0:T(8,128)(2,1)S(1)}, bf16[320,640]{1,0:T(8,128)(2,1)S(1)}, u32[]{:S(2)}, u32[]{:S(2)}) collective-permute-start(bf16[320,640]{1,0:T(8,128)(2,1)S(1)} %constant_dynamic-slice_fusion.5), channel_id=1, source_target_pairs={{0,12},{4,0},{8,4},{12,8},{1,13},{5,1},{9,5},{13,9},{2,14},{6,2},{... | collective-permute-start | bytes 1228808 | tf_op jit(solution)/shard_map/ppermute | solution.py:488
  83.2 11.4 %copy-start.26 = (bf16[320,640]{1,0:T(8,128)(2,1)}, bf16[320,640]{1,0:T(8,128)(2,1)S(1)}, u32[]{:S(2)}) copy-start(bf16[320,640]{1,0:T(8,128)(2,1)S(1)} %collective-permute-done.12.refs_1_) | copy-start | bytes 1228804
  83.2 14.3 %collective-permute-start.13 = (bf16[320,640]{1,0:T(8,128)(2,1)S(1)}, bf16[320,640]{1,0:T(8,128)(2,1)S(1)}, u32[]{:S(2)}, u32[]{:S(2)}) collective-permute-start(bf16[320,640]{1,0:T(8,128)(2,1)S(1)} %collective-permute-done.12.refs_1_), channel_id=1, source_target_pairs={{0,16},{16,0},{1,17},{17,1},{2,18},{18,2},{3,19},{19,3},{4,20},{20... | collective-permute-start | bytes 1228808 | tf_op jit(solution)/shard_map/ppermute | solution.py:500
  84.8 18.7 %collective-permute-start.14 = (bf16[320,640]{1,0:T(8,128)(2,1)S(1)}, bf16[320,640]{1,0:T(8,128)(2,1)}, u32[]{:S(2)}, u32[]{:S(2)}) collective-permute-start(bf16[320,640]{1,0:T(8,128)(2,1)S(1)} %collective-permute-done.12.refs_1_), channel_id=1, source_target_pairs={{0,4},{4,8},{8,12},{12,0},{1,5},{5,9},{9,13},{13,1},{2,6},{6,10},{... | collective-permute-start | bytes 1228808 | tf_op jit(solution)/shard_map/ppermute | solution.py:488
  94.6 12.5 %copy-start.27 = (bf16[320,640]{1,0:T(8,128)(2,1)}, bf16[320,640]{1,0:T(8,128)(2,1)S(1)}, u32[]{:S(2)}) copy-start(bf16[320,640]{1,0:T(8,128)(2,1)S(1)} %collective-permute-done.16.refs_5_) | copy-start | bytes 1228804
  94.6 12.5 %collective-permute-start.17 = (bf16[320,640]{1,0:T(8,128)(2,1)S(1)}, bf16[320,640]{1,0:T(8,128)(2,1)S(1)}, u32[]{:S(2)}, u32[]{:S(2)}) collective-permute-start(bf16[320,640]{1,0:T(8,128)(2,1)S(1)} %collective-permute-done.16.refs_5_), channel_id=1, source_target_pairs={{0,16},{16,0},{1,17},{17,1},{2,18},{18,2},{3,19},{19,3},{4,20},{20... | collective-permute-start | bytes 1228808 | tf_op jit(solution)/shard_map/ppermute | solution.py:500
  95.5 13.9 %collective-permute-start.18 = (bf16[320,640]{1,0:T(8,128)(2,1)S(1)}, bf16[320,640]{1,0:T(8,128)(2,1)S(1)}, u32[]{:S(2)}, u32[]{:S(2)}) collective-permute-start(bf16[320,640]{1,0:T(8,128)(2,1)S(1)} %constant_dynamic-slice_fusion.4), channel_id=1, source_target_pairs={{0,4},{4,8},{8,12},{12,0},{1,5},{5,9},{9,13},{13,1},{2,6},{6,10},{... | collective-permute-start | bytes 1228808 | tf_op jit(solution)/shard_map/ppermute | solution.py:488
  97.5 18.7 %copy-start.28 = (bf16[320,640]{1,0:T(8,128)(2,1)}, bf16[320,640]{1,0:T(8,128)(2,1)S(1)}, u32[]{:S(2)}) copy-start(bf16[320,640]{1,0:T(8,128)(2,1)S(1)} %collective-permute-done.13.refs_2_) | copy-start | bytes 1228804
  103.5 12.7 %collective-permute-start.15 = (bf16[320,640]{1,0:T(8,128)(2,1)}, bf16[320,640]{1,0:T(8,128)(2,1)}, u32[]{:S(2)}, u32[]{:S(2)}) collective-permute-start(bf16[320,640]{1,0:T(8,128)(2,1)} %collective-permute-done.14.refs_3_), channel_id=1, source_target_pairs={{0,16},{16,0},{1,17},{17,1},{2,18},{18,2},{3,19},{19,3},{4,20},{20... | collective-permute-start | bytes 1228808 | tf_op jit(solution)/shard_map/ppermute | solution.py:500
  109.3 22.9 %collective-permute-start.19 = (bf16[320,640]{1,0:T(8,128)(2,1)S(1)}, bf16[320,640]{1,0:T(8,128)(2,1)S(1)}, u32[]{:S(2)}, u32[]{:S(2)}) collective-permute-start(bf16[320,640]{1,0:T(8,128)(2,1)S(1)} %collective-permute-done.18.refs_4_.refs_3_), channel_id=1, source_target_pairs={{0,16},{16,0},{1,17},{17,1},{2,18},{18,2},{3,19},{19,3},{4,20},{20... | collective-permute-start | bytes 1228808 | tf_op jit(solution)/shard_map/ppermute | solution.py:500
  110.9 21.3 %collective-permute-start.21 = (bf16[320,640]{1,0:T(8,128)(2,1)S(1)}, bf16[320,640]{1,0:T(8,128)(2,1)S(1)}, u32[]{:S(2)}, u32[]{:S(2)}) collective-permute-start(bf16[320,640]{1,0:T(8,128)(2,1)S(1)} %constant_dynamic-slice_fusion.4), channel_id=1, source_target_pairs={{0,12},{4,0},{8,4},{12,8},{1,13},{5,1},{9,5},{13,9},{2,14},{6,2},{... | collective-permute-start | bytes 1228808 | tf_op jit(solution)/shard_map/ppermute | solution.py:488
  113.6 27.9 %collective-permute-start.20 = (bf16[320,640]{1,0:T(8,128)(2,1)S(1)}, bf16[320,640]{1,0:T(8,128)(2,1)S(1)}, u32[]{:S(2)}, u32[]{:S(2)}) collective-permute-start(bf16[320,640]{1,0:T(8,128)(2,1)S(1)} %collective-permute-done.18.refs_4_.refs_3_), channel_id=1, source_target_pairs={{0,4},{4,8},{8,12},{12,0},{1,5},{5,9},{9,13},{13,1},{2,6},{6,10},{... | collective-permute-start | bytes 1228808 | tf_op jit(solution)/shard_map/ppermute | solution.py:488
  132.2 10.0 %collective-permute-start.22 = (bf16[320,640]{1,0:T(8,128)(2,1)S(1)}, bf16[320,640]{1,0:T(8,128)(2,1)S(1)}, u32[]{:S(2)}, u32[]{:S(2)}) collective-permute-start(bf16[320,640]{1,0:T(8,128)(2,1)S(1)} %collective-permute-done.19.refs_5_.refs_4_), channel_id=1, source_target_pairs={{0,4},{4,8},{8,12},{12,0},{1,5},{5,9},{9,13},{13,1},{2,6},{6,10},{... | collective-permute-start | bytes 1228808 | tf_op jit(solution)/shard_map/ppermute | solution.py:488
  132.5 10.5 %collective-permute-start.23 = (bf16[320,640]{1,0:T(8,128)(2,1)S(1)}, bf16[320,640]{1,0:T(8,128)(2,1)}, u32[]{:S(2)}, u32[]{:S(2)}) collective-permute-start(bf16[320,640]{1,0:T(8,128)(2,1)S(1)} %collective-permute-done.21.refs_8_.refs_7_), channel_id=1, source_target_pairs={{0,16},{16,0},{1,17},{17,1},{2,18},{18,2},{3,19},{19,3},{4,20},{20... | collective-permute-start | bytes 1228808 | tf_op jit(solution)/shard_map/ppermute | solution.py:500
  133.3 9.8 %copy-start.11 = (s32[3]{0:T(128)S(1)}, s32[3]{0:T(128)}, u32[]{:S(2)}) copy-start(s32[3]{0:T(128)} %get-tuple-element.72.picked_ref.refs_0_) | copy-start | bytes 40
  133.3 16.0 %copy-start.31 = (s32[3]{0:T(128)S(1)}, s32[3]{0:T(128)}, u32[]{:S(2)}) copy-start(s32[3]{0:T(128)} %param.14) | copy-start | bytes 40
  133.3 16.2 %copy-start.18 = (s32[896]{0:T(1024)S(1)}, s32[896]{0:T(1024)}, u32[]{:S(2)}) copy-start(s32[896]{0:T(1024)} %param.13) | copy-start | bytes 10756
  149.2 10.1 %collective-permute-start.24 = (bf16[2,448,640]{2,1,0:T(8,128)(2,1)}, bf16[2,448,640]{2,1,0:T(8,128)(2,1)}, u32[]{:S(2)}, u32[]{:S(2)}) collective-permute-start(bf16[2,448,640]{2,1,0:T(8,128)(2,1)} %get-tuple-element.59), channel_id=1, source_target_pairs={{0,1},{1,0},{2,3},{3,2},{4,5},{5,4},{6,7},{7,6},{8,9},{9,8},{10,11... | collective-permute-start | bytes 3440648 | tf_op jit(solution)/shard_map/ppermute | solution.py:543
  156.1 9.5 %collective-permute-start.28 = (f32[4,8,640]{2,1,0:T(8,128)S(1)}, f32[4,8,640]{2,1,0:T(8,128)S(1)}, u32[]{:S(2)}, u32[]{:S(2)}) collective-permute-start(f32[4,8,640]{2,1,0:T(8,128)S(1)} %constant_dynamic-update-slice_fusion), channel_id=1, source_target_pairs={{0,1},{1,0},{2,3},{3,2},{4,5},{5,4},{6,7},{7,6},{8,9},{9,8},{10,11... | collective-permute-start | bytes 245768 | tf_op jit(solution)/shard_map/ppermute | solution.py:543
  157.5 18.7 %collective-permute-start.25 = (bf16[2,448,640]{2,1,0:T(8,128)(2,1)}, bf16[2,448,640]{2,1,0:T(8,128)(2,1)}, u32[]{:S(2)}, u32[]{:S(2)}) collective-permute-start(bf16[2,448,640]{2,1,0:T(8,128)(2,1)} %copy-done.12), channel_id=1, source_target_pairs={{0,1},{1,0},{2,3},{3,2},{4,5},{5,4},{6,7},{7,6},{8,9},{9,8},{10,11... | collective-permute-start | bytes 3440648 | tf_op jit(solution)/shard_map/ppermute | solution.py:543
  157.5 8.2 %collective-permute-start.29 = (f32[4,8,640]{2,1,0:T(8,128)S(1)}, f32[4,8,640]{2,1,0:T(8,128)S(1)}, u32[]{:S(2)}, u32[]{:S(2)}) collective-permute-start(f32[4,8,640]{2,1,0:T(8,128)S(1)} %constant_dynamic-update-slice_fusion), channel_id=1, source_target_pairs={{0,2},{1,3},{2,0},{3,1},{4,6},{5,7},{6,4},{7,5},{8,10},{9,11},{10,... | collective-permute-start | bytes 245768 | tf_op jit(solution)/shard_map/ppermute | solution.py:543
  158.3 7.3 %collective-permute-start.30 = (f32[4,8,640]{2,1,0:T(8,128)S(1)}, f32[4,8,640]{2,1,0:T(8,128)S(1)}, u32[]{:S(2)}, u32[]{:S(2)}) collective-permute-start(f32[4,8,640]{2,1,0:T(8,128)S(1)} %constant_dynamic-update-slice_fusion), channel_id=1, source_target_pairs={{0,3},{1,2},{2,1},{3,0},{4,7},{5,6},{6,5},{7,4},{8,11},{9,10},{10,... | collective-permute-start | bytes 245768 | tf_op jit(solution)/shard_map/ppermute | solution.py:543
  164.7 27.9 %collective-permute-start.26 = (bf16[2,448,640]{2,1,0:T(8,128)(2,1)}, bf16[2,448,640]{2,1,0:T(8,128)(2,1)}, u32[]{:S(2)}, u32[]{:S(2)}) collective-permute-start(bf16[2,448,640]{2,1,0:T(8,128)(2,1)} %out_project.6), channel_id=1, source_target_pairs={{0,2},{1,3},{2,0},{3,1},{4,6},{5,7},{6,4},{7,5},{8,10},{9,11},{10,... | collective-permute-start | bytes 3440648 | tf_op jit(solution)/shard_map/ppermute | solution.py:543
  165.8 6.5 %collective-permute-start.33 = (bf16[5,8,640]{2,1,0:T(8,128)(2,1)S(1)}, bf16[5,8,640]{2,1,0:T(8,128)(2,1)S(1)}, u32[]{:S(2)}, u32[]{:S(2)}) collective-permute-start(bf16[5,8,640]{2,1,0:T(8,128)(2,1)S(1)} %get-tuple-element.91), channel_id=1, source_target_pairs={{0,12},{4,0},{8,4},{12,8},{1,13},{5,1},{9,5},{13,9},{2,14},{6,2},{... | collective-permute-start | bytes 153608 | tf_op jit(solution)/shard_map/ppermute | solution.py:488
  170.2 5.0 %collective-permute-start.32 = (bf16[5,8,640]{2,1,0:T(8,128)(2,1)S(1)}, bf16[5,8,640]{2,1,0:T(8,128)(2,1)S(1)}, u32[]{:S(2)}, u32[]{:S(2)}) collective-permute-start(bf16[5,8,640]{2,1,0:T(8,128)(2,1)S(1)} %get-tuple-element.91), channel_id=1, source_target_pairs={{0,8},{4,12},{8,0},{12,4},{1,9},{5,13},{9,1},{13,5},{2,10},{6,14},... | collective-permute-start | bytes 153608 | tf_op jit(solution)/shard_map/ppermute | solution.py:488
  170.2 5.9 %collective-permute-start.31 = (bf16[5,8,640]{2,1,0:T(8,128)(2,1)S(1)}, bf16[5,8,640]{2,1,0:T(8,128)(2,1)S(1)}, u32[]{:S(2)}, u32[]{:S(2)}) collective-permute-start(bf16[5,8,640]{2,1,0:T(8,128)(2,1)S(1)} %get-tuple-element.91), channel_id=1, source_target_pairs={{0,4},{4,8},{8,12},{12,0},{1,5},{5,9},{9,13},{13,1},{2,6},{6,10},{... | collective-permute-start | bytes 153608 | tf_op jit(solution)/shard_map/ppermute | solution.py:488
  194.9 2.5 %collective-permute-start.27 = (bf16[448,640]{1,0:T(8,128)(2,1)S(1)}, bf16[448,640]{1,0:T(8,128)(2,1)S(1)}, u32[]{:S(2)}, u32[]{:S(2)}) collective-permute-start(bf16[448,640]{1,0:T(8,128)(2,1)S(1)} %get-tuple-element.75), channel_id=1, source_target_pairs={{0,1},{1,0},{2,3},{3,2},{4,5},{5,4},{6,7},{7,6},{8,9},{9,8},{10,11... | collective-permute-start | bytes 1720328 | tf_op jit(solution)/shard_map/ppermute | solution.py:543
  (19 other events, 57.8 us)
Sparse Core Ops, SparseCore 0:
  9.6 39.3 all-gather.2
